TPU v7x, 32 devices: a whole 2x2x4 slice. The times are simulated.
32 devices in a mesh: seq: 4 (over y, core), batch: 8 (over z, x).
Axes of the slice: x: 2, y: 2, z: 4, core: 2. Of those that a mesh axis runs over, the one named last changes fastest.
Arguments:
- block_input: bfloat16 [8, 1024, 1024], P('batch', 'seq'), may hold values from -6 to 6
- segment_ids: int32 [8, 1024], P('batch', 'seq'), may hold values from 0 to 2, never falling along the last dimension, each value on 1 to 512 neighbouring positions
- out_cotangent: bfloat16 [8, 1024, 1024], P('batch', 'seq'), may hold values from -6 to 6
- lower_bound: float32 [1024], replicated, as said below
- gain_first: bfloat16 [1024], P(('seq', 'batch')), may hold values from 0.099609375 to 1.8984375
- w_input: bfloat16 [1024, 2048], P('batch', 'seq'), may hold values from -0.1875 to 0.1875
- w_forget: bfloat16 [1024, 1024], P('batch', 'seq'), may hold values from -0.1875 to 0.1875
- w_outgate: bfloat16 [1024, 2048], P('batch', 'seq'), may hold values from -0.1875 to 0.1875
- phase_angle: bfloat16 [1024], P(('seq', 'batch')), may hold values from -3.140625 to 3.140625
- gain_mixer: bfloat16 [2048], P(('seq', 'batch')), may hold values from 0.099609375 to 1.8984375
- w_output: bfloat16 [2048, 1024], P('batch', 'seq'), may hold values from -0.125 to 0.125
- gain_second: bfloat16 [1024], P(('seq', 'batch')), may hold values from 0.099609375 to 1.8984375
- w_gate: bfloat16 [1024, 2816], P('batch', 'seq'), may hold values from -0.1875 to 0.1875
- w_up: bfloat16 [1024, 2816], P('batch', 'seq'), may hold values from -0.1875 to 0.1875
- w_down: bfloat16 [2816, 1024], P('seq', 'batch'), may hold values from -0.109375 to 0.109375
Outputs:
- block_output: bfloat16 [8, 1024, 1024], P('batch', 'seq')
- grad_input: bfloat16 [8, 1024, 1024], P('batch', 'seq')
- grad_gain_first: float32 [1024], P(('seq', 'batch'))
- grad_w_input: float32 [1024, 2048], P('batch', 'seq')
- grad_w_forget: float32 [1024, 1024], P('batch', 'seq')
- grad_w_outgate: float32 [1024, 2048], P('batch', 'seq')
- grad_phase_angle: float32 [1024], P(('seq', 'batch'))
- grad_gain_mixer: float32 [2048], P(('seq', 'batch'))
- grad_w_output: float32 [2048, 1024], P('batch', 'seq')
- grad_gain_second: float32 [1024], P(('seq', 'batch'))
- grad_w_gate: float32 [1024, 2816], P('batch', 'seq')
- grad_w_up: float32 [1024, 2816], P('batch', 'seq')
- grad_w_down: float32 [2816, 1024], P('seq', 'batch')
Inputs may be any that keep to these rules, and one draw needn't show every extreme that they name: `segment_ids`: within a row the ids never fall; a token whose id differs from its predecessor's starts a new document and the recurrence restarts there. `lower_bound`: every entry lies in [0.85, 1).
All inputs are finite; a program needn't handle non-finite values.
Results may differ from a plain program's by a relative error of at most 0.014.
Values may be sent and summed in bfloat16 or wider, within the bound.
No kernel may reach another device: no remote copies, remote signals or barrier semaphores. Data moves between devices by JAX's collectives and lax.ppermute only.
A program may use at most 256 MiB of HBM per device.

v0:
```python
import functools
import math

import jax
import jax.numpy as jnp
from jax import lax
from jax.experimental import pallas as pl
from jax.experimental.pallas import tpu as pltpu
from jax.sharding import PartitionSpec as P

EPS = 1e-6
F32 = jnp.float32
BF = jnp.bfloat16
MB = 1024 * 1024

CORE = [(s, s ^ 1) for s in range(4)]
YSWAP = [(s, s ^ 2) for s in range(4)]
XSWAP = [(b, b ^ 1) for b in range(8)]


def zshift(k):
    return [(2 * z + x, 2 * ((z + k) % 4) + x) for z in range(4) for x in range(2)]


def out_block_perm():
    pairs = []
    for s in range(4):
        for b in range(8):
            y, c, part = b & 1, (b >> 1) & 1, b >> 2
            ys, cs = s >> 1, s & 1
            pairs.append((s * 8 + b, (2 * y + c) * 8 + 2 * (2 * part + cs) + ys))
    return pairs


OUT_PERM = out_block_perm()
OUT_BACK = [(d, s) for s, d in OUT_PERM]
FORGET_PERM = [(2 * (d & 1) + (d >> 1), d) for d in range(4)]


def sigm(v):
    return 0.5 * jnp.tanh(0.5 * v) + 0.5


def mm(a, b):
    return jnp.dot(a, b, preferred_element_type=F32)


def mm_bt(a, b):
    return lax.dot_general(a, b, (((1,), (1,)), ((), ())), preferred_element_type=F32)


def mm_at(a, b):
    return lax.dot_general(a, b, (((0,), (0,)), ((), ())), preferred_element_type=F32)


def sds(shape, dtype):
    return jax.ShapeDtypeStruct(shape, dtype)


HBM, SMEM, VMEM = "hbm", "smem", "vmem"


def tiled_bytes(a):
    shape = (1, 1) + tuple(a.shape)
    lanes, rows = -(-shape[-1] // 128) * 128, -(-shape[-2] // 16) * 16
    return math.prod(shape[:-2]) * rows * lanes * jnp.dtype(a.dtype).itemsize


def call(body, outs, args, kinds=None, okinds=None, scratch=(), room=8, flops=0, name=None):
    kinds = kinds or [VMEM] * len(args)
    okinds = okinds or [VMEM] * len(outs)
    held = sum(tiled_bytes(a) for a, k in zip(args, kinds) if k == VMEM)
    held += sum(tiled_bytes(o) for o, k in zip(outs, okinds) if k == VMEM)
    held += sum(tiled_bytes(m) for m in scratch if m.memory_space == pltpu.VMEM)
    vmem = 63 if room is None else -(-held // MB) + room
    space = {HBM: pl.ANY, SMEM: pltpu.SMEM, VMEM: pltpu.VMEM}
    nbytes = sum(a.size * a.dtype.itemsize for a in args)
    nbytes += sum(o.size * o.dtype.itemsize for o in outs)
    return pl.pallas_call(
        body,
        out_shape=outs,
        in_specs=[pl.BlockSpec(memory_space=space[k]) for k in kinds],
        out_specs=[pl.BlockSpec(memory_space=space[k]) for k in okinds],
        scratch_shapes=list(scratch),
        compiler_params=pltpu.CompilerParams(vmem_limit_bytes=vmem * MB),
        cost_estimate=pl.CostEstimate(
            flops=10 * (flops + 3 * 10**8), bytes_accessed=nbytes, transcendentals=0
        ),
        name=name,
    )(*args)


def hilo(col):
    rows = col.shape[0]
    hi = col.astype(BF)
    lo = (col - hi.astype(F32)).astype(BF)
    lane = lax.broadcasted_iota(jnp.int32, (rows, 128), 1)
    hi_b = jnp.broadcast_to(hi.astype(F32), (rows, 128))
    lo_b = jnp.broadcast_to(lo.astype(F32), (rows, 128))
    return jnp.where(lane == 0, hi_b, jnp.where(lane == 1, lo_b, 0.0)).astype(BF)


def lanesum(tile):
    return jnp.sum(tile.astype(F32), axis=1, keepdims=True)


def interleave(blk, back):
    row = lax.broadcasted_iota(jnp.int32, (blk, blk), 0)
    col = lax.broadcasted_iota(jnp.int32, (blk, blk), 1)
    if back:
        row, col = col, row
    hit = col == (row % 8) * (blk // 8) + row // 8
    return jnp.where(hit, 1.0, 0.0).astype(BF)


class Copies:
    def __init__(self, sems):
        self.sems, self.used = sems, 0

    def start(self, pairs):
        made = []
        for src, dst in pairs:
            made.append(pltpu.make_async_copy(src, dst, self.sems.at[self.used]))
            made[-1].start()
            self.used += 1
        return made


def wait_all(made):
    for m in made:
        m.wait()


def rows_of(i, n):
    return pl.ds(pl.multiple_of(i * n, n), n)


def norm1_body(x_ref, c_ref, o_ref, xp_ref, cp_ref):
    perm = interleave(x_ref.shape[0], False)
    x = mm(perm, x_ref[...])
    xp_ref[...] = x.astype(BF)
    cp_ref[...] = mm(perm, c_ref[...]).astype(BF)
    sc = lax.rsqrt(jnp.mean(x * x, axis=1, keepdims=True) + EPS)
    o_ref[...] = (x * sc).astype(BF)


def line_body(g1_ref, g2_ref, ph_ref, gm_ref, id_ref, o_ref):
    line = jnp.concatenate([g1_ref[...], g2_ref[...], ph_ref[...], gm_ref[...]])[None, :]
    line = jnp.concatenate([line.astype(F32), jnp.zeros((1, 256 - line.shape[1]), F32)], axis=1)
    both = jnp.concatenate([id_ref[...].astype(F32), line], axis=1)
    o_ref[...] = jnp.broadcast_to(both, o_ref.shape).astype(BF)


def pack_body(idx_ref, in_ref, og_ref, far_ref, fg_ref, out_ref, l_ref, lx_ref, o_ref, both_ref):
    rows, ch = fg_ref.shape
    nat = rows_of(idx_ref[2], ch)
    o_ref[0:rows, 0:ch] = in_ref[:, nat]
    o_ref[0:rows, ch : 2 * ch] = far_ref[:, 0:ch]
    o_ref[0:rows, 2 * ch : 3 * ch] = fg_ref[...]
    o_ref[0:rows, 3 * ch : 4 * ch] = og_ref[:, nat]
    o_ref[0:rows, 4 * ch : 5 * ch] = far_ref[:, ch:]
    o_ref[0:rows, 5 * ch : 6 * ch] = out_ref[0:rows, :]
    o_ref[0:rows, 6 * ch : 7 * ch] = out_ref[rows:, :]
    top = lax.broadcasted_iota(jnp.int32, l_ref.shape, 0) < 8
    both_ref[...] = jnp.where(top, l_ref[...].astype(F32), lx_ref[...].astype(F32)).astype(BF)


def smalls_body(
    idx_ref, v0, v1, v2, v3, lb_in,
    g1_ref, g2_ref, cos_ref, sin_ref, gm_ref, lb_ref, keep_ref,
    line_ref, ph_ref, gmix_ref,
):
    s, x, y, z = (idx_ref[i] for i in range(4))
    width = g1_ref.shape[1]
    ch = cos_ref.shape[1]
    blk = keep_ref.shape[1]
    vs = [
        jnp.concatenate([v[8 * j : 8 * j + 1, :] for j in range(8)], axis=0)
        for v in (v0, v1, v2, v3)
    ]
    rows = jnp.concatenate([v[:, blk:].astype(F32) for v in vs], axis=0)
    r = lax.broadcasted_iota(jnp.int32, (32, width), 0)
    lane = lax.broadcasted_iota(jnp.int32, (32, width), 1)
    i = r & 7
    piece = 2 * ((z - (i >> 1)) & 3) + jnp.where((i & 1) == 0, x, 1 - x)
    device = ((r >> 3) ^ s) * 8 + piece

    def spread(first, size):
        place = lax.broadcasted_iota(jnp.int32, (256, width), 0) - first
        to = lax.broadcasted_iota(jnp.int32, (256, width), 1) & (size - 1)
        one = jnp.where(place == to, 1.0, 0.0).astype(BF)
        wide = mm(rows.astype(BF), one)
        out = []
        for part in range(32 * size // width):
            mine = (lane + part * width) // size == device
            out.append(jnp.sum(jnp.where(mine, wide, 0.0), axis=0, keepdims=True))
        return out

    g1_ref[...] = spread(0, 32)[0]
    g2_ref[...] = spread(32, 32)[0]
    ph_ref[...] = spread(64, 32)[0]
    both = spread(96, 64)
    gmix_ref[0] = both[0]
    gmix_ref[1] = both[1]
    here = rows_of(2 * (s & 1) + (s >> 1), ch)
    phase = ph_ref[:, here]
    cos_ref[...] = jnp.cos(phase)
    sin_ref[...] = jnp.where(y == 0, 1.0, -1.0) * jnp.sin(phase)
    line_ref[...] = lb_in[...]
    lb_ref[...] = line_ref[:, here]
    gm_ref[:, 0:ch] = gmix_ref[y, :, here]
    gm_ref[:, ch:] = gmix_ref[1 - y, :, here]

    ids = [v[0:1, 0:blk].astype(F32) for v in vs]
    perm = interleave(blk, False)
    first = lax.broadcasted_iota(jnp.int32, (16, blk), 1) == 0
    for k in range(4):
        at = k ^ s
        last = jnp.full((1, 1), -1.0, F32)
        for q in range(4):
            last = jnp.where((q ^ s) == at - 1, ids[q][:, blk - 1 : blk], last)
        mine = jnp.broadcast_to(ids[k], (16, blk))
        before = jnp.where(first, jnp.broadcast_to(last, (16, blk)), pltpu.roll(mine, 1, 1))
        same = jnp.where(mine == before, 1.0, 0.0).astype(BF)
        keep_ref[k] = mm_bt(perm, same)[:, 0:1]


def rot_power(cos, sin, steps):
    n = 1
    while n < steps:
        cos, sin = cos * cos - sin * sin, 2.0 * cos * sin
        n *= 2
    return cos, sin


def combine_segments(s, order, end_ref, prod_ref, init_ref, ch, cn, sn):
    ca = jnp.zeros((1, ch), F32)
    cb = jnp.zeros((1, ch), F32)
    for at in order:
        k = at ^ s
        for j in range(8) if order[0] == 0 else reversed(range(8)):
            init_ref[k, j : j + 1, 0:ch] = ca
            init_ref[k, j : j + 1, ch : 2 * ch] = cb
            pj = prod_ref[k, j : j + 1, :]
            ta = pj * (cn * ca - sn * cb) + end_ref[k, j : j + 1, 0:ch]
            cb = pj * (cn * cb + sn * ca) + end_ref[k, j : j + 1, ch : 2 * ch]
            ca = ta


def blocks_in(refs, dst, blk):
    return [(r, dst.at[rows_of(k, blk)]) for k, r in enumerate(refs)]


def mix_in_copies(idx_ref, pieces, dst):
    cols = dst.shape[1]
    if len(pieces) == 1:
        return [(pieces[0].at[:, pl.ds(0, cols)], dst)]
    rows = dst.shape[0] // 8
    return [
        (p.at[pl.ds(0, rows), pl.ds(0, cols)], dst.at[rows_of(idx_ref[4 + i], rows)])
        for i, p in enumerate(pieces)
    ]


def mix_out_copies(idx_ref, pieces, dst):
    ch = dst.shape[0] // 2
    if len(pieces) == 1:
        return [(pieces[0], dst)]
    half = ch // 2
    out = []
    for i, p in enumerate(pieces):
        for j in range(2):
            rows = pl.ds(pl.multiple_of(idx_ref[12 + i] * ch + j * half, half), half)
            src = p.at[pl.ds(0, half), pl.ds((5 + j) * ch, ch)]
            out.append((src, dst.at[rows, rows_of(idx_ref[20 + i], ch)]))
    return out


def mixer_fwd_body(*refs, pieces):
    idx_ref, *refs = refs
    xs, refs = refs[:4], refs[4:]
    ps, refs = refs[:pieces], refs[pieces:]
    os, refs = (refs[:1], refs[1:]) if pieces == 1 else (ps, refs)
    (
        g1_ref, keep_ref, lb_ref, cos_ref, sin_ref, gm_ref,
        pre_out, dk_out, h_out, kr_out, k0_out, k1_out, s_out,
        x_ref, w_ref, wo_ref, pre_ref, dk_ref, h_ref, kr_ref, k0_ref, k1_ref, sout_ref,
        src_ref, gs_ref, end_ref, prod_ref, init_ref, sems,
    ) = refs
    s = idx_ref[0]
    ch = lb_ref.shape[1]
    blk = dk_ref.shape[1]
    width = wo_ref.shape[1]
    n = blk // 8
    dma = Copies(sems)
    need = dma.start(blocks_in(xs, x_ref, blk) + mix_in_copies(idx_ref, ps, w_ref))
    need_out = dma.start(mix_out_copies(idx_ref, os, wo_ref))
    wait_all(need)

    lb = lb_ref[...]
    g1 = g1_ref[...]
    saved = []
    for k in range(4):
        xg = (x_ref[rows_of(k, blk), :].astype(F32) * g1).astype(BF)
        p = mm(xg, w_ref[...])
        pre_ref[k] = p.astype(BF)
        sig = sigm(p[:, 2 * ch : 3 * ch])
        om = (1.0 - lb) * (1.0 - sig)
        dk_ref[k] = keep_ref[k] * (lb + (1.0 - lb) * sig)
        a = p[:, 0:ch]
        b = p[:, ch : 2 * ch]
        src_ref[k, :, 0:ch] = a * sigm(a) * om
        src_ref[k, :, ch : 2 * ch] = b * sigm(b) * om
        gs_ref[k] = sigm(p[:, 3 * ch : 5 * ch])
        saved += dma.start([(pre_ref.at[k], pre_out.at[k]), (dk_ref.at[k], dk_out.at[k])])

    cos = cos_ref[...][None]
    sin = sin_ref[...][None]
    zero = jnp.zeros((4, 8, ch), F32)

    def load(i):
        rows = rows_of(i, 8)
        return dk_ref[:, rows, :], src_ref[:, rows, 0:ch], src_ref[:, rows, ch : 2 * ch]

    def first_pass(i, st):
        ha, hb, prod = st
        d, sa, sb = load(i)
        ra = cos * ha - sin * hb
        rb = cos * hb + sin * ha
        return d * ra + sa, d * rb + sb, prod * d

    ha, hb, prod = lax.fori_loop(0, n, first_pass, (zero, zero, zero + 1.0), unroll=4)
    end_ref[:, :, 0:ch] = ha
    end_ref[:, :, ch : 2 * ch] = hb
    prod_ref[...] = prod
    cn, sn = rot_power(cos_ref[...], sin_ref[...], n)
    combine_segments(s, (0, 1, 2, 3), end_ref, prod_ref, init_ref, ch, cn, sn)

    def second_pass(i, st):
        ha, hb = st
        d, sa, sb = load(i)
        rows = rows_of(i, 8)
        ra = cos * ha - sin * hb
        rb = cos * hb + sin * ha
        ha = d * ra + sa
        hb = d * rb + sb
        live = d > 0.0
        h_ref[:, rows, 0:ch] = ha
        h_ref[:, rows, ch : 2 * ch] = hb
        kr_ref[:, rows, 0:ch] = jnp.where(live, ra, 0.0)
        kr_ref[:, rows, ch : 2 * ch] = jnp.where(live, rb, 0.0)
        return ha, hb

    lax.fori_loop(
        0, n, second_pass, (init_ref[:, :, 0:ch], init_ref[:, :, ch : 2 * ch]), unroll=4
    )
    saved += dma.start([(h_ref, h_out), (kr_ref, kr_out)])
    wait_all(need_out)
    gm = gm_ref[...]

    def emit(k):
        gated = h_ref[k] * gs_ref[k]
        ss = jnp.sum(gated * gated, axis=1, keepdims=True)
        return mm((gated * gm).astype(BF), wo_ref[...]), hilo(ss)

    for i in range(2):
        v, tail = emit(2 * i + 1)
        sout_ref[i, :, 0:width] = v.astype(BF)
        sout_ref[i, :, width:] = tail
        saved += dma.start([(sout_ref.at[i], s_out.at[i])])
    for k, ref, out in ((2, k1_ref, k1_out), (0, k0_ref, k0_out)):
        v, tail = emit(k)
        ref[:, 0:width] = v.astype(BF)
        ref[:, width:] = tail
        saved += dma.start([(ref, out)])
    wait_all(saved)


def resid_body(x_ref, own_ref, got_ref, ry_ref, g2_ref, resid_ref, fin_ref, sc_ref, *, chans):
    width = x_ref.shape[1]
    tot = own_ref[...].astype(F32) + got_ref[0].astype(F32) + ry_ref[...].astype(F32)
    ss = jnp.sum(tot[:, width:], axis=1, keepdims=True)
    sc = lax.rsqrt(ss / chans + EPS)
    resid = x_ref[...].astype(F32) + sc * tot[:, 0:width]
    resid_ref[...] = resid
    sc2 = lax.rsqrt(jnp.mean(resid * resid, axis=1, keepdims=True) + EPS)
    fin_ref[...] = (resid * sc2 * g2_ref[...]).astype(BF)
    sc_ref[...] = jnp.broadcast_to(sc, sc_ref.shape)


def col_copies(idx_ref, pieces, dst):
    if len(pieces) == 1:
        return [(pieces[0], dst)]
    out = []
    for i, p in enumerate(pieces):
        rows, cols = p.shape
        place = i if i < 8 else 2 if i == 8 else 6
        at = pl.ds(0 if i < 8 else rows, rows)
        out.append((p, dst.at[at, rows_of(idx_ref[4 + place], cols)]))
    return out


def ffn_body(*refs, pieces):
    idx_ref, *refs = refs
    xs, cots, refs = refs[:4], refs[4:8], refs[8:]
    ps, refs = refs[:pieces], refs[pieces:]
    (
        hid_out, ggu_out, k0_out, k1_out, s_out, kept2_out, s2_out,
        x_ref, c_ref, w_ref, hid_ref, ggu_ref, k0_ref, k1_ref, sout_ref, kept2_ref, s2_ref, sems,
    ) = refs
    blk = k0_ref.shape[0]
    hu = hid_ref.shape[1]
    dma = Copies(sems)
    need = dma.start(blocks_in(xs, x_ref, blk) + col_copies(idx_ref, ps, w_ref))
    later = dma.start(blocks_in(cots, c_ref, blk))
    wait_all(need)
    saved = []
    for k in (1, 3, 2, 0):
        rel = pl.ds(k * blk, blk)
        gu = mm_bt(x_ref[rel, :], w_ref[0 : 2 * hu, :])
        wait_all(later)
        later = []
        gh = mm_bt(c_ref[rel, :], w_ref[2 * hu :, :])
        g = gu[:, 0:hu]
        u = gu[:, hu : 2 * hu]
        sg = sigm(g)
        q = g * sg
        hid_ref[rel, :] = (q * u).astype(BF)
        dg = gh * (u * (sg + q * (1.0 - sg)))
        both = jnp.concatenate([dg, gh * q], axis=1).astype(BF)
        ggu_ref[rel, :] = both
        saved += dma.start(
            [(hid_ref.at[rel], hid_out.at[rel]), (ggu_ref.at[rel], ggu_out.at[rel])]
        )
        back = mm(both, w_ref[0 : 2 * hu, :])
        if k in (1, 3):
            sout_ref[k // 2] = back.astype(BF)
            saved += dma.start([(sout_ref.at[k // 2], s_out.at[k // 2])])
        else:
            ref, out = (k1_ref, k1_out) if k == 2 else (k0_ref, k0_out)
            ref[...] = back.astype(BF)
            saved += dma.start([(ref, out)])
    ffn_grad_part(idx_ref, 2, ggu_ref, hid_ref, x_ref, c_ref, kept2_ref, s2_ref)
    wait_all(saved + dma.start([(kept2_ref, kept2_out), (s2_ref, s2_out)]))


def down_body(*refs, pieces):
    idx_ref, h_ref, *refs = refs
    ps, refs = refs[:pieces], refs[pieces:]
    k0_ref, k1_ref, sout_ref, wd_ref, sems = refs
    blk = k0_ref.shape[0]
    hu = h_ref.shape[1]
    if pieces > 1:
        last = {2: ps[8], 6: ps[9]}
        ps = [last.get(i, p) for i, p in enumerate(ps[:8])]
    ps = [p.at[pl.ds(p.shape[0] - hu, hu)] for p in ps]
    wait_all(Copies(sems).start(col_copies(idx_ref, ps, wd_ref)))

    def emit(k):
        return mm(h_ref[rows_of(k, blk), :], wd_ref[...])

    sout_ref[0] = emit(1).astype(BF)
    sout_ref[1] = emit(3).astype(BF)
    k1_ref[...] = emit(2).astype(BF)
    k0_ref[...] = emit(0).astype(BF)


def put_parts(kk, keep, send, outs, where):
    kept_ref, send_ref = outs[kk]
    kept_ref[where] = keep.astype(kept_ref.dtype)
    send_ref[where] = send.astype(BF)


def ffn_grad_part(idx_ref, kk, g_ref, h_ref, x_ref, c_ref, keep_ref, send_ref):
    first = idx_ref[1] == 0
    hu = h_ref.shape[1]
    cols = rows_of((idx_ref[3] + kk) & 3, 256)
    for src, left, at, size in ((x_ref, g_ref, 0, 2 * hu), (c_ref, h_ref, 2 * hu, hu)):
        v = mm_at(left[...], src[:, cols])
        lo, hi = v[:, 0:128], v[:, 128:256]
        where = pl.ds(at, size)
        keep_ref[where, :] = jnp.where(first, lo, hi).astype(keep_ref.dtype)
        send_ref[where, :] = jnp.where(first, hi, lo).astype(send_ref.dtype)


def ffn_grad_body(
    idx_ref, h_ref, g_ref, x0, x1, x2, x3, c0, c1, c2, c3,
    own_ref, k1_ref, k3_ref, s1_ref, s3_ref, s0_ref, x_ref, c_ref, sems,
):
    blk = x_ref.shape[0] // 4
    dma = Copies(sems)
    need = dma.start(blocks_in((x0, x1, x2, x3), x_ref, blk))
    need += dma.start(blocks_in((c0, c1, c2, c3), c_ref, blk))
    wait_all(need)
    for kk, keep, send in (
        (1, k1_ref, s1_ref), (3, k3_ref, s3_ref), (0, own_ref, s0_ref),
    ):
        ffn_grad_part(idx_ref, kk, g_ref, h_ref, x_ref, c_ref, keep, send)


def gresid_body(
    own_ref, got_ref, ry_ref, c_ref, resid_ref, x_ref, sc_ref, g2_ref,
    gres_ref, pay_ref, gg2_ref, *, chans,
):
    width = x_ref.shape[1]
    gfi = own_ref[...].astype(F32) + got_ref[0].astype(F32) + ry_ref[...].astype(F32)
    resid = resid_ref[...]
    sc2 = lax.rsqrt(jnp.mean(resid * resid, axis=1, keepdims=True) + EPS)
    second = resid * sc2
    gg2_ref[...] = jnp.sum(gfi * second, axis=0, keepdims=True)
    g = gfi * g2_ref[...]
    gres = c_ref[...].astype(F32) + sc2 * (
        g - second * jnp.mean(g * second, axis=1, keepdims=True)
    )
    gres_ref[...] = gres
    sc = sc_ref[:, 0:1]
    branch = resid - x_ref[...].astype(F32)
    kappa = sc * sc * (jnp.sum(gres * branch, axis=1, keepdims=True) / chans)
    pay_ref[:, 0:width] = (gres * sc).astype(BF)
    pay_ref[:, width:] = hilo(kappa)


def bwd_body(*refs, pieces):
    idx_ref, *refs = refs
    pays, xs, refs = refs[:4], refs[4:8], refs[8:]
    ps, refs = refs[:pieces], refs[pieces:]
    os, refs = (refs[:1], refs[1:]) if pieces == 1 else (ps, refs)
    (
        pre_in, dk_in, h_in, kr_in, lb_ref, cos_ref, sin_ref, g1_ref, gm_ref,
        ggm_ref, gph_ref, own_out, e1_out, e3_out, e2_out, s2_out, s1_out, s3_out, s0_out,
        k0_out, k1_out, s_out,
        own_ref, e1_ref, e3_ref, e2_ref, s2_ref, s1_ref, s3_ref, s0_ref,
        k0_ref, k1_ref, sout_ref,
        p_ref, x_ref, w_ref, wo_ref, pre_ref, dk_ref, h_ref, kr_ref, u_ref, g_ref, dir_ref,
        end_ref, prod_ref, init_ref, sems,
    ) = refs
    s = idx_ref[0]
    ch = lb_ref.shape[1]
    blk = dk_ref.shape[1]
    n = blk // 8
    width = wo_ref.shape[1]
    dma = Copies(sems)
    need = dma.start(blocks_in(pays, p_ref, blk) + mix_out_copies(idx_ref, os, wo_ref))
    by_block = [
        dma.start([(pre_in.at[k], pre_ref.at[k]), (h_in.at[k], h_ref.at[k])]) for k in range(4)
    ]
    need2 = dma.start([(dk_in, dk_ref), (kr_in, kr_ref)])
    need3 = dma.start(blocks_in(xs, x_ref, blk) + mix_in_copies(idx_ref, ps, w_ref))
    wait_all(need)
    gm = gm_ref[...]
    ggm_ref[...] = jnp.zeros_like(ggm_ref)

    for k in range(4):
        rel = pl.ds(k * blk, blk)
        back = mm_bt(p_ref[rel, 0:width], wo_ref[...])
        wait_all(by_block[k])
        kappa = lanesum(p_ref[rel, width:])
        gs = sigm(pre_ref[k, :, 3 * ch : 5 * ch].astype(F32))
        h = h_ref[k]
        gated = h * gs
        u_ref[rel, :] = (gated * gm).astype(BF)
        ggm_ref[...] += jnp.sum(back * gated, axis=0, keepdims=True)
        d = (back * gm - gated * kappa) * gs
        dir_ref[k] = d
        g_ref[rel, 3 * ch : 5 * ch] = (d * h * (1.0 - gs)).astype(BF)

    wait_all(need2)
    gph_ref[...] = jnp.zeros_like(gph_ref)
    cos = cos_ref[...][None]
    sin = sin_ref[...][None]
    zero = jnp.zeros((4, 8, ch), F32)

    def load(i):
        rows = rows_of(i, 8)
        return dk_ref[:, rows, :], dir_ref[:, rows, 0:ch], dir_ref[:, rows, ch : 2 * ch]

    def first_pass(j, st):
        fa, fb, prod = st
        d, da, db = load(n - 1 - j)
        ga = da + fa
        gb = db + fb
        return d * (cos * ga + sin * gb), d * (cos * gb - sin * ga), prod * d

    fa, fb, prod = lax.fori_loop(0, n, first_pass, (zero, zero, zero + 1.0), unroll=4)
    end_ref[:, :, 0:ch] = fa
    end_ref[:, :, ch : 2 * ch] = fb
    prod_ref[...] = prod
    cn, sn = rot_power(cos_ref[...], sin_ref[...], n)
    combine_segments(s, (3, 2, 1, 0), end_ref, prod_ref, init_ref, ch, cn, -sn)

    def second_pass(j, st):
        fa, fb = st
        i = n - 1 - j
        d, da, db = load(i)
        rows = rows_of(i, 8)
        ga = da + fa
        gb = db + fb
        dir_ref[:, rows, 0:ch] = ga
        dir_ref[:, rows, ch : 2 * ch] = gb
        return d * (cos * ga + sin * gb), d * (cos * gb - sin * ga)

    lax.fori_loop(
        0, n, second_pass, (init_ref[:, :, 0:ch], init_ref[:, :, ch : 2 * ch]), unroll=4
    )
    lb = lb_ref[...]

    def grads(k, carry):
        rel = rows_of(k, blk)
        ga = dir_ref[k, :, 0:ch]
        gb = dir_ref[k, :, ch : 2 * ch]
        ra = kr_ref[k, :, 0:ch]
        rb = kr_ref[k, :, ch : 2 * ch]
        a = pre_ref[k, :, 0:ch].astype(F32)
        b = pre_ref[k, :, ch : 2 * ch].astype(F32)
        sf = sigm(pre_ref[k, :, 2 * ch : 3 * ch].astype(F32))
        sa = sigm(a)
        sb = sigm(b)
        om = (1.0 - lb) * (1.0 - sf)
        gdec = ga * ra + gb * rb - (ga * a * sa + gb * b * sb)
        gph_ref[...] += jnp.sum(dk_ref[k] * (gb * ra - ga * rb), axis=0, keepdims=True)
        g_ref[rel, 0:ch] = (ga * (sa * (1.0 + a * (1.0 - sa))) * om).astype(BF)
        g_ref[rel, ch : 2 * ch] = (gb * (sb * (1.0 + b * (1.0 - sb))) * om).astype(BF)
        g_ref[rel, 2 * ch : 3 * ch] = (gdec * om * sf).astype(BF)
        return carry

    lax.fori_loop(0, 4, grads, 0)
    wait_all(need3)

    def emit(k):
        return mm_bt(g_ref[rows_of(k, blk), :], w_ref[...])

    sout_ref[0] = emit(1).astype(BF)
    sout_ref[1] = emit(3).astype(BF)
    saved = dma.start([(sout_ref, s_out)])
    k1_ref[...] = emit(2).astype(BF)
    k0_ref[...] = emit(0).astype(BF)
    saved += dma.start([(k1_ref, k1_out), (k0_ref, k0_out)])

    g1 = g1_ref[...]

    def gain(k, carry):
        rel = rows_of(k, blk)
        x_ref[rel, :] = (x_ref[rel, :].astype(F32) * g1).astype(BF)
        return carry

    lax.fori_loop(0, 4, gain, 0)
    first = idx_ref[1] == 0
    outs = ((own_ref, s0_ref), (e1_ref, s1_ref), (e2_ref, s2_ref), (e3_ref, s3_ref))
    targets = ((own_out, s0_out), (e1_out, s1_out), (e2_out, s2_out), (e3_out, s3_out))
    half = own_ref.shape[0]
    for kk in (2, 1, 3, 0):
        zz = (idx_ref[3] + kk) & 3
        v = mm_at(x_ref[:, rows_of(zz, 2 * half)], g_ref[...])
        lo, hi = v[0:half, :], v[half:, :]
        put_parts(
            kk, jnp.where(first, lo, hi), jnp.where(first, hi, lo), outs,
            (slice(None), pl.ds(0, 5 * ch)),
        )
        u = u_ref[:, rows_of((zz >> 1) ^ idx_ref[2], ch)]
        lo = mm_at(u, p_ref[:, rows_of(zz & 1, ch)])
        hi = mm_at(u, p_ref[:, rows_of(2 + (zz & 1), ch)])
        keep, send = jnp.where(first, lo, hi), jnp.where(first, hi, lo)
        for j in range(2):
            rows = slice(j * half, (j + 1) * half)
            put_parts(
                kk, keep[rows], send[rows], outs, (slice(None), pl.ds((5 + j) * ch, ch)),
            )
        saved += dma.start(list(zip(outs[kk], targets[kk])))
    wait_all(saved)


def gin_body(own_ref, got_ref, ry_ref, x_ref, gres_ref, g1_ref, out_ref, gg1_ref):
    gn = own_ref[...].astype(F32) + got_ref[0].astype(F32) + ry_ref[...].astype(F32)
    x = x_ref[...].astype(F32)
    sc = lax.rsqrt(jnp.mean(x * x, axis=1, keepdims=True) + EPS)
    first = x * sc
    gg1_ref[...] = jnp.sum(gn * first, axis=0, keepdims=True)
    nn = gn * g1_ref[...]
    res = gres_ref[...] + sc * (nn - first * jnp.mean(nn * first, axis=1, keepdims=True))
    out_ref[...] = mm(interleave(x.shape[0], True), res.astype(BF)).astype(BF)


def finish_body(idx_ref, m_ref, far_ref, o_in, f_in, gi_ref, go_ref, o_ref, f_ref):
    rows = m_ref.shape[0]
    ch = far_ref.shape[1] // 2
    nat, far = rows_of(idx_ref[2], ch), rows_of(1 - idx_ref[2], ch)
    gi_ref[:, nat] = m_ref[:, 0:ch]
    gi_ref[:, far] = far_ref[:, 0:ch].astype(F32)
    go_ref[:, nat] = m_ref[:, 3 * ch : 4 * ch]
    go_ref[:, far] = far_ref[:, ch:].astype(F32)
    o_ref[0:rows, :] = o_in[:, 0:ch].astype(F32)
    o_ref[rows:, :] = o_in[:, ch:].astype(F32)
    f_ref[...] = f_in[...].astype(F32)


def blockout_body(resid_ref, own_ref, got_ref, ry_ref, out_ref):
    res = resid_ref[...] + own_ref[...].astype(F32) + got_ref[0].astype(F32) + ry_ref[...].astype(F32)
    out_ref[...] = mm(interleave(res.shape[0], True), res.astype(BF)).astype(BF)


def after(value, *deps):
    return lax.optimization_barrier((value, deps))[0]


def seq_gather(v):
    yv = lax.ppermute(v, "seq", YSWAP)
    cv = lax.ppermute(v, "seq", CORE)
    ycv = lax.ppermute(yv, "seq", CORE)
    return [v, cv, yv, ycv]


def seq_scatter(k1, got):
    far = plus(k1, got[1])
    return got, lax.ppermute(far, "seq", YSWAP)


def batch_pieces():
    b = lax.axis_index("batch")
    z, x = b // 2, b % 2
    at = [2 * ((z + 4 - k) % 4) + x for k in range(4)]
    return at + [a ^ 1 for a in at]


def xsend(pack):
    return lax.ppermute(pack, "batch", XSWAP)


def plus(a, b):
    return (a.astype(F32) + b.astype(F32)).astype(BF)


class Scatter:
    def __init__(self, own, kept1, kept3, kept2, s2, s1, s3, s0):
        self.kept = [own, kept1, kept2, kept3]
        self.send = [s0, s1, s2, s3]
        self.got, self.part, self.z = {}, {}, {}

    def along_x(self, kk, *deps):
        self.got[kk] = xsend(after(self.send[kk], *deps) if deps else self.send[kk])

    def add(self, kk, *deps):
        kept = after(self.kept[kk], *deps) if deps else self.kept[kk]
        self.part[kk] = plus(kept, self.got[kk])

    def along_z(self, kk):
        self.z[kk] = lax.ppermute(self.part[kk], "batch", zshift(kk))

    def total(self, *deps):
        out = after(self.kept[0], *deps) + self.got[0].astype(F32)
        for v in self.z.values():
            out = out + v.astype(F32)
        return out


def small_sum(v, *deps):
    v = v + lax.ppermute(v, "seq", CORE)
    v = v + lax.ppermute(v, "seq", YSWAP)
    v = v + lax.ppermute(v, "batch", XSWAP)
    v = after(v, *deps)
    return v + sum(lax.ppermute(v, "batch", zshift(k)) for k in (1, 2, 3))


def per_device(
    block_input, segment_ids, out_cotangent, lower_bound, gain_first, w_input, w_forget,
    w_outgate, phase_angle, gain_mixer, w_output, gain_second, w_gate, w_up, w_down,
):
    s = lax.axis_index("seq")
    b = lax.axis_index("batch")
    y, c = s // 2, s % 2
    z, x = b // 2, b % 2
    nb = lax.axis_size("batch")
    blk, width = block_input.shape[1:]
    tok = 4 * blk
    ch = width // 4
    hu = w_gate.shape[1]
    start = 2 * ch * c + ch * y
    wide = nb == 8
    dma = pltpu.SemaphoreType.DMA
    tail = width + 128
    row8 = width // 8

    far_cols = (1 - y) * ch
    far_src = jnp.concatenate(
        [
            lax.dynamic_slice(w_input, (0, far_cols), (w_input.shape[0], ch)),
            lax.dynamic_slice(w_outgate, (0, far_cols), (w_input.shape[0], ch)),
        ],
        axis=1,
    )
    far = lax.ppermute(far_src, "seq", YSWAP)
    fg = lax.ppermute(w_forget, "seq", FORGET_PERM)
    x_own, xp, cp = call(
        norm1_body, [sds((blk, width), BF)] * 3, [block_input[0], out_cotangent[0]],
        name="norm1",
    )
    pack_f = jnp.concatenate([w_gate.T, w_up.T, w_down], axis=0)
    zero = jnp.zeros((), jnp.int32)
    smem1 = [SMEM] + [VMEM] * 11
    if wide:
        at = batch_pieces()
        brow = [(a // 4) ^ y for a in at]
        bcol = [2 * (a % 2) + (a // 2) % 2 for a in at]
        idx = jnp.stack([s, x, y, z] + at + brow + bcol).astype(jnp.int32)
        moved = lax.ppermute(w_output, ("seq", "batch"), OUT_PERM)
        line = call(
            line_body, [sds((16, 512), BF)],
            [gain_first, gain_second, phase_angle, gain_mixer, segment_ids], room=None,
            name="line",
        )[0]
        line_x = xsend(line)
        pack_m, both = call(
            pack_body, [sds((row8, 7 * ch), BF), sds((16, 512), BF)],
            [idx, w_input, w_outgate, far, fg, moved, line, line_x],
            smem1[:8], room=None, name="pack",
        )
        mz1 = lax.ppermute(pack_m, "batch", zshift(1))
        mx0 = xsend(pack_m)
        mz3 = lax.ppermute(after(pack_m, mz1), "batch", zshift(3))
        mx1 = xsend(after(mz1, mx0))
        mz2 = lax.ppermute(after(pack_m, mz3, mx1), "batch", zshift(2))
        mx3 = xsend(after(mz3, mx1))
        xs = seq_gather(after(x_own, far))
        xs[3] = lax.ppermute(after(xs[2], mx3), "seq", CORE)
        mx2 = xsend(after(mz2, mx1, mx3))
        fz1 = lax.ppermute(after(pack_f, mz2), "batch", zshift(1))
        fz3 = lax.ppermute(after(pack_f, fz1), "batch", zshift(3))
        fx0 = xsend(after(pack_f, mx2))
        half = 3 * hu // 2
        fz2a = lax.ppermute(after(pack_f[0:half], fz3), "batch", zshift(2))
        fz2b = lax.ppermute(after(pack_f[half:], fz2a), "batch", zshift(2))
        fx1 = xsend(after(fz1, fx0))
        fx3 = xsend(after(fz3, fx1))
        fx2a = xsend(after(fz2a, fx3))
        fx2b = xsend(after(fz2b, fx3))
        mixes = [pack_m, mz1, mz2, mz3, mx0, mx1, mx2, mx3]
        ffns = [pack_f, fz1, fz2a, fz3, fx0, fx1, fx2a, fx3, fz2b, fx2b]
        lines = jnp.concatenate(
            [both] + [lax.ppermute(after(both, xs[2]), "batch", zshift(k)) for k in (1, 2, 3)], axis=0
        )
        lines = seq_gather(after(lines, mx3))
        cots = seq_gather(after(cp, lines[2]))
        gain1, gain2, cos, sin, gm, lb, keep = call(
            smalls_body,
            [sds((1, width), F32)] * 2 + [sds((1, ch), F32)] * 2
            + [sds((1, 2 * ch), F32), sds((1, ch), F32), sds((4, blk, 1), F32)],
            [idx, *lines, lower_bound[None]], smem1[:6],
            scratch=[
                pltpu.VMEM((1, width), F32), pltpu.VMEM((1, width), F32),
                pltpu.VMEM((2, 1, width), F32),
            ],
            room=None, name="smalls",
        )
        outs_w = []
    else:
        idx = jnp.stack([s, zero, y, zero] + [zero] * 24).astype(jnp.int32)
        xs = seq_gather(x_own)
        cots = seq_gather(cp)
        nat = lambda w: lax.dynamic_slice(w, (0, y * ch), (w.shape[0], ch))
        mix = [nat(w_input), far[:, 0:ch], fg, nat(w_outgate), far[:, ch:]]
        mixes = [lax.all_gather(jnp.concatenate(mix, axis=1), "batch", axis=0, tiled=True)]
        ffns = [lax.all_gather(pack_f, "batch", axis=1, tiled=True)]
        full = lax.all_gather(w_output, "batch", axis=0, tiled=True)
        full = lax.all_gather(full, "seq", axis=1, tiled=True)
        outs_w = [
            jnp.concatenate(
                [
                    lax.dynamic_slice(full, (y * width + start, 0), (ch, width)),
                    lax.dynamic_slice(full, ((1 - y) * width + start, 0), (ch, width)),
                ],
                axis=0,
            )
        ]
        small = jnp.concatenate(
            [gain_first, gain_second, phase_angle, gain_mixer, segment_ids[0].astype(BF)]
        )
        g1n, gmn = gain_first.shape[0], gain_mixer.shape[0]
        every = lax.all_gather(small, ("seq", "batch"), axis=0).reshape(4, nb, -1)
        gain1 = every[:, :, 0:g1n].reshape(1, width).astype(F32)
        gain2 = every[:, :, g1n : 2 * g1n].reshape(1, width).astype(F32)
        phase = every[:, :, 2 * g1n : 3 * g1n].reshape(1, width).astype(F32)
        gainm = every[:, :, 3 * g1n : 3 * g1n + gmn].reshape(2, width).astype(F32)
        ids = lax.dynamic_index_in_dim(every[:, :, 3 * g1n + gmn :], b, 1, False).reshape(tok)
        keep = jnp.concatenate([jnp.zeros((1,), F32), (ids[1:] == ids[:-1]).astype(F32)])
        keep = jnp.swapaxes(keep.reshape(4, 8, blk // 8), 1, 2).reshape(4, blk)
        keep = jnp.where(c == 1, keep[jnp.array([1, 0, 3, 2])], keep)
        keep = jnp.where(y == 1, keep[jnp.array([2, 3, 0, 1])], keep)[:, :, None]
        phase = lax.dynamic_slice(phase, (0, start), (1, ch))
        cos = jnp.cos(phase)
        sin = jnp.sin(phase) * jnp.where(y == 0, 1.0, -1.0).astype(F32)
        lb = lax.dynamic_slice(lower_bound[None, :], (0, start), (1, ch))
        gm = jnp.concatenate(
            [
                lax.dynamic_slice(gainm, (y, start), (1, ch)),
                lax.dynamic_slice(gainm, (1 - y, start), (1, ch)),
            ],
            axis=1,
        )
    early = [fz1] if wide else []
    pieces = len(mixes)
    fpieces = len(ffns)
    sign = jnp.where(y == 0, 1.0, -1.0).astype(F32)

    scan_scratch = [
        pltpu.VMEM((4, 8, 2 * ch), F32), pltpu.VMEM((4, 8, ch), F32),
        pltpu.VMEM((4, 8, 2 * ch), F32),
    ]
    full_tok = pltpu.VMEM((tok, width), BF)
    big = pltpu.VMEM((4, blk, 2 * ch), F32)
    mix_all = mixes + outs_w
    pre, dk, h, kr, k0, k1, sout = call(
        functools.partial(mixer_fwd_body, pieces=pieces),
        [
            sds((4, blk, 5 * ch), BF), sds((4, blk, ch), F32), sds((4, blk, 2 * ch), F32),
            sds((4, blk, 2 * ch), F32), sds((blk, tail), BF), sds((blk, tail), BF),
            sds((2, blk, tail), BF),
        ],
        [idx, *xs, *mix_all, after(gain1, *early), keep, lb, cos, sin, gm],
        [SMEM] + [HBM] * (4 + len(mix_all)) + [VMEM] * 6,
        [HBM] * 7,
        scratch=[
            full_tok, pltpu.VMEM((width, 5 * ch), BF), pltpu.VMEM((2 * ch, width), BF),
            pltpu.VMEM((4, blk, 5 * ch), BF), pltpu.VMEM((4, blk, ch), F32), big, big,
            pltpu.VMEM((blk, tail), BF), pltpu.VMEM((blk, tail), BF),
            pltpu.VMEM((2, blk, tail), BF), big, big, *scan_scratch, dma((48,)),
        ],
        room=None, flops=2 * tok * width * 7 * ch, name="mixer_fwd",
    )
    if wide:
        sout = after(sout, fz3, fx0, *cots[1:3])
    got, near = seq_scatter(k1, lax.ppermute(sout, "seq", CORE))
    if wide:
        near = after(near, fz2a, fx1, cots[3])
    resid, fin, sc = call(
        functools.partial(resid_body, chans=2.0 * width),
        [sds((blk, width), F32), sds((blk, width), BF), sds((blk, 128), F32)],
        [xp, k0, got, near, gain2], name="resid",
    )
    fins = seq_gather(fin)
    if wide:
        fins[3] = lax.ppermute(after(fins[2], fx2a, fz2b), "seq", CORE)
    scat = [sds((blk, width), BF), sds((blk, width), BF), sds((2, blk, width), BF)]
    scat_v = [pltpu.VMEM(v.shape, v.dtype) for v in scat]
    part_f = sds((3 * hu, row8), BF)
    hid, ggu, k02, k12, sout2, kept2, s2 = call(
        functools.partial(ffn_body, pieces=fpieces),
        [sds((tok, hu), BF), sds((tok, 2 * hu), BF)] + scat + [part_f, part_f],
        [idx, *fins, *cots, *ffns], [SMEM] + [HBM] * (8 + fpieces),
        [HBM] * 7,
        scratch=[
            full_tok, full_tok, pltpu.VMEM((3 * hu, width), BF),
            pltpu.VMEM((tok, hu), BF), pltpu.VMEM((tok, 2 * hu), BF), *scat_v,
            pltpu.VMEM(part_f.shape, BF), pltpu.VMEM(part_f.shape, BF), dma((40,)),
        ],
        room=None, flops=10 * tok * width * hu, name="ffn",
    )

    got2 = lax.ppermute(sout2, "seq", CORE)
    far2 = plus(k12, got2[1])
    near2 = lax.ppermute(far2, "seq", YSWAP)
    own_f, kept1, kept3, s1, s3, s0 = call(
        ffn_grad_body,
        [sds((3 * hu, row8), F32)] + [part_f] * 5,
        [idx, after(hid, far2), ggu, *fins, *cots],
        [SMEM, VMEM, VMEM] + [HBM] * 8, scratch=[full_tok, full_tok, dma((8,))],
        room=None, flops=6 * tok * width * hu, name="ffn_grad",
    )
    fsc = Scatter(own_f, kept1, kept3, kept2, s2, s1, s3, s0)
    first_sum = [s1]
    if wide:
        fsc.along_x(2)
        fsc.add(2, s1)
        fsc.along_z(2)
        fsc.along_x(1, fsc.got[2])
        fsc.along_x(3, fsc.got[1])
        first_sum.append(fsc.part[2])
    gres, pay, gg2 = call(
        functools.partial(gresid_body, chans=2.0 * width),
        [sds((blk, width), F32), sds((blk, tail), BF), sds((1, width), F32)],
        [k02, got2, near2, after(cp, *first_sum), resid, xp, sc, gain2], room=None, name="gresid",
    )
    pays = seq_gather(pay)
    if wide:
        fsc.add(1, pay)
        fsc.along_z(1)
        pays[2] = after(pays[2], fsc.part[1])
        pays[3] = lax.ppermute(pays[2], "seq", CORE)
        fsc.add(3, pays[2])
        fsc.along_z(3)
        fsc.along_x(0, fsc.got[3])
        pays[1] = after(pays[1], fsc.part[3])
    part_m = [sds((row8, 7 * ch), F32)] + [sds((row8, 7 * ch), BF)] * 7
    ggm, gph, *msc, k04, k14, sout4 = call(
        functools.partial(bwd_body, pieces=pieces),
        [sds((1, 2 * ch), F32), sds((1, ch), F32)] + part_m + scat,
        [idx, *pays, *xs, *mix_all, pre, dk, h, kr, lb, cos, sin, gain1, gm],
        [SMEM] + [HBM] * (12 + len(mix_all)) + [VMEM] * 5, [VMEM] * 2 + [HBM] * 11,
        scratch=[
            *[pltpu.VMEM(v.shape, v.dtype) for v in part_m + scat],
            pltpu.VMEM((tok, tail), BF), full_tok, pltpu.VMEM((width, 5 * ch), BF),
            pltpu.VMEM((2 * ch, width), BF), pltpu.VMEM((4, blk, 5 * ch), BF),
            pltpu.VMEM((4, blk, ch), F32), big, big, pltpu.VMEM((tok, 2 * ch), BF),
            pltpu.VMEM((tok, 5 * ch), BF), big, *scan_scratch, dma((64,)),
        ],
        room=None, flops=6 * tok * width * 5 * ch, name="bwd",
    )
    msc = Scatter(*msc)
    if wide:
        msc.along_x(2)
        sout4 = after(sout4, *fsc.z.values(), fsc.got[0])
    got4, near4 = seq_scatter(k14, lax.ppermute(sout4, "seq", CORE))
    if wide:
        msc.add(2)
        msc.along_z(2)
        msc.along_x(1, msc.part[2])
        k04 = after(k04, msc.part[2])
    grad_input, gg1 = call(
        gin_body, [sds((blk, width), BF), sds((1, width), F32)],
        [k04, got4, near4, xp, gres, gain1], room=None, name="gin",
    )
    k03, k13, sout3 = call(
        functools.partial(down_body, pieces=fpieces), scat,
        [idx, after(hid, gg1), *ffns], [SMEM, VMEM] + [HBM] * fpieces,
        scratch=[pltpu.VMEM((hu, width), BF), dma((8,))],
        room=None, flops=2 * tok * width * hu, name="down",
    )
    got3, near3 = seq_scatter(k13, lax.ppermute(sout3, "seq", CORE))
    if wide:
        msc.add(1, gg1)
        msc.along_z(1)
        msc.along_x(3, msc.part[1])
        msc.add(3, sout3, msc.z[2])
        msc.along_z(3)
        msc.along_x(0, msc.part[3])
    block_output = call(
        blockout_body, [sds((blk, width), BF)], [resid, k03, got3, near3], name="blockout",
    )[0]

    if wide:
        g_f3 = fsc.total(msc.part[3])
        g_m = msc.total(near3)
        o_back = lax.ppermute(g_m[:, 5 * ch :].astype(BF), ("seq", "batch"), OUT_BACK)
    else:
        def whole(parts):
            lo = jnp.stack([v.astype(F32) for v in parts.kept])
            hi = jnp.stack([v.astype(F32) for v in parts.send])
            return jnp.stack([lo, hi], axis=1).reshape((8,) + parts.send[0].shape)

        f8 = whole(fsc)
        g_f3 = lax.psum_scatter(
            jnp.swapaxes(f8, 0, 1).reshape(3 * hu, width), "batch", scatter_dimension=1,
            tiled=True,
        )
        m8 = whole(msc)
        g_m = lax.psum_scatter(
            m8[:, :, 0 : 5 * ch].reshape(width, 5 * ch), "batch", scatter_dimension=0, tiled=True
        )
        o8 = m8[:, :, 5 * ch :].reshape(2, 2, 2, row8, 2, ch)
        o_full = jnp.transpose(o8, (0, 4, 3, 2, 1, 5)).reshape(2, ch, width)
        spread = jnp.zeros((2, width, width), F32)
        spread = lax.dynamic_update_slice(spread, o_full, (0, start, 0)).reshape(
            2 * width, width
        )
        g_o = lax.psum_scatter(spread, "batch", scatter_dimension=0, tiled=True)
        g_o = lax.psum_scatter(g_o, "seq", scatter_dimension=1, tiled=True)

    far_back = lax.ppermute(
        jnp.concatenate([g_m[:, ch : 2 * ch], g_m[:, 4 * ch : 5 * ch]], axis=1).astype(BF),
        "seq", YSWAP,
    )
    g_f = lax.ppermute(
        g_m[:, 2 * ch : 3 * ch].astype(BF), "seq", [(d, q2) for q2, d in FORGET_PERM]
    )

    if wide:
        g_in, g_og, g_o, g_f = call(
            finish_body,
            [
                sds((row8, 2 * ch), F32), sds((row8, 2 * ch), F32), sds((2 * row8, ch), F32),
                sds((row8, ch), F32),
            ],
            [idx, g_m, far_back, o_back, g_f], [SMEM] + [VMEM] * 4, name="finish",
        )
    else:
        g_f = g_f.astype(F32)
        far_back = far_back.astype(F32)

        def rejoin(nat, farp):
            return jnp.where(
                y == 0,
                jnp.concatenate([nat, farp], axis=1),
                jnp.concatenate([farp, nat], axis=1),
            )

        g_in = rejoin(g_m[:, 0:ch], far_back[:, 0:ch])
        g_og = rejoin(g_m[:, 3 * ch : 4 * ch], far_back[:, ch:])

    ggm2 = jnp.where(
        y == 0,
        ggm.reshape(2, ch),
        jnp.concatenate([ggm[:, ch:], ggm[:, 0:ch]], axis=0),
    )
    spread_gm = lax.dynamic_update_slice(jnp.zeros((2, width), F32), ggm2, (0, start))
    spread_ph = lax.dynamic_update_slice(jnp.zeros((1, width), F32), gph * sign, (0, start))
    nd = 4 * nb
    vec = jnp.concatenate(
        [
            gg1.reshape(nd, -1), gg2.reshape(nd, -1), spread_ph.reshape(nd, -1),
            spread_gm.reshape(nd, -1),
        ],
        axis=1,
    )
    mine = small_sum(after(vec, sout3), msc.got[0], near3) if wide else lax.psum(vec, ("seq", "batch"))
    mine = lax.dynamic_index_in_dim(mine, s * nb + b, 0, False)
    g1n = gain_first.shape[0]
    gg1o = mine[0:g1n]
    gg2o = mine[g1n : 2 * g1n]
    gpho = mine[2 * g1n : 3 * g1n]
    ggmo = mine[3 * g1n :]
    return (
        block_output[None], grad_input[None], gg1o, g_in, g_f, g_og, gpho, ggmo, g_o, gg2o,
        g_f3[0:hu].T, g_f3[hu : 2 * hu].T, g_f3[2 * hu :],
    )


def solution(mesh):
    both = P(("seq", "batch"))
    mat = P("batch", "seq")
    in_specs = (
        P("batch", "seq", None), P("batch", "seq"), P("batch", "seq", None), P(), both, mat,
        mat, mat, both, both, mat, both, mat, mat, P("seq", "batch"),
    )
    out_specs = (
        P("batch", "seq", None), P("batch", "seq", None), both, mat, mat, mat, both, both, mat,
        both, mat, mat, P("seq", "batch"),
    )
    return jax.shard_map(
        per_device, mesh=mesh, in_specs=in_specs, out_specs=out_specs, check_vma=False
    )
```

profile of v0, /device:TPU:3, one launch (start us, length us, event | category | flops | bytes accessed | tf_op | source)
XLA Modules:
  0.0 315.5 jit_solution(11528762225999948101)
XLA Ops:
  2.9 4.0 %collective-permute-start.4 = (bf16[256,256]{1,0:T(8,128)(2,1)}, bf16[256,256]{1,0:T(8,128)(2,1)}, u32[]{:S(2)}, u32[]{:S(2)}) collective-permute-start(bf16[256,256]{1,0:T(8,128)(2,1)} %param.25), channel_id=1, source_target_pairs={{0,0},{1,16},{2,8},{3,24},{4,4},{5,20},{6,12},{7,28},{8,2},{9,18},... | collective-permute-start | bytes 393224 | tf_op jit(solution)/shard_map/ppermute | solution.py:804
  6.8 1.9 collective-permute-start.3
  8.8 1.4 line.1.l_ref
  10.2 1.7 collective-permute-start.5
  13.9 2.0 pack.1
  16.2 1.5 collective-permute-start.8
  17.7 12.6 %collective-permute-done.6.refs_6_.refs_10_ = bf16[128,1792]{1,0:T(8,128)(2,1)S(1)} collective-permute-done((bf16[128,1792]{1,0:T(8,128)(2,1)}, bf16[128,1792]{1,0:T(8,128)(2,1)S(1)}, u32[]{:S(2)}, u32[]{:S(2)}) %collective-permute-start.6) | collective-permute-done | bytes 458784 | tf_op jit(solution)/shard_map/ppermute | solution.py:816
  30.5 1.7 collective-permute-start.7
  33.3 1.4 norm1.1
  35.5 6.7 %collective-permute-done.9.refs_10_.refs_14_ = bf16[128,1792]{1,0:T(8,128)(2,1)S(1)} collective-permute-done((bf16[128,1792]{1,0:T(8,128)(2,1)S(1)}, bf16[128,1792]{1,0:T(8,128)(2,1)S(1)}, u32[]{:S(2)}, u32[]{:S(2)}) %collective-permute-start.9) | collective-permute-done | bytes 458784 | tf_op jit(solution)/shard_map/ppermute | solution.py:725
  42.6 1.6 collective-permute-start.12
  44.4 4.2 %collective-permute-done.2.refs_3_.refs_7_ = bf16[256,1024]{1,0:T(8,128)(2,1)} collective-permute-done((bf16[256,1024]{1,0:T(8,128)(2,1)}, bf16[256,1024]{1,0:T(8,128)(2,1)}, u32[]{:S(2)}, u32[]{:S(2)}) %collective-permute-start.2) | collective-permute-done | bytes 524320 | tf_op jit(solution)/shard_map/ppermute | solution.py:706
  48.6 1.4 collective-permute-start.15
  50.0 1.8 collective-permute-start.16
  51.9 13.6 %collective-permute-done.12.refs_7_.refs_11_ = bf16[128,1792]{1,0:T(8,128)(2,1)} collective-permute-done((bf16[128,1792]{1,0:T(8,128)(2,1)S(1)}, bf16[128,1792]{1,0:T(8,128)(2,1)}, u32[]{:S(2)}, u32[]{:S(2)}) %collective-permute-start.12) | collective-permute-done | bytes 458784 | tf_op jit(solution)/shard_map/ppermute | solution.py:820
  65.5 2.0 collective-permute-start.1
  68.7 2.2 collective-permute-done.18.v2
  70.8 1.6 collective-permute-start.17
  75.2 2.2 smalls.1
  77.4 2.3 collective-permute-done.13.refs_11_.refs_15_
  80.8 2.4 collective-permute-done.20.refs_10_.refs_3_
  84.1 1.4 collective-permute-start.21
  85.5 11.1 %mixer_fwd.1 = (bf16[4,256,1280]{2,1,0:T(8,128)(2,1)}, f32[4,256,256]{2,1,0:T(8,128)}, f32[4,256,512]{2,1,0:T(8,128)}, f32[4,256,512]{2,1,0:T(8,128)}, bf16[256,...) custom-call(s32[28]{0:T(128)} %stack.115.idx_ref.refs_0_, ...), custom_call_target="tpu_custom_call" | custom-call | flops 40580964352 | bytes 16004208 | tf_op jit(solution)/shard_map/mixer_fwd/pallas_call | solution.py:79
  96.8 2.0 collective-permute-start.25
  98.9 2.7 collective-permute-done.25.got_ref
  105.6 10.9 %collective-permute-done.28.refs_14_.refs_7_ = bf16[2112,128]{1,0:T(8,128)(2,1)S(1)} collective-permute-done((bf16[2112,128]{1,0:T(8,128)(2,1)}, bf16[2112,128]{1,0:T(8,128)(2,1)S(1)}, u32[]{:S(2)}, u32[]{:S(2)}) %collective-permute-start.28) | collective-permute-done | bytes 540704 | tf_op jit(solution)/shard_map/ppermute | solution.py:725
  117.1 2.2 collective-permute-done.27.refs_11_.refs_4_
  121.5 1.5 collective-permute-start.31
  123.0 6.1 %collective-permute-done.32.refs_16_.refs_9_ = bf16[2112,128]{1,0:T(8,128)(2,1)S(1)} collective-permute-done((bf16[2112,128]{1,0:T(8,128)(2,1)}, bf16[2112,128]{1,0:T(8,128)(2,1)S(1)}, u32[]{:S(2)}, u32[]{:S(2)}) %collective-permute-start.32) | collective-permute-done | bytes 540704 | tf_op jit(solution)/shard_map/ppermute | solution.py:725
  129.7 2.6 collective-permute-start.30
  132.3 5.3 %collective-permute-done.34.refs_17_.refs_10_ = bf16[1056,128]{1,0:T(8,128)(2,1)S(1)} collective-permute-done((bf16[1056,128]{1,0:T(8,128)(2,1)S(1)}, bf16[1056,128]{1,0:T(8,128)(2,1)S(1)}, u32[]{:S(2)}, u32[]{:S(2)}) %collective-permute-start.34) | collective-permute-done | bytes 270368 | tf_op jit(solution)/shard_map/ppermute | solution.py:830
  138.7 7.6 %collective-permute-done.36.refs_18_.refs_11_ = bf16[1056,128]{1,0:T(8,128)(2,1)S(1)} collective-permute-done((bf16[1056,128]{1,0:T(8,128)(2,1)S(1)}, bf16[1056,128]{1,0:T(8,128)(2,1)S(1)}, u32[]{:S(2)}, u32[]{:S(2)}) %collective-permute-start.36) | collective-permute-done | bytes 270368 | tf_op jit(solution)/shard_map/ppermute | solution.py:725
  147.2 15.4 %ffn.1 = (bf16[1024,704]{1,0:T(8,128)(2,1)}, bf16[1024,1408]{1,0:T(8,128)(2,1)}, bf16[256,1024]{1,0:T(8,128)(2,1)}, bf16[256,1024]{1,0:T(8,128)(2,1)}, bf16[2,25...) custom-call(s32[28]{0:T(128)} %stack.115.idx_ref.refs_0_, bf16[256,1024]{1,0:T(8,128)(2,1)} %copy-done.3, ...), custom_call_target="tpu_custom_call" | custom-call | flops 76819750912 | bytes 16023664 | tf_op jit(solution)/shard_map/ffn/pallas_call | solution.py:79
  164.0 2.0 collective-permute-done.37.got_ref
  166.0 2.4 fusion.3
  169.4 9.5 %ffn_grad.1 = (f32[2112,128]{1,0:T(8,128)}, bf16[2112,128]{1,0:T(8,128)(2,1)}, bf16[2112,128]{1,0:T(8,128)(2,1)}, bf16[2112,128]{1,0:T(8,128)(2,1)}, bf16[2112,1...) custom-call(s32[28]{0:T(128)} %stack.115.idx_ref.refs_0_, bf16[1024,704]{1,0:T(8,128)(2,1)} %get-tuple-element.195.h_ref.refs_1_, ...), custom_call_target="tpu_custom_call" | custom-call | flops 47291850752 | bytes 12304496 | tf_op jit(solution)/shard_map/ffn_grad/pallas_call | solution.py:79
  179.6 2.0 add_convert_fusion.2
  182.2 4.2 %gresid.1 = (f32[256,1024]{1,0:T(8,128)}, bf16[256,1152]{1,0:T(8,128)(2,1)}, f32[1,1024]{1,0:T(1,128)}) custom-call(bf16[256,1024]{1,0:T(8,128)(2,1)} %get-tuple-element.159.own_ref, bf16[2,256,1024]{2,1,0:T(8,128)(2,1)} %copy-done.24, bf16[256,1024]{1,0:T(8,128)(2,1)} %collective-permute-done.38.ry_ref, ...), custom_call_target="tpu_custom_call" | custom-call | flops 3000000000 | bytes 5971968 | tf_op jit(solution)/shard_map/gresid/pallas_call | solution.py:79
  187.1 1.5 collective-permute-start.40
  188.6 3.8 %collective-permute-done.42 = bf16[2112,128]{1,0:T(8,128)(2,1)} collective-permute-done((bf16[2112,128]{1,0:T(8,128)(2,1)}, bf16[2112,128]{1,0:T(8,128)(2,1)}, u32[]{:S(2)}, u32[]{:S(2)}) %collective-permute-start.42) | collective-permute-done | bytes 540704 | tf_op jit(solution)/shard_map/ppermute | solution.py:725
  193.1 2.2 add_convert_fusion.1
  195.2 9.8 %collective-permute-done.43 = bf16[2112,128]{1,0:T(8,128)(2,1)S(1)} collective-permute-done((bf16[2112,128]{1,0:T(8,128)(2,1)}, bf16[2112,128]{1,0:T(8,128)(2,1)S(1)}, u32[]{:S(2)}, u32[]{:S(2)}) %collective-permute-start.43) | collective-permute-done | bytes 540704 | tf_op jit(solution)/shard_map/ppermute | solution.py:725
  205.6 2.6 collective-permute-start.44
  209.2 3.2 %collective-permute-start.48 = (bf16[2112,128]{1,0:T(8,128)(2,1)}, bf16[2112,128]{1,0:T(8,128)(2,1)}, u32[]{:S(2)}, u32[]{:S(2)}) collective-permute-start(bf16[2112,128]{1,0:T(8,128)(2,1)} %add_convert_fusion), channel_id=1, source_target_pairs={{0,6},{1,7},{2,0},{3,1},{4,2},{5,3},{6,4},{7,5},{8,14},{9,15},{10,... | collective-permute-start | bytes 1622024 | tf_op jit(solution)/shard_map/ppermute | solution.py:746
  213.2 18.2 %bwd.1 = (f32[1,512]{1,0:T(1,128)}, f32[1,256]{1,0:T(1,128)}, f32[128,1792]{1,0:T(8,128)}, bf16[128,1792]{1,0:T(8,128)(2,1)}, bf16[128,1792]{1,0:T(8,128)(2,1)},...) custom-call(s32[28]{0:T(128)} %stack.115.idx_ref.refs_0_, ...), custom_call_target="tpu_custom_call" | custom-call | flops 83530637312 | bytes 22229104 | tf_op jit(solution)/shard_map/bwd/pallas_call | solution.py:79
  235.8 1.6 fusion.2
  237.9 6.7 %collective-permute-done.45 = bf16[128,1792]{1,0:T(8,128)(2,1)S(1)} collective-permute-done((bf16[128,1792]{1,0:T(8,128)(2,1)}, bf16[128,1792]{1,0:T(8,128)(2,1)S(1)}, u32[]{:S(2)}, u32[]{:S(2)}) %collective-permute-start.45) | collective-permute-done | bytes 458784 | tf_op jit(solution)/shard_map/ppermute | solution.py:725
  246.6 4.2 %collective-permute-done.51.ry_ref = bf16[256,1024]{1,0:T(8,128)(2,1)S(1)} collective-permute-done((bf16[256,1024]{1,0:T(8,128)(2,1)S(1)}, bf16[256,1024]{1,0:T(8,128)(2,1)S(1)}, u32[]{:S(2)}, u32[]{:S(2)}) %collective-permute-start.51) | collective-permute-done | bytes 524320 | tf_op jit(solution)/shard_map/ppermute | solution.py:714
  251.6 3.7 %gin.1 = (bf16[256,1024]{1,0:T(8,128)(2,1)}, f32[1,1024]{1,0:T(1,128)}) custom-call(bf16[256,1024]{1,0:T(8,128)(2,1)} %get-tuple-element.187.own_ref, bf16[2,256,1024]{2,1,0:T(8,128)(2,1)} %copy-done.23, bf16[256,1024]{1,0:T(8,128)(2,1)} %copy-done.39, bf16[256,1024]{1,0:T(8,128)(2,1)} %copy-done.6, f32[256,1024]{1,0:T(8,128)} %get-tuple-element.193.gres_ref, ...), custom_call_target="tpu_custom_call" | custom-call | flops 3000000000 | bytes 4202496 | tf_op jit(solution)/shard_map/gin/pallas_call | solution.py:79
  255.3 1.7 collective-permute-done.58
  257.0 2.0 add_convert_fusion.4
  259.9 5.6 %down.1 = (bf16[256,1024]{1,0:T(8,128)(2,1)}, bf16[256,1024]{1,0:T(8,128)(2,1)}, bf16[2,256,1024]{2,1,0:T(8,128)(2,1)}) custom-call(s32[28]{0:T(128)} %stack.115.idx_ref.refs_0_, bf16[1024,704]{1,0:T(8,128)(2,1)} %get-tuple-element.195.h_ref.refs_1_, bf16[2112,128]{1,0:T(8,128)(2,1)} %copy-done.20, ...), custom_call_target="tpu_custom_call" | custom-call | flops 17763950592 | bytes 7864432 | tf_op jit(solution)/shard_map/down/pallas_call | solution.py:79
  265.5 2.1 collective-permute-start.52
  271.0 2.3 collective-permute-done.55
  274.3 1.8 collective-permute-done.56
  280.2 1.7 convert_add_fusion.1
  282.9 5.2 %collective-permute-done.60 = bf16[128,1792]{1,0:T(8,128)(2,1)S(1)} collective-permute-done((bf16[128,1792]{1,0:T(8,128)(2,1)}, bf16[128,1792]{1,0:T(8,128)(2,1)S(1)}, u32[]{:S(2)}, u32[]{:S(2)}) %collective-permute-start.60) | collective-permute-done | bytes 458784 | tf_op jit(solution)/shard_map/ppermute | solution.py:725
  288.1 2.1 collective-permute-done.53.ry_ref
  290.8 2.7 collective-permute-start.63
  293.5 5.0 %collective-permute-done.65 = bf16[128,1792]{1,0:T(8,128)(2,1)S(1)} collective-permute-done((bf16[128,1792]{1,0:T(8,128)(2,1)S(1)}, bf16[128,1792]{1,0:T(8,128)(2,1)S(1)}, u32[]{:S(2)}, u32[]{:S(2)}) %collective-permute-start.65) | collective-permute-done | bytes 458784 | tf_op jit(solution)/shard_map/ppermute | solution.py:746
  300.2 3.9 %collective-permute-start.68 = (bf16[128,256]{1,0:T(8,128)(2,1)S(1)}, bf16[128,256]{1,0:T(8,128)(2,1)S(1)}, u32[]{:S(2)}, u32[]{:S(2)}) collective-permute-start(bf16[128,256]{1,0:T(8,128)(2,1)S(1)} %get-tuple-element.228), channel_id=1, source_target_pairs={{0,0},{8,16},{16,8},{24,24},{1,1},{9,17},{17,9},{25,25},{2,2},{10,... | collective-permute-start | bytes 196616 | tf_op jit(solution)/shard_map/ppermute | solution.py:1070
  305.5 2.8 collective-permute-start.67
  309.5 4.0 %collective-permute-done.67.o_in = bf16[128,512]{1,0:T(8,128)(2,1)S(1)} collective-permute-done((bf16[128,512]{1,0:T(8,128)(2,1)S(1)}, bf16[128,512]{1,0:T(8,128)(2,1)S(1)}, u32[]{:S(2)}, u32[]{:S(2)}) %collective-permute-start.67) | collective-permute-done | bytes 131104 | tf_op jit(solution)/shard_map/ppermute | solution.py:1041
  313.6 1.5 finish.1
  (244 shorter events, 53.0 us)
Async XLA Ops:
  1.6 11.7 %collective-permute-start = (bf16[128,512]{1,0:T(8,128)(2,1)S(1)}, bf16[128,512]{1,0:T(8,128)(2,1)S(1)}, u32[]{:S(2)}, u32[]{:S(2)}) collective-permute-start(bf16[128,512]{1,0:T(8,128)(2,1)S(1)} %pad_maximum_fusion.3), channel_id=1, source_target_pairs={{0,16},{8,24},{16,0},{24,8},{1,17},{9,25},{17,1},{25,9},{2,18},{10... | collective-permute-start | bytes 393224 | tf_op jit(solution)/shard_map/ppermute | solution.py:790
  2.9 10.4 %collective-permute-start.4 = (bf16[256,256]{1,0:T(8,128)(2,1)}, bf16[256,256]{1,0:T(8,128)(2,1)}, u32[]{:S(2)}, u32[]{:S(2)}) collective-permute-start(bf16[256,256]{1,0:T(8,128)(2,1)} %param.25), channel_id=1, source_target_pairs={{0,0},{1,16},{2,8},{3,24},{4,4},{5,20},{6,12},{7,28},{8,2},{9,18},... | collective-permute-start | bytes 393224 | tf_op jit(solution)/shard_map/ppermute | solution.py:804
  6.8 6.4 %collective-permute-start.3 = (bf16[128,256]{1,0:T(8,128)(2,1)}, bf16[128,256]{1,0:T(8,128)(2,1)S(1)}, u32[]{:S(2)}, u32[]{:S(2)}) collective-permute-start(bf16[128,256]{1,0:T(8,128)(2,1)} %param.21), channel_id=1, source_target_pairs={{0,0},{16,8},{8,16},{24,24},{1,1},{17,9},{9,17},{25,25},{2,2},{18,... | collective-permute-start | bytes 196616 | tf_op jit(solution)/shard_map/ppermute | solution.py:791
  10.2 3.0 collective-permute-start.5
  15.9 14.4 %collective-permute-start.6 = (bf16[128,1792]{1,0:T(8,128)(2,1)}, bf16[128,1792]{1,0:T(8,128)(2,1)S(1)}, u32[]{:S(2)}, u32[]{:S(2)}) collective-permute-start(bf16[128,1792]{1,0:T(8,128)(2,1)} %get-tuple-element.126.refs_5_.refs_9_), channel_id=1, source_target_pairs={{0,2},{1,3},{2,4},{3,5},{4,6},{5,7},{6,0},{7,1},{8,10},{9,11},{10,... | collective-permute-start | bytes 1376264 | tf_op jit(solution)/shard_map/ppermute | solution.py:816
  16.2 14.0 %collective-permute-start.8 = (bf16[128,1792]{1,0:T(8,128)(2,1)}, bf16[128,1792]{1,0:T(8,128)(2,1)S(1)}, u32[]{:S(2)}, u32[]{:S(2)}) collective-permute-start(bf16[128,1792]{1,0:T(8,128)(2,1)} %get-tuple-element.126.refs_5_.refs_9_), channel_id=1, source_target_pairs={{0,1},{1,0},{2,3},{3,2},{4,5},{5,4},{6,7},{7,6},{8,9},{9,8},{10,11... | collective-permute-start | bytes 1376264 | tf_op jit(solution)/shard_map/ppermute | solution.py:725
  30.3 11.9 %collective-permute-start.9 = (bf16[128,1792]{1,0:T(8,128)(2,1)S(1)}, bf16[128,1792]{1,0:T(8,128)(2,1)S(1)}, u32[]{:S(2)}, u32[]{:S(2)}) collective-permute-start(bf16[128,1792]{1,0:T(8,128)(2,1)S(1)} %collective-permute-done.6.refs_6_.refs_10_), channel_id=1, source_target_pairs={{0,1},{1,0},{2,3},{3,2},{4,5},{5,4},{6,7},{7,6},{8,9},{9,8},{10,11... | collective-permute-start | bytes 1376264 | tf_op jit(solution)/shard_map/ppermute | solution.py:725
  30.5 12.1 %collective-permute-start.7 = (bf16[128,1792]{1,0:T(8,128)(2,1)}, bf16[128,1792]{1,0:T(8,128)(2,1)S(1)}, u32[]{:S(2)}, u32[]{:S(2)}) collective-permute-start(bf16[128,1792]{1,0:T(8,128)(2,1)} %get-tuple-element.126.refs_5_.refs_9_), channel_id=1, source_target_pairs={{0,6},{1,7},{2,0},{3,1},{4,2},{5,3},{6,4},{7,5},{8,14},{9,15},{10,... | collective-permute-start | bytes 1376264 | tf_op jit(solution)/shard_map/ppermute | solution.py:818
  35.5 13.1 %collective-permute-start.2 = (bf16[256,1024]{1,0:T(8,128)(2,1)}, bf16[256,1024]{1,0:T(8,128)(2,1)}, u32[]{:S(2)}, u32[]{:S(2)}) collective-permute-start(bf16[256,1024]{1,0:T(8,128)(2,1)} %get-tuple-element.120.refs_1_.refs_5_), channel_id=1, source_target_pairs={{0,16},{8,24},{16,0},{24,8},{1,17},{9,25},{17,1},{25,9},{2,18},{10... | collective-permute-start | bytes 1572872 | tf_op jit(solution)/shard_map/ppermute | solution.py:706
  42.6 22.8 %collective-permute-start.12 = (bf16[128,1792]{1,0:T(8,128)(2,1)S(1)}, bf16[128,1792]{1,0:T(8,128)(2,1)}, u32[]{:S(2)}, u32[]{:S(2)}) collective-permute-start(bf16[128,1792]{1,0:T(8,128)(2,1)S(1)} %copy-done.40), channel_id=1, source_target_pairs={{0,4},{1,5},{2,6},{3,7},{4,0},{5,1},{6,2},{7,3},{8,12},{9,13},{10,... | collective-permute-start | bytes 1376264 | tf_op jit(solution)/shard_map/ppermute | solution.py:820
  44.2 23.2 %collective-permute-start.10 = (bf16[128,1792]{1,0:T(8,128)(2,1)S(1)}, bf16[128,1792]{1,0:T(8,128)(2,1)S(1)}, u32[]{:S(2)}, u32[]{:S(2)}) collective-permute-start(bf16[128,1792]{1,0:T(8,128)(2,1)S(1)} %collective-permute-done.7.refs_8_.refs_12_), channel_id=1, source_target_pairs={{0,1},{1,0},{2,3},{3,2},{4,5},{5,4},{6,7},{7,6},{8,9},{9,8},{10,11... | collective-permute-start | bytes 1376264 | tf_op jit(solution)/shard_map/ppermute | solution.py:725
  48.6 18.9 %collective-permute-start.14 = (bf16[16,512]{1,0:T(8,128)(2,1)S(1)}, bf16[16,512]{1,0:T(8,128)(2,1)S(1)}, u32[]{:S(2)}, u32[]{:S(2)}) collective-permute-start(bf16[16,512]{1,0:T(8,128)(2,1)S(1)} %copy-done.26), channel_id=1, source_target_pairs={{0,2},{1,3},{2,4},{3,5},{4,6},{5,7},{6,0},{7,1},{8,10},{9,11},{10,... | collective-permute-start | bytes 49160 | tf_op jit(solution)/shard_map/ppermute | solution.py:838
  48.6 19.0 %collective-permute-start.15 = (bf16[16,512]{1,0:T(8,128)(2,1)S(1)}, bf16[16,512]{1,0:T(8,128)(2,1)S(1)}, u32[]{:S(2)}, u32[]{:S(2)}) collective-permute-start(bf16[16,512]{1,0:T(8,128)(2,1)S(1)} %copy-done.26), channel_id=1, source_target_pairs={{0,4},{1,5},{2,6},{3,7},{4,0},{5,1},{6,2},{7,3},{8,12},{9,13},{10,... | collective-permute-start | bytes 49160 | tf_op jit(solution)/shard_map/ppermute | solution.py:838
  50.0 17.6 %collective-permute-start.16 = (bf16[16,512]{1,0:T(8,128)(2,1)S(1)}, bf16[16,512]{1,0:T(8,128)(2,1)S(1)}, u32[]{:S(2)}, u32[]{:S(2)}) collective-permute-start(bf16[16,512]{1,0:T(8,128)(2,1)S(1)} %copy-done.26), channel_id=1, source_target_pairs={{0,6},{1,7},{2,0},{3,1},{4,2},{5,3},{6,4},{7,5},{8,14},{9,15},{10,... | collective-permute-start | bytes 49160 | tf_op jit(solution)/shard_map/ppermute | solution.py:838
  65.5 18.6 %collective-permute-start.1 = (bf16[256,1024]{1,0:T(8,128)(2,1)}, bf16[256,1024]{1,0:T(8,128)(2,1)}, u32[]{:S(2)}, u32[]{:S(2)}) collective-permute-start(bf16[256,1024]{1,0:T(8,128)(2,1)} %get-tuple-element.120.refs_1_.refs_5_), channel_id=1, source_target_pairs={{0,8},{8,0},{16,24},{24,16},{1,9},{9,1},{17,25},{25,17},{2,10},{10... | collective-permute-start | bytes 1572872 | tf_op jit(solution)/shard_map/ppermute | solution.py:707
  67.5 15.7 %collective-permute-start.20 = (bf16[2112,128]{1,0:T(8,128)(2,1)S(1)}, bf16[2112,128]{1,0:T(8,128)(2,1)}, u32[]{:S(2)}, u32[]{:S(2)}) collective-permute-start(bf16[2112,128]{1,0:T(8,128)(2,1)S(1)} %pad_maximum_fusion.refs_9_.refs_2_), channel_id=1, source_target_pairs={{0,2},{1,3},{2,4},{3,5},{4,6},{5,7},{6,0},{7,1},{8,10},{9,11},{10,... | collective-permute-start | bytes 1622024 | tf_op jit(solution)/shard_map/ppermute | solution.py:825
  67.5 18.0 %collective-permute-start.11 = (bf16[256,1024]{1,0:T(8,128)(2,1)}, bf16[256,1024]{1,0:T(8,128)(2,1)}, u32[]{:S(2)}, u32[]{:S(2)}) collective-permute-start(bf16[256,1024]{1,0:T(8,128)(2,1)} %collective-permute-done.2.refs_3_.refs_7_), channel_id=1, source_target_pairs={{0,8},{8,0},{16,24},{24,16},{1,9},{9,1},{17,25},{25,17},{2,10},{10... | collective-permute-start | bytes 1572872 | tf_op jit(solution)/shard_map/ppermute | solution.py:823
  67.6 3.2 %collective-permute-start.18 = (bf16[64,512]{1,0:T(8,128)(2,1)S(1)}, bf16[64,512]{1,0:T(8,128)(2,1)S(1)}, u32[]{:S(2)}, u32[]{:S(2)}) collective-permute-start(bf16[64,512]{1,0:T(8,128)(2,1)S(1)} %pad_maximum_fusion.5.v0), channel_id=1, source_target_pairs={{0,16},{8,24},{16,0},{24,8},{1,17},{9,25},{17,1},{25,9},{2,18},{10... | collective-permute-start | bytes 196616 | tf_op jit(solution)/shard_map/ppermute | solution.py:706
  67.7 12.0 %collective-permute-start.13 = (bf16[128,1792]{1,0:T(8,128)(2,1)}, bf16[128,1792]{1,0:T(8,128)(2,1)}, u32[]{:S(2)}, u32[]{:S(2)}) collective-permute-start(bf16[128,1792]{1,0:T(8,128)(2,1)} %collective-permute-done.12.refs_7_.refs_11_), channel_id=1, source_target_pairs={{0,1},{1,0},{2,3},{3,2},{4,5},{5,4},{6,7},{7,6},{8,9},{9,8},{10,11... | collective-permute-start | bytes 1376264 | tf_op jit(solution)/shard_map/ppermute | solution.py:725
  74.6 22.0 %collective-permute-start.23 = (bf16[256,1024]{1,0:T(8,128)(2,1)}, bf16[256,1024]{1,0:T(8,128)(2,1)}, u32[]{:S(2)}, u32[]{:S(2)}) collective-permute-start(bf16[256,1024]{1,0:T(8,128)(2,1)} %get-tuple-element.168.refs_5_.c0.c_ref), channel_id=1, source_target_pairs={{0,8},{8,0},{16,24},{24,16},{1,9},{9,1},{17,25},{25,17},{2,10},{10... | collective-permute-start | bytes 1572872 | tf_op jit(solution)/shard_map/ppermute | solution.py:707
  79.8 16.8 %collective-permute-start.24 = (bf16[256,1024]{1,0:T(8,128)(2,1)}, bf16[256,1024]{1,0:T(8,128)(2,1)}, u32[]{:S(2)}, u32[]{:S(2)}) collective-permute-start(bf16[256,1024]{1,0:T(8,128)(2,1)} %get-tuple-element.168.refs_5_.c0.c_ref), channel_id=1, source_target_pairs={{0,16},{8,24},{16,0},{24,8},{1,17},{9,25},{17,1},{25,9},{2,18},{10... | collective-permute-start | bytes 1572872 | tf_op jit(solution)/shard_map/ppermute | solution.py:706
  83.2 13.4 %collective-permute-start.22 = (bf16[2112,128]{1,0:T(8,128)(2,1)S(1)}, bf16[2112,128]{1,0:T(8,128)(2,1)}, u32[]{:S(2)}, u32[]{:S(2)}) collective-permute-start(bf16[2112,128]{1,0:T(8,128)(2,1)S(1)} %pad_maximum_fusion.refs_9_.refs_2_), channel_id=1, source_target_pairs={{0,1},{1,0},{2,3},{3,2},{4,5},{5,4},{6,7},{7,6},{8,9},{9,8},{10,11... | collective-permute-start | bytes 1622024 | tf_op jit(solution)/shard_map/ppermute | solution.py:725
  84.1 12.8 %collective-permute-start.21 = (bf16[2112,128]{1,0:T(8,128)(2,1)S(1)}, bf16[2112,128]{1,0:T(8,128)(2,1)}, u32[]{:S(2)}, u32[]{:S(2)}) collective-permute-start(bf16[2112,128]{1,0:T(8,128)(2,1)S(1)} %pad_maximum_fusion.refs_9_.refs_2_), channel_id=1, source_target_pairs={{0,6},{1,7},{2,0},{3,1},{4,2},{5,3},{6,4},{7,5},{8,14},{9,15},{10,... | collective-permute-start | bytes 1622024 | tf_op jit(solution)/shard_map/ppermute | solution.py:826
  96.8 4.7 %collective-permute-start.25 = (bf16[2,256,1152]{2,1,0:T(8,128)(2,1)}, bf16[2,256,1152]{2,1,0:T(8,128)(2,1)S(1)}, u32[]{:S(2)}, u32[]{:S(2)}) collective-permute-start(bf16[2,256,1152]{2,1,0:T(8,128)(2,1)} %get-tuple-element.145), channel_id=1, source_target_pairs={{0,8},{8,0},{16,24},{24,16},{1,9},{9,1},{17,25},{25,17},{2,10},{10... | collective-permute-start | bytes 3538952 | tf_op jit(solution)/shard_map/ppermute | solution.py:930
  102.9 16.5 %collective-permute-start.26 = (bf16[256,1152]{1,0:T(8,128)(2,1)S(1)}, bf16[256,1152]{1,0:T(8,128)(2,1)S(1)}, u32[]{:S(2)}, u32[]{:S(2)}) collective-permute-start(bf16[256,1152]{1,0:T(8,128)(2,1)S(1)} %fusion), channel_id=1, source_target_pairs={{0,16},{8,24},{16,0},{24,8},{1,17},{9,25},{17,1},{25,9},{2,18},{10... | collective-permute-start | bytes 1769480 | tf_op jit(solution)/shard_map/ppermute | solution.py:714
  103.0 13.6 %collective-permute-start.28 = (bf16[2112,128]{1,0:T(8,128)(2,1)}, bf16[2112,128]{1,0:T(8,128)(2,1)S(1)}, u32[]{:S(2)}, u32[]{:S(2)}) collective-permute-start(bf16[2112,128]{1,0:T(8,128)(2,1)} %collective-permute-done.20.refs_10_.refs_3_), channel_id=1, source_target_pairs={{0,1},{1,0},{2,3},{3,2},{4,5},{5,4},{6,7},{7,6},{8,9},{9,8},{10,11... | collective-permute-start | bytes 1622024 | tf_op jit(solution)/shard_map/ppermute | solution.py:725
  103.6 13.5 %collective-permute-start.29 = (bf16[256,1024]{1,0:T(8,128)(2,1)}, bf16[256,1024]{1,0:T(8,128)(2,1)S(1)}, u32[]{:S(2)}, u32[]{:S(2)}) collective-permute-start(bf16[256,1024]{1,0:T(8,128)(2,1)} %collective-permute-done.24.refs_7_.c2), channel_id=1, source_target_pairs={{0,8},{8,0},{16,24},{24,16},{1,9},{9,1},{17,25},{25,17},{2,10},{10... | collective-permute-start | bytes 1572872 | tf_op jit(solution)/shard_map/ppermute | solution.py:708
  104.5 14.9 %collective-permute-start.27 = (bf16[1056,128]{1,0:T(8,128)(2,1)S(1)}, bf16[1056,128]{1,0:T(8,128)(2,1)S(1)}, u32[]{:S(2)}, u32[]{:S(2)}) collective-permute-start(bf16[1056,128]{1,0:T(8,128)(2,1)S(1)} %get-tuple-element.147), channel_id=1, source_target_pairs={{0,4},{1,5},{2,6},{3,7},{4,0},{5,1},{6,2},{7,3},{8,12},{9,13},{10,... | collective-permute-start | bytes 811016 | tf_op jit(solution)/shard_map/ppermute | solution.py:829
  116.5 12.6 %collective-permute-start.32 = (bf16[2112,128]{1,0:T(8,128)(2,1)}, bf16[2112,128]{1,0:T(8,128)(2,1)S(1)}, u32[]{:S(2)}, u32[]{:S(2)}) collective-permute-start(bf16[2112,128]{1,0:T(8,128)(2,1)} %collective-permute-done.21.refs_12_.refs_5_), channel_id=1, source_target_pairs={{0,1},{1,0},{2,3},{3,2},{4,5},{5,4},{6,7},{7,6},{8,9},{9,8},{10,11... | collective-permute-start | bytes 1622024 | tf_op jit(solution)/shard_map/ppermute | solution.py:725
  121.5 16.1 %collective-permute-start.31 = (bf16[256,1024]{1,0:T(8,128)(2,1)S(1)}, bf16[256,1024]{1,0:T(8,128)(2,1)S(1)}, u32[]{:S(2)}, u32[]{:S(2)}) collective-permute-start(bf16[256,1024]{1,0:T(8,128)(2,1)S(1)} %get-tuple-element.152.refs_1_.x0), channel_id=1, source_target_pairs={{0,16},{8,24},{16,0},{24,8},{1,17},{9,25},{17,1},{25,9},{2,18},{10... | collective-permute-start | bytes 1572872 | tf_op jit(solution)/shard_map/ppermute | solution.py:706
  123.0 14.6 %collective-permute-start.34 = (bf16[1056,128]{1,0:T(8,128)(2,1)S(1)}, bf16[1056,128]{1,0:T(8,128)(2,1)S(1)}, u32[]{:S(2)}, u32[]{:S(2)}) collective-permute-start(bf16[1056,128]{1,0:T(8,128)(2,1)S(1)} %get-tuple-element.155), channel_id=1, source_target_pairs={{0,4},{1,5},{2,6},{3,7},{4,0},{5,1},{6,2},{7,3},{8,12},{9,13},{10,... | collective-permute-start | bytes 811016 | tf_op jit(solution)/shard_map/ppermute | solution.py:830
  129.1 8.5 %collective-permute-start.33 = (bf16[1056,128]{1,0:T(8,128)(2,1)S(1)}, bf16[1056,128]{1,0:T(8,128)(2,1)S(1)}, u32[]{:S(2)}, u32[]{:S(2)}) collective-permute-start(bf16[1056,128]{1,0:T(8,128)(2,1)S(1)} %collective-permute-done.27.refs_11_.refs_4_), channel_id=1, source_target_pairs={{0,1},{1,0},{2,3},{3,2},{4,5},{5,4},{6,7},{7,6},{8,9},{9,8},{10,11... | collective-permute-start | bytes 811016 | tf_op jit(solution)/shard_map/ppermute | solution.py:725
  129.7 16.6 %collective-permute-start.30 = (bf16[256,1024]{1,0:T(8,128)(2,1)S(1)}, bf16[256,1024]{1,0:T(8,128)(2,1)S(1)}, u32[]{:S(2)}, u32[]{:S(2)}) collective-permute-start(bf16[256,1024]{1,0:T(8,128)(2,1)S(1)} %get-tuple-element.152.refs_1_.x0), channel_id=1, source_target_pairs={{0,8},{8,0},{16,24},{24,16},{1,9},{9,1},{17,25},{25,17},{2,10},{10... | collective-permute-start | bytes 1572872 | tf_op jit(solution)/shard_map/ppermute | solution.py:707
  137.6 9.5 %collective-permute-start.35 = (bf16[256,1024]{1,0:T(8,128)(2,1)S(1)}, bf16[256,1024]{1,0:T(8,128)(2,1)}, u32[]{:S(2)}, u32[]{:S(2)}) collective-permute-start(bf16[256,1024]{1,0:T(8,128)(2,1)S(1)} %collective-permute-done.31.refs_3_.x2), channel_id=1, source_target_pairs={{0,8},{8,0},{16,24},{24,16},{1,9},{9,1},{17,25},{25,17},{2,10},{10... | collective-permute-start | bytes 1572872 | tf_op jit(solution)/shard_map/ppermute | solution.py:940
  138.2 8.1 %collective-permute-start.36 = (bf16[1056,128]{1,0:T(8,128)(2,1)S(1)}, bf16[1056,128]{1,0:T(8,128)(2,1)S(1)}, u32[]{:S(2)}, u32[]{:S(2)}) collective-permute-start(bf16[1056,128]{1,0:T(8,128)(2,1)S(1)} %collective-permute-done.34.refs_17_.refs_10_), channel_id=1, source_target_pairs={{0,1},{1,0},{2,3},{3,2},{4,5},{5,4},{6,7},{7,6},{8,9},{9,8},{10,11... | collective-permute-start | bytes 811016 | tf_op jit(solution)/shard_map/ppermute | solution.py:725
  162.6 3.4 %collective-permute-start.37 = (bf16[2,256,1024]{2,1,0:T(8,128)(2,1)}, bf16[2,256,1024]{2,1,0:T(8,128)(2,1)S(1)}, u32[]{:S(2)}, u32[]{:S(2)}) collective-permute-start(bf16[2,256,1024]{2,1,0:T(8,128)(2,1)} %get-tuple-element.160), channel_id=1, source_target_pairs={{0,8},{8,0},{16,24},{24,16},{1,9},{9,1},{17,25},{25,17},{2,10},{10... | collective-permute-start | bytes 3145736 | tf_op jit(solution)/shard_map/ppermute | solution.py:957
  163.5 15.4 %collective-permute-start.39 = (bf16[2112,128]{1,0:T(8,128)(2,1)}, bf16[2112,128]{1,0:T(8,128)(2,1)}, u32[]{:S(2)}, u32[]{:S(2)}) collective-permute-start(bf16[2112,128]{1,0:T(8,128)(2,1)} %get-tuple-element.167), channel_id=1, source_target_pairs={{0,1},{1,0},{2,3},{3,2},{4,5},{5,4},{6,7},{7,6},{8,9},{9,8},{10,11... | collective-permute-start | bytes 1622024 | tf_op jit(solution)/shard_map/ppermute | solution.py:725
  168.4 13.8 %collective-permute-start.38 = (bf16[256,1024]{1,0:T(8,128)(2,1)}, bf16[256,1024]{1,0:T(8,128)(2,1)}, u32[]{:S(2)}, u32[]{:S(2)}) collective-permute-start(bf16[256,1024]{1,0:T(8,128)(2,1)} %fusion.3), channel_id=1, source_target_pairs={{0,16},{8,24},{16,0},{24,8},{1,17},{9,25},{17,1},{25,9},{2,18},{10... | collective-permute-start | bytes 1572872 | tf_op jit(solution)/shard_map/ppermute | solution.py:959
  178.9 13.5 %collective-permute-start.42 = (bf16[2112,128]{1,0:T(8,128)(2,1)}, bf16[2112,128]{1,0:T(8,128)(2,1)}, u32[]{:S(2)}, u32[]{:S(2)}) collective-permute-start(bf16[2112,128]{1,0:T(8,128)(2,1)} %get-tuple-element.174), channel_id=1, source_target_pairs={{0,1},{1,0},{2,3},{3,2},{4,5},{5,4},{6,7},{7,6},{8,9},{9,8},{10,11... | collective-permute-start | bytes 1622024 | tf_op jit(solution)/shard_map/ppermute | solution.py:725
  181.6 49.8 %collective-permute-start.46 = (bf16[2112,128]{1,0:T(8,128)(2,1)}, bf16[2112,128]{1,0:T(8,128)(2,1)S(1)}, u32[]{:S(2)}, u32[]{:S(2)}) collective-permute-start(bf16[2112,128]{1,0:T(8,128)(2,1)} %add_convert_fusion.2), channel_id=1, source_target_pairs={{0,4},{1,5},{2,6},{3,7},{4,0},{5,1},{6,2},{7,3},{8,12},{9,13},{10,... | collective-permute-start | bytes 1622024 | tf_op jit(solution)/shard_map/ppermute | solution.py:746
  186.5 19.2 %collective-permute-start.41 = (bf16[256,1152]{1,0:T(8,128)(2,1)}, bf16[256,1152]{1,0:T(8,128)(2,1)S(1)}, u32[]{:S(2)}, u32[]{:S(2)}) collective-permute-start(bf16[256,1152]{1,0:T(8,128)(2,1)} %get-tuple-element.170.refs_1_), channel_id=1, source_target_pairs={{0,16},{8,24},{16,0},{24,8},{1,17},{9,25},{17,1},{25,9},{2,18},{10... | collective-permute-start | bytes 1769480 | tf_op jit(solution)/shard_map/ppermute | solution.py:706
  187.1 22.1 %collective-permute-start.40 = (bf16[256,1152]{1,0:T(8,128)(2,1)}, bf16[256,1152]{1,0:T(8,128)(2,1)S(1)}, u32[]{:S(2)}, u32[]{:S(2)}) collective-permute-start(bf16[256,1152]{1,0:T(8,128)(2,1)} %get-tuple-element.170.refs_1_), channel_id=1, source_target_pairs={{0,8},{8,0},{16,24},{24,16},{1,9},{9,1},{17,25},{25,17},{2,10},{10... | collective-permute-start | bytes 1769480 | tf_op jit(solution)/shard_map/ppermute | solution.py:707
  192.5 12.6 %collective-permute-start.43 = (bf16[2112,128]{1,0:T(8,128)(2,1)}, bf16[2112,128]{1,0:T(8,128)(2,1)S(1)}, u32[]{:S(2)}, u32[]{:S(2)}) collective-permute-start(bf16[2112,128]{1,0:T(8,128)(2,1)} %get-tuple-element.178), channel_id=1, source_target_pairs={{0,1},{1,0},{2,3},{3,2},{4,5},{5,4},{6,7},{7,6},{8,9},{9,8},{10,11... | collective-permute-start | bytes 1622024 | tf_op jit(solution)/shard_map/ppermute | solution.py:725
  195.2 36.2 %collective-permute-start.47 = (bf16[2112,128]{1,0:T(8,128)(2,1)}, bf16[2112,128]{1,0:T(8,128)(2,1)}, u32[]{:S(2)}, u32[]{:S(2)}) collective-permute-start(bf16[2112,128]{1,0:T(8,128)(2,1)} %add_convert_fusion.1), channel_id=1, source_target_pairs={{0,2},{1,3},{2,4},{3,5},{4,6},{5,7},{6,0},{7,1},{8,10},{9,11},{10,... | collective-permute-start | bytes 1622024 | tf_op jit(solution)/shard_map/ppermute | solution.py:746
  205.0 26.4 %collective-permute-start.49 = (bf16[2112,128]{1,0:T(8,128)(2,1)}, bf16[2112,128]{1,0:T(8,128)(2,1)}, u32[]{:S(2)}, u32[]{:S(2)}) collective-permute-start(bf16[2112,128]{1,0:T(8,128)(2,1)} %get-tuple-element.190), channel_id=1, source_target_pairs={{0,1},{1,0},{2,3},{3,2},{4,5},{5,4},{6,7},{7,6},{8,9},{9,8},{10,11... | collective-permute-start | bytes 1622024 | tf_op jit(solution)/shard_map/ppermute | solution.py:725
  205.6 6.8 %collective-permute-start.44 = (bf16[256,1152]{1,0:T(8,128)(2,1)S(1)}, bf16[256,1152]{1,0:T(8,128)(2,1)S(1)}, u32[]{:S(2)}, u32[]{:S(2)}) collective-permute-start(bf16[256,1152]{1,0:T(8,128)(2,1)S(1)} %collective-permute-done.41.refs_3_), channel_id=1, source_target_pairs={{0,8},{8,0},{16,24},{24,16},{1,9},{9,1},{17,25},{25,17},{2,10},{10... | collective-permute-start | bytes 1769480 | tf_op jit(solution)/shard_map/ppermute | solution.py:986
  209.2 22.6 %collective-permute-start.48 = (bf16[2112,128]{1,0:T(8,128)(2,1)}, bf16[2112,128]{1,0:T(8,128)(2,1)}, u32[]{:S(2)}, u32[]{:S(2)}) collective-permute-start(bf16[2112,128]{1,0:T(8,128)(2,1)} %add_convert_fusion), channel_id=1, source_target_pairs={{0,6},{1,7},{2,0},{3,1},{4,2},{5,3},{6,4},{7,5},{8,14},{9,15},{10,... | collective-permute-start | bytes 1622024 | tf_op jit(solution)/shard_map/ppermute | solution.py:746
  231.8 3.9 %collective-permute-start.50 = (bf16[2,256,1024]{2,1,0:T(8,128)(2,1)}, bf16[2,256,1024]{2,1,0:T(8,128)(2,1)S(1)}, u32[]{:S(2)}, u32[]{:S(2)}) collective-permute-start(bf16[2,256,1024]{2,1,0:T(8,128)(2,1)} %get-tuple-element.191), channel_id=1, source_target_pairs={{0,8},{8,0},{16,24},{24,16},{1,9},{9,1},{17,25},{25,17},{2,10},{10... | collective-permute-start | bytes 3145736 | tf_op jit(solution)/shard_map/ppermute | solution.py:1010
  232.3 12.3 %collective-permute-start.45 = (bf16[128,1792]{1,0:T(8,128)(2,1)}, bf16[128,1792]{1,0:T(8,128)(2,1)S(1)}, u32[]{:S(2)}, u32[]{:S(2)}) collective-permute-start(bf16[128,1792]{1,0:T(8,128)(2,1)} %get-tuple-element.186), channel_id=1, source_target_pairs={{0,1},{1,0},{2,3},{3,2},{4,5},{5,4},{6,7},{7,6},{8,9},{9,8},{10,11... | collective-permute-start | bytes 1376264 | tf_op jit(solution)/shard_map/ppermute | solution.py:725
  237.4 13.3 %collective-permute-start.51 = (bf16[256,1024]{1,0:T(8,128)(2,1)S(1)}, bf16[256,1024]{1,0:T(8,128)(2,1)S(1)}, u32[]{:S(2)}, u32[]{:S(2)}) collective-permute-start(bf16[256,1024]{1,0:T(8,128)(2,1)S(1)} %fusion.2), channel_id=1, source_target_pairs={{0,16},{8,24},{16,0},{24,8},{1,17},{9,25},{17,1},{25,9},{2,18},{10... | collective-permute-start | bytes 1572872 | tf_op jit(solution)/shard_map/ppermute | solution.py:714
  245.5 11.5 %collective-permute-start.58 = (bf16[128,1792]{1,0:T(8,128)(2,1)}, bf16[128,1792]{1,0:T(8,128)(2,1)}, u32[]{:S(2)}, u32[]{:S(2)}) collective-permute-start(bf16[128,1792]{1,0:T(8,128)(2,1)} %get-tuple-element.211), channel_id=1, source_target_pairs={{0,1},{1,0},{2,3},{3,2},{4,5},{5,4},{6,7},{7,6},{8,9},{9,8},{10,11... | collective-permute-start | bytes 1376264 | tf_op jit(solution)/shard_map/ppermute | solution.py:725
  246.3 28.0 %collective-permute-start.57 = (bf16[128,1792]{1,0:T(8,128)(2,1)}, bf16[128,1792]{1,0:T(8,128)(2,1)}, u32[]{:S(2)}, u32[]{:S(2)}) collective-permute-start(bf16[128,1792]{1,0:T(8,128)(2,1)} %add_convert_fusion.5), channel_id=1, source_target_pairs={{0,4},{1,5},{2,6},{3,7},{4,0},{5,1},{6,2},{7,3},{8,12},{9,13},{10,... | collective-permute-start | bytes 1376264 | tf_op jit(solution)/shard_map/ppermute | solution.py:746
  259.0 17.1 %collective-permute-start.59 = (bf16[128,1792]{1,0:T(8,128)(2,1)}, bf16[128,1792]{1,0:T(8,128)(2,1)}, u32[]{:S(2)}, u32[]{:S(2)}) collective-permute-start(bf16[128,1792]{1,0:T(8,128)(2,1)} %get-tuple-element.212), channel_id=1, source_target_pairs={{0,1},{1,0},{2,3},{3,2},{4,5},{5,4},{6,7},{7,6},{8,9},{9,8},{10,11... | collective-permute-start | bytes 1376264 | tf_op jit(solution)/shard_map/ppermute | solution.py:725
  265.5 14.1 %collective-permute-start.52 = (bf16[2,256,1024]{2,1,0:T(8,128)(2,1)}, bf16[2,256,1024]{2,1,0:T(8,128)(2,1)S(1)}, u32[]{:S(2)}, u32[]{:S(2)}) collective-permute-start(bf16[2,256,1024]{2,1,0:T(8,128)(2,1)} %get-tuple-element.197), channel_id=1, source_target_pairs={{0,8},{8,0},{16,24},{24,16},{1,9},{9,1},{17,25},{25,17},{2,10},{10... | collective-permute-start | bytes 3145736 | tf_op jit(solution)/shard_map/ppermute | solution.py:1026
  273.9 19.5 %collective-permute-start.64 = (bf16[128,1792]{1,0:T(8,128)(2,1)}, bf16[128,1792]{1,0:T(8,128)(2,1)S(1)}, u32[]{:S(2)}, u32[]{:S(2)}) collective-permute-start(bf16[128,1792]{1,0:T(8,128)(2,1)} %add_convert_fusion.4), channel_id=1, source_target_pairs={{0,2},{1,3},{2,4},{3,5},{4,6},{5,7},{6,0},{7,1},{8,10},{9,11},{10,... | collective-permute-start | bytes 1376264 | tf_op jit(solution)/shard_map/ppermute | solution.py:746
  277.4 21.1 %collective-permute-start.65 = (bf16[128,1792]{1,0:T(8,128)(2,1)S(1)}, bf16[128,1792]{1,0:T(8,128)(2,1)S(1)}, u32[]{:S(2)}, u32[]{:S(2)}) collective-permute-start(bf16[128,1792]{1,0:T(8,128)(2,1)S(1)} %add_convert_fusion.3), channel_id=1, source_target_pairs={{0,6},{1,7},{2,0},{3,1},{4,2},{5,3},{6,4},{7,5},{8,14},{9,15},{10,... | collective-permute-start | bytes 1376264 | tf_op jit(solution)/shard_map/ppermute | solution.py:746
  278.5 9.5 %collective-permute-start.60 = (bf16[128,1792]{1,0:T(8,128)(2,1)}, bf16[128,1792]{1,0:T(8,128)(2,1)S(1)}, u32[]{:S(2)}, u32[]{:S(2)}) collective-permute-start(bf16[128,1792]{1,0:T(8,128)(2,1)} %get-tuple-element.213), channel_id=1, source_target_pairs={{0,1},{1,0},{2,3},{3,2},{4,5},{5,4},{6,7},{7,6},{8,9},{9,8},{10,11... | collective-permute-start | bytes 1376264 | tf_op jit(solution)/shard_map/ppermute | solution.py:725
  279.7 10.5 %collective-permute-start.53 = (bf16[256,1024]{1,0:T(8,128)(2,1)S(1)}, bf16[256,1024]{1,0:T(8,128)(2,1)S(1)}, u32[]{:S(2)}, u32[]{:S(2)}) collective-permute-start(bf16[256,1024]{1,0:T(8,128)(2,1)S(1)} %fusion.1), channel_id=1, source_target_pairs={{0,16},{8,24},{16,0},{24,8},{1,17},{9,25},{17,1},{25,9},{2,18},{10... | collective-permute-start | bytes 1572872 | tf_op jit(solution)/shard_map/ppermute | solution.py:714
  290.2 15.3 %collective-permute-start.61 = (f32[32,160]{1,0:T(8,128)S(1)}, f32[32,160]{1,0:T(8,128)S(1)}, u32[]{:S(2)}, u32[]{:S(2)}) collective-permute-start(f32[32,160]{1,0:T(8,128)S(1)} %add.275), channel_id=1, source_target_pairs={{0,2},{1,3},{2,4},{3,5},{4,6},{5,7},{6,0},{7,1},{8,10},{9,11},{10,... | collective-permute-start | bytes 61448 | tf_op jit(solution)/shard_map/ppermute | solution.py:760
  290.2 18.1 %collective-permute-start.62 = (f32[32,160]{1,0:T(8,128)S(1)}, f32[32,160]{1,0:T(8,128)S(1)}, u32[]{:S(2)}, u32[]{:S(2)}) collective-permute-start(f32[32,160]{1,0:T(8,128)S(1)} %add.275), channel_id=1, source_target_pairs={{0,4},{1,5},{2,6},{3,7},{4,0},{5,1},{6,2},{7,3},{8,12},{9,13},{10,... | collective-permute-start | bytes 61448 | tf_op jit(solution)/shard_map/ppermute | solution.py:760
  290.8 17.5 %collective-permute-start.63 = (f32[32,160]{1,0:T(8,128)S(1)}, f32[32,160]{1,0:T(8,128)S(1)}, u32[]{:S(2)}, u32[]{:S(2)}) collective-permute-start(f32[32,160]{1,0:T(8,128)S(1)} %add.275), channel_id=1, source_target_pairs={{0,6},{1,7},{2,0},{3,1},{4,2},{5,3},{6,4},{7,5},{8,14},{9,15},{10,... | collective-permute-start | bytes 61448 | tf_op jit(solution)/shard_map/ppermute | solution.py:760
  299.9 9.7 %collective-permute-start.66 = (bf16[128,512]{1,0:T(8,128)(2,1)S(1)}, bf16[128,512]{1,0:T(8,128)(2,1)S(1)}, u32[]{:S(2)}, u32[]{:S(2)}) collective-permute-start(bf16[128,512]{1,0:T(8,128)(2,1)S(1)} %pad_maximum_fusion.4), channel_id=1, source_target_pairs={{0,16},{8,24},{16,0},{24,8},{1,17},{9,25},{17,1},{25,9},{2,18},{10... | collective-permute-start | bytes 393224 | tf_op jit(solution)/shard_map/ppermute | solution.py:1066
  300.2 9.3 %collective-permute-start.68 = (bf16[128,256]{1,0:T(8,128)(2,1)S(1)}, bf16[128,256]{1,0:T(8,128)(2,1)S(1)}, u32[]{:S(2)}, u32[]{:S(2)}) collective-permute-start(bf16[128,256]{1,0:T(8,128)(2,1)S(1)} %get-tuple-element.228), channel_id=1, source_target_pairs={{0,0},{8,16},{16,8},{24,24},{1,1},{9,17},{17,9},{25,25},{2,2},{10,... | collective-permute-start | bytes 196616 | tf_op jit(solution)/shard_map/ppermute | solution.py:1070
  305.5 8.1 %collective-permute-start.67 = (bf16[128,512]{1,0:T(8,128)(2,1)S(1)}, bf16[128,512]{1,0:T(8,128)(2,1)S(1)}, u32[]{:S(2)}, u32[]{:S(2)}) collective-permute-start(bf16[128,512]{1,0:T(8,128)(2,1)S(1)} %slice.105), channel_id=1, source_target_pairs={{0,0},{16,1},{8,2},{24,3},{4,4},{20,5},{12,6},{28,7},{2,8},{18,9},... | collective-permute-start | bytes 393224 | tf_op jit(solution)/shard_map/ppermute | solution.py:1041
  (61 other events, 566.0 us)
where the time goes:
time: 322 us; the launch traced here: 316 us
  waiting for transfers between devices  132 us (41%)
  Pallas kernels  77.9 us (24%)
  starting transfers between devices  70.6 us (22%)
  other arithmetic  21.5 us (7%)
  local copies, waits for them, and re-layouts  11.5 us (4%)
    pallas_call x14, Pallas kernels, call(): pl.pallas_call(body, out_shape=outs, in_specs=[pl.BlockSpec(memory_space=...  77.9 us
    ppermute x18, waiting for transfers between devices, xsend(): return lax.ppermute(pack, 'batch', XSWAP)  61.4 us
    convert_element_type x10, other arithmetic, plus(): return (a.astype(F32) + b.astype(F32)).astype(BF)  14.9 us
    ppermute x18, starting transfers between devices, xsend(): return lax.ppermute(pack, 'batch', XSWAP)  13.7 us
    ppermute x1, waiting for transfers between devices, per_device(): mz2 = lax.ppermute(after(pack_m, mz3, mx1), 'batch', zshift(2))  13.6 us
    ppermute x1, waiting for transfers between devices, per_device(): mz1 = lax.ppermute(pack_m, 'batch', zshift(1))  12.6 us
    ppermute x5, starting transfers between devices, seq_gather(): cv = lax.ppermute(v, 'seq', CORE)  8.03 us
    unnamed x112, local copies, waits for them, and re-layouts  7 us
  transfers between devices with their start and end apart: 69, of which 32 were waited for; matrix products, arithmetic and copies ran while one was open for 8% of the time, Pallas kernels for 19%

commit v1 on v0

--- a/solution.py
+++ b/solution.py
@@ -507,7 +507,11 @@
     resid = resid_ref[...]
     sc2 = lax.rsqrt(jnp.mean(resid * resid, axis=1, keepdims=True) + EPS)
     second = resid * sc2
-    gg2_ref[...] = jnp.sum(gfi * second, axis=0, keepdims=True)
+    @pl.when(pl.program_id(0) == 0)
+    def _():
+        gg2_ref[...] = jnp.zeros_like(gg2_ref)
+
+    gg2_ref[...] += jnp.sum(gfi * second, axis=0, keepdims=True)
     g = gfi * g2_ref[...]
     gres = c_ref[...].astype(F32) + sc2 * (
         g - second * jnp.mean(g * second, axis=1, keepdims=True)
@@ -742,8 +746,9 @@
         kept = after(self.kept[kk], *deps) if deps else self.kept[kk]
         self.part[kk] = plus(kept, self.got[kk])
 
-    def along_z(self, kk):
-        self.z[kk] = lax.ppermute(self.part[kk], "batch", zshift(kk))
+    def along_z(self, kk, *deps):
+        part = after(self.part[kk], *deps) if deps else self.part[kk]
+        self.z[kk] = lax.ppermute(part, "batch", zshift(kk))
 
     def total(self, *deps):
         out = after(self.kept[0], *deps) + self.got[0].astype(F32)
@@ -973,11 +978,24 @@
         fsc.along_x(1, fsc.got[2])
         fsc.along_x(3, fsc.got[1])
         first_sum.append(fsc.part[2])
-    gres, pay, gg2 = call(
+    rows4 = blk // 4
+    row = lambda w: pl.BlockSpec((rows4, w), lambda i: (i, 0))
+    one = pl.BlockSpec((1, width), lambda i: (0, 0))
+    gres, pay, gg2 = pl.pallas_call(
         functools.partial(gresid_body, chans=2.0 * width),
-        [sds((blk, width), F32), sds((blk, tail), BF), sds((1, width), F32)],
-        [k02, got2, near2, after(cp, *first_sum), resid, xp, sc, gain2], room=None, name="gresid",
-    )
+        grid=(4,),
+        out_shape=[sds((blk, width), F32), sds((blk, tail), BF), sds((1, width), F32)],
+        in_specs=[
+            row(width), pl.BlockSpec((1, rows4, width), lambda i: (0, i, 0)), row(width),
+            row(width), row(width), row(width), row(128), one,
+        ],
+        out_specs=[row(width), row(tail), one],
+        compiler_params=pltpu.CompilerParams(vmem_limit_bytes=63 * MB),
+        cost_estimate=pl.CostEstimate(
+            flops=3 * 10**9, bytes_accessed=6 * 10**6, transcendentals=0
+        ),
+        name="gresid",
+    )(k02, got2, near2, after(cp, *first_sum), resid, xp, sc, gain2)
     pays = seq_gather(pay)
     if wide:
         fsc.add(1, pay)
@@ -985,7 +1003,6 @@
         pays[2] = after(pays[2], fsc.part[1])
         pays[3] = lax.ppermute(pays[2], "seq", CORE)
         fsc.add(3, pays[2])
-        fsc.along_z(3)
         fsc.along_x(0, fsc.got[3])
         pays[1] = after(pays[1], fsc.part[3])
     part_m = [sds((row8, 7 * ch), F32)] + [sds((row8, 7 * ch), BF)] * 7
@@ -1006,7 +1023,8 @@
     msc = Scatter(*msc)
     if wide:
         msc.along_x(2)
-        sout4 = after(sout4, *fsc.z.values(), fsc.got[0])
+        fsc.along_z(3, ggm)
+        sout4 = after(sout4, fsc.z[2], fsc.z[1], fsc.got[0])
     got4, near4 = seq_scatter(k14, lax.ppermute(sout4, "seq", CORE))
     if wide:
         msc.add(2)
@@ -1019,7 +1037,7 @@
     )
     k03, k13, sout3 = call(
         functools.partial(down_body, pieces=fpieces), scat,
-        [idx, after(hid, gg1), *ffns], [SMEM, VMEM] + [HBM] * fpieces,
+        [idx, after(hid, gg1, *([fsc.z[3]] if wide else [])), *ffns], [SMEM, VMEM] + [HBM] * fpieces,
         scratch=[pltpu.VMEM((hu, width), BF), dma((8,))],
         room=None, flops=2 * tok * width * hu, name="down",
     )

time: 322 us -> 320 us (level)
    ppermute x18, waiting for transfers between devices: 61.4 us -> 56 us  [xsend(): return lax.ppermute(pack, 'batch', XSWAP)]
    pallas_call x0 -> x1, Pallas kernels: none -> 4.81 us  [per_device(): pl.pallas_call(functools.partial(gresid_body, chans=2.0 * width), grid=(4...]
    pallas_call x14 -> x13, Pallas kernels: 77.9 us -> 73.7 us  [call(): pl.pallas_call(body, out_shape=outs, in_specs=[pl.BlockSpec(memory_space=...]
    unnamed x112 -> x114, local copies, waits for them, and re-layouts: 7 us -> 7.03 us
  transfers between devices with their start and end apart: 69 -> 69, of which waited for: 32 -> 31; matrix products, arithmetic and copies ran while one was open for 8% -> 8% of each run, Pallas kernels for 19% -> 19%
where the time goes in v1:
time: 320 us; the launch traced here: 314 us
  waiting for transfers between devices  129 us (40%)
  Pallas kernels  78.5 us (25%)
  starting transfers between devices  70.9 us (22%)
  other arithmetic  21.4 us (7%)
  local copies, waits for them, and re-layouts  11.6 us (4%)
    pallas_call x13, Pallas kernels, call(): pl.pallas_call(body, out_shape=outs, in_specs=[pl.BlockSpec(memory_space=...  73.7 us
    ppermute x18, waiting for transfers between devices, xsend(): return lax.ppermute(pack, 'batch', XSWAP)  56 us
    convert_element_type x10, other arithmetic, plus(): return (a.astype(F32) + b.astype(F32)).astype(BF)  14.8 us
    ppermute x1, waiting for transfers between devices, per_device(): mz2 = lax.ppermute(after(pack_m, mz3, mx1), 'batch', zshift(2))  13.5 us
    ppermute x18, starting transfers between devices, xsend(): return lax.ppermute(pack, 'batch', XSWAP)  13 us
    ppermute x1, waiting for transfers between devices, per_device(): mz1 = lax.ppermute(pack_m, 'batch', zshift(1))  12.6 us
    ppermute x3, waiting for transfers between devices, seq_scatter(): return (got, lax.ppermute(far, 'seq', YSWAP))  8.95 us
    ppermute x5, starting transfers between devices, seq_gather(): cv = lax.ppermute(v, 'seq', CORE)  8.02 us
  transfers between devices with their start and end apart: 69, of which 31 were waited for; matrix products, arithmetic and copies ran while one was open for 8% of the time, Pallas kernels for 19%

profile of v1, /device:TPU:3, one launch (start us, length us, event | category | flops | bytes accessed | tf_op | source)
XLA Modules:
  0.0 313.5 jit_solution(508245151587095679)
XLA Ops:
  2.9 4.0 %collective-permute-start.4 = (bf16[256,256]{1,0:T(8,128)(2,1)}, bf16[256,256]{1,0:T(8,128)(2,1)}, u32[]{:S(2)}, u32[]{:S(2)}) collective-permute-start(bf16[256,256]{1,0:T(8,128)(2,1)} %param.25), channel_id=1, source_target_pairs={{0,0},{1,16},{2,8},{3,24},{4,4},{5,20},{6,12},{7,28},{8,2},{9,18},... | collective-permute-start | bytes 393224 | tf_op jit(solution)/shard_map/ppermute | solution.py:809
  6.8 1.9 collective-permute-start.3
  8.8 1.4 line.1.l_ref
  10.2 1.7 collective-permute-start.5
  13.9 2.0 pack.1
  16.2 1.5 collective-permute-start.8
  17.7 12.6 %collective-permute-done.6.refs_6_.refs_10_ = bf16[128,1792]{1,0:T(8,128)(2,1)S(1)} collective-permute-done((bf16[128,1792]{1,0:T(8,128)(2,1)}, bf16[128,1792]{1,0:T(8,128)(2,1)S(1)}, u32[]{:S(2)}, u32[]{:S(2)}) %collective-permute-start.6) | collective-permute-done | bytes 458784 | tf_op jit(solution)/shard_map/ppermute | solution.py:821
  30.5 1.7 collective-permute-start.7
  33.3 1.4 norm1.1
  35.5 6.6 %collective-permute-done.9.refs_10_.refs_14_ = bf16[128,1792]{1,0:T(8,128)(2,1)S(1)} collective-permute-done((bf16[128,1792]{1,0:T(8,128)(2,1)S(1)}, bf16[128,1792]{1,0:T(8,128)(2,1)S(1)}, u32[]{:S(2)}, u32[]{:S(2)}) %collective-permute-start.9) | collective-permute-done | bytes 458784 | tf_op jit(solution)/shard_map/ppermute | solution.py:729
  42.6 1.6 collective-permute-start.12
  44.4 4.2 %collective-permute-done.2.refs_3_.refs_7_ = bf16[256,1024]{1,0:T(8,128)(2,1)} collective-permute-done((bf16[256,1024]{1,0:T(8,128)(2,1)}, bf16[256,1024]{1,0:T(8,128)(2,1)}, u32[]{:S(2)}, u32[]{:S(2)}) %collective-permute-start.2) | collective-permute-done | bytes 524320 | tf_op jit(solution)/shard_map/ppermute | solution.py:710
  48.6 1.4 collective-permute-start.15
  50.1 1.8 collective-permute-start.16
  51.9 13.5 %collective-permute-done.12.refs_7_.refs_11_ = bf16[128,1792]{1,0:T(8,128)(2,1)} collective-permute-done((bf16[128,1792]{1,0:T(8,128)(2,1)S(1)}, bf16[128,1792]{1,0:T(8,128)(2,1)}, u32[]{:S(2)}, u32[]{:S(2)}) %collective-permute-start.12) | collective-permute-done | bytes 458784 | tf_op jit(solution)/shard_map/ppermute | solution.py:825
  65.5 2.0 collective-permute-start.1
  68.7 2.2 collective-permute-done.18.v2
  70.8 1.6 collective-permute-start.17
  75.2 2.2 smalls.1
  77.4 2.3 collective-permute-done.13.refs_11_.refs_15_
  80.8 2.4 collective-permute-done.20.refs_10_.refs_3_
  84.1 1.4 collective-permute-start.21
  85.5 11.0 %mixer_fwd.1 = (bf16[4,256,1280]{2,1,0:T(8,128)(2,1)}, f32[4,256,256]{2,1,0:T(8,128)}, f32[4,256,512]{2,1,0:T(8,128)}, f32[4,256,512]{2,1,0:T(8,128)}, bf16[256,...) custom-call(s32[28]{0:T(128)} %stack.115.idx_ref.refs_0_, ...), custom_call_target="tpu_custom_call" | custom-call | flops 40580964352 | bytes 16004208 | tf_op jit(solution)/shard_map/mixer_fwd/pallas_call | solution.py:79
  96.8 2.0 collective-permute-start.25
  98.9 2.7 collective-permute-done.25.got_ref
  105.6 10.9 %collective-permute-done.28.refs_14_.refs_7_ = bf16[2112,128]{1,0:T(8,128)(2,1)S(1)} collective-permute-done((bf16[2112,128]{1,0:T(8,128)(2,1)}, bf16[2112,128]{1,0:T(8,128)(2,1)S(1)}, u32[]{:S(2)}, u32[]{:S(2)}) %collective-permute-start.28) | collective-permute-done | bytes 540704 | tf_op jit(solution)/shard_map/ppermute | solution.py:729
  117.1 2.2 collective-permute-done.27.refs_11_.refs_4_
  121.5 1.5 collective-permute-start.31
  123.0 6.1 %collective-permute-done.32.refs_16_.refs_9_ = bf16[2112,128]{1,0:T(8,128)(2,1)S(1)} collective-permute-done((bf16[2112,128]{1,0:T(8,128)(2,1)}, bf16[2112,128]{1,0:T(8,128)(2,1)S(1)}, u32[]{:S(2)}, u32[]{:S(2)}) %collective-permute-start.32) | collective-permute-done | bytes 540704 | tf_op jit(solution)/shard_map/ppermute | solution.py:729
  129.7 2.6 collective-permute-start.30
  132.3 5.3 %collective-permute-done.34.refs_17_.refs_10_ = bf16[1056,128]{1,0:T(8,128)(2,1)S(1)} collective-permute-done((bf16[1056,128]{1,0:T(8,128)(2,1)S(1)}, bf16[1056,128]{1,0:T(8,128)(2,1)S(1)}, u32[]{:S(2)}, u32[]{:S(2)}) %collective-permute-start.34) | collective-permute-done | bytes 270368 | tf_op jit(solution)/shard_map/ppermute | solution.py:835
  138.7 7.6 %collective-permute-done.36.refs_18_.refs_11_ = bf16[1056,128]{1,0:T(8,128)(2,1)S(1)} collective-permute-done((bf16[1056,128]{1,0:T(8,128)(2,1)S(1)}, bf16[1056,128]{1,0:T(8,128)(2,1)S(1)}, u32[]{:S(2)}, u32[]{:S(2)}) %collective-permute-start.36) | collective-permute-done | bytes 270368 | tf_op jit(solution)/shard_map/ppermute | solution.py:729
  147.1 15.4 %ffn.1 = (bf16[1024,704]{1,0:T(8,128)(2,1)}, bf16[1024,1408]{1,0:T(8,128)(2,1)}, bf16[256,1024]{1,0:T(8,128)(2,1)}, bf16[256,1024]{1,0:T(8,128)(2,1)}, bf16[2,25...) custom-call(s32[28]{0:T(128)} %stack.115.idx_ref.refs_0_, bf16[256,1024]{1,0:T(8,128)(2,1)} %copy-done.3, ...), custom_call_target="tpu_custom_call" | custom-call | flops 76819750912 | bytes 16023664 | tf_op jit(solution)/shard_map/ffn/pallas_call | solution.py:79
  164.0 2.0 collective-permute-done.37.got_ref
  166.0 2.4 fusion.3
  169.4 9.5 %ffn_grad.1 = (f32[2112,128]{1,0:T(8,128)}, bf16[2112,128]{1,0:T(8,128)(2,1)}, bf16[2112,128]{1,0:T(8,128)(2,1)}, bf16[2112,128]{1,0:T(8,128)(2,1)}, bf16[2112,1...) custom-call(s32[28]{0:T(128)} %stack.115.idx_ref.refs_0_, bf16[1024,704]{1,0:T(8,128)(2,1)} %get-tuple-element.198.h_ref.refs_1_, ...), custom_call_target="tpu_custom_call" | custom-call | flops 47291850752 | bytes 12304496 | tf_op jit(solution)/shard_map/ffn_grad/pallas_call | solution.py:79
  179.6 2.0 add_convert_fusion.2
  182.2 4.8 %gresid.1 = (f32[256,1024]{1,0:T(8,128)}, bf16[256,1152]{1,0:T(8,128)(2,1)}, f32[1,1024]{1,0:T(1,128)}) custom-call(bf16[256,1024]{1,0:T(8,128)(2,1)} %get-tuple-element.160.own_ref, bf16[2,256,1024]{2,1,0:T(8,128)(2,1)} %copy-done.24, bf16[256,1024]{1,0:T(8,128)(2,1)} %collective-permute-done.38.ry_ref, ...), custom_call_target="tpu_custom_call" | custom-call | flops 3000000000 | bytes 6000000 | tf_op jit(solution)/shard_map/gresid/pallas_call | solution.py:984
  187.8 1.5 collective-permute-start.40
  189.2 3.2 %collective-permute-done.42 = bf16[2112,128]{1,0:T(8,128)(2,1)} collective-permute-done((bf16[2112,128]{1,0:T(8,128)(2,1)}, bf16[2112,128]{1,0:T(8,128)(2,1)}, u32[]{:S(2)}, u32[]{:S(2)}) %collective-permute-start.42) | collective-permute-done | bytes 540704 | tf_op jit(solution)/shard_map/ppermute | solution.py:729
  193.1 2.2 add_convert_fusion.1
  195.3 9.8 %collective-permute-done.43 = bf16[2112,128]{1,0:T(8,128)(2,1)S(1)} collective-permute-done((bf16[2112,128]{1,0:T(8,128)(2,1)}, bf16[2112,128]{1,0:T(8,128)(2,1)S(1)}, u32[]{:S(2)}, u32[]{:S(2)}) %collective-permute-start.43) | collective-permute-done | bytes 540704 | tf_op jit(solution)/shard_map/ppermute | solution.py:729
  205.6 2.6 collective-permute-start.44
  210.7 18.2 %bwd.1 = (f32[1,512]{1,0:T(1,128)}, f32[1,256]{1,0:T(1,128)}, f32[128,1792]{1,0:T(8,128)}, bf16[128,1792]{1,0:T(8,128)(2,1)}, bf16[128,1792]{1,0:T(8,128)(2,1)},...) custom-call(s32[28]{0:T(128)} %stack.115.idx_ref.refs_0_, ...), custom_call_target="tpu_custom_call" | custom-call | flops 83530637312 | bytes 22229104 | tf_op jit(solution)/shard_map/bwd/pallas_call | solution.py:79
  232.8 3.2 %collective-permute-start.51 = (bf16[2112,128]{1,0:T(8,128)(2,1)}, bf16[2112,128]{1,0:T(8,128)(2,1)}, u32[]{:S(2)}, u32[]{:S(2)}) collective-permute-start(bf16[2112,128]{1,0:T(8,128)(2,1)} %add_convert_fusion), channel_id=1, source_target_pairs={{0,6},{1,7},{2,0},{3,1},{4,2},{5,3},{6,4},{7,5},{8,14},{9,15},{10,... | collective-permute-start | bytes 1622024 | tf_op jit(solution)/shard_map/ppermute | solution.py:751
  236.1 1.6 fusion.2
  238.1 3.5 %collective-permute-done.45 = bf16[128,1792]{1,0:T(8,128)(2,1)S(1)} collective-permute-done((bf16[128,1792]{1,0:T(8,128)(2,1)}, bf16[128,1792]{1,0:T(8,128)(2,1)S(1)}, u32[]{:S(2)}, u32[]{:S(2)}) %collective-permute-start.45) | collective-permute-done | bytes 458784 | tf_op jit(solution)/shard_map/ppermute | solution.py:729
  243.6 7.0 %collective-permute-done.50.ry_ref = bf16[256,1024]{1,0:T(8,128)(2,1)S(1)} collective-permute-done((bf16[256,1024]{1,0:T(8,128)(2,1)S(1)}, bf16[256,1024]{1,0:T(8,128)(2,1)S(1)}, u32[]{:S(2)}, u32[]{:S(2)}) %collective-permute-start.50) | collective-permute-done | bytes 524320 | tf_op jit(solution)/shard_map/ppermute | solution.py:718
  251.4 3.7 %gin.1 = (bf16[256,1024]{1,0:T(8,128)(2,1)}, f32[1,1024]{1,0:T(1,128)}) custom-call(bf16[256,1024]{1,0:T(8,128)(2,1)} %get-tuple-element.188.own_ref, bf16[2,256,1024]{2,1,0:T(8,128)(2,1)} %copy-done.23, bf16[256,1024]{1,0:T(8,128)(2,1)} %copy-done.39, bf16[256,1024]{1,0:T(8,128)(2,1)} %copy-done.6, f32[256,1024]{1,0:T(8,128)} %get-tuple-element.194.gres_ref, ...), custom_call_target="tpu_custom_call" | custom-call | flops 3000000000 | bytes 4202496 | tf_op jit(solution)/shard_map/gin/pallas_call | solution.py:79
  255.1 2.0 add_convert_fusion.4
  257.8 5.6 %down.1 = (bf16[256,1024]{1,0:T(8,128)(2,1)}, bf16[256,1024]{1,0:T(8,128)(2,1)}, bf16[2,256,1024]{2,1,0:T(8,128)(2,1)}) custom-call(s32[28]{0:T(128)} %stack.115.idx_ref.refs_0_, bf16[1024,704]{1,0:T(8,128)(2,1)} %get-tuple-element.198.h_ref.refs_1_, bf16[2112,128]{1,0:T(8,128)(2,1)} %copy-done.20, ...), custom_call_target="tpu_custom_call" | custom-call | flops 17763950592 | bytes 7864432 | tf_op jit(solution)/shard_map/down/pallas_call | solution.py:79
  263.4 1.8 collective-permute-start.52
  268.6 2.3 collective-permute-done.55
  271.9 1.9 collective-permute-done.56
  275.0 2.7 collective-permute-start.65
  279.0 1.7 convert_add_fusion.1
  281.7 5.3 %collective-permute-done.60 = bf16[128,1792]{1,0:T(8,128)(2,1)S(1)} collective-permute-done((bf16[128,1792]{1,0:T(8,128)(2,1)S(1)}, bf16[128,1792]{1,0:T(8,128)(2,1)S(1)}, u32[]{:S(2)}, u32[]{:S(2)}) %collective-permute-start.60) | collective-permute-done | bytes 458784 | tf_op jit(solution)/shard_map/ppermute | solution.py:729
  287.0 2.0 collective-permute-done.53.ry_ref
  289.6 2.6 collective-permute-start.63
  292.2 4.3 %collective-permute-done.65 = bf16[128,1792]{1,0:T(8,128)(2,1)S(1)} collective-permute-done((bf16[128,1792]{1,0:T(8,128)(2,1)S(1)}, bf16[128,1792]{1,0:T(8,128)(2,1)S(1)}, u32[]{:S(2)}, u32[]{:S(2)}) %collective-permute-start.65) | collective-permute-done | bytes 458784 | tf_op jit(solution)/shard_map/ppermute | solution.py:751
  298.4 3.8 %collective-permute-start.68 = (bf16[128,256]{1,0:T(8,128)(2,1)S(1)}, bf16[128,256]{1,0:T(8,128)(2,1)S(1)}, u32[]{:S(2)}, u32[]{:S(2)}) collective-permute-start(bf16[128,256]{1,0:T(8,128)(2,1)S(1)} %get-tuple-element.230), channel_id=1, source_target_pairs={{0,0},{8,16},{16,8},{24,24},{1,1},{9,17},{17,9},{25,25},{2,2},{10,... | collective-permute-start | bytes 196616 | tf_op jit(solution)/shard_map/ppermute | solution.py:1088
  303.5 2.5 collective-permute-start.67
  307.2 4.3 %collective-permute-done.67.o_in = bf16[128,512]{1,0:T(8,128)(2,1)S(1)} collective-permute-done((bf16[128,512]{1,0:T(8,128)(2,1)S(1)}, bf16[128,512]{1,0:T(8,128)(2,1)S(1)}, u32[]{:S(2)}, u32[]{:S(2)}) %collective-permute-start.67) | collective-permute-done | bytes 131104 | tf_op jit(solution)/shard_map/ppermute | solution.py:1059
  311.6 1.5 finish.1
  (246 shorter events, 51.5 us)
Async XLA Ops:
  1.6 11.7 %collective-permute-start = (bf16[128,512]{1,0:T(8,128)(2,1)S(1)}, bf16[128,512]{1,0:T(8,128)(2,1)S(1)}, u32[]{:S(2)}, u32[]{:S(2)}) collective-permute-start(bf16[128,512]{1,0:T(8,128)(2,1)S(1)} %pad_maximum_fusion.3), channel_id=1, source_target_pairs={{0,16},{8,24},{16,0},{24,8},{1,17},{9,25},{17,1},{25,9},{2,18},{10... | collective-permute-start | bytes 393224 | tf_op jit(solution)/shard_map/ppermute | solution.py:795
  2.9 10.4 %collective-permute-start.4 = (bf16[256,256]{1,0:T(8,128)(2,1)}, bf16[256,256]{1,0:T(8,128)(2,1)}, u32[]{:S(2)}, u32[]{:S(2)}) collective-permute-start(bf16[256,256]{1,0:T(8,128)(2,1)} %param.25), channel_id=1, source_target_pairs={{0,0},{1,16},{2,8},{3,24},{4,4},{5,20},{6,12},{7,28},{8,2},{9,18},... | collective-permute-start | bytes 393224 | tf_op jit(solution)/shard_map/ppermute | solution.py:809
  6.8 6.4 %collective-permute-start.3 = (bf16[128,256]{1,0:T(8,128)(2,1)}, bf16[128,256]{1,0:T(8,128)(2,1)S(1)}, u32[]{:S(2)}, u32[]{:S(2)}) collective-permute-start(bf16[128,256]{1,0:T(8,128)(2,1)} %param.21), channel_id=1, source_target_pairs={{0,0},{16,8},{8,16},{24,24},{1,1},{17,9},{9,17},{25,25},{2,2},{18,... | collective-permute-start | bytes 196616 | tf_op jit(solution)/shard_map/ppermute | solution.py:796
  10.2 3.0 collective-permute-start.5
  15.9 14.4 %collective-permute-start.6 = (bf16[128,1792]{1,0:T(8,128)(2,1)}, bf16[128,1792]{1,0:T(8,128)(2,1)S(1)}, u32[]{:S(2)}, u32[]{:S(2)}) collective-permute-start(bf16[128,1792]{1,0:T(8,128)(2,1)} %get-tuple-element.127.refs_5_.refs_9_), channel_id=1, source_target_pairs={{0,2},{1,3},{2,4},{3,5},{4,6},{5,7},{6,0},{7,1},{8,10},{9,11},{10,... | collective-permute-start | bytes 1376264 | tf_op jit(solution)/shard_map/ppermute | solution.py:821
  16.2 14.0 %collective-permute-start.8 = (bf16[128,1792]{1,0:T(8,128)(2,1)}, bf16[128,1792]{1,0:T(8,128)(2,1)S(1)}, u32[]{:S(2)}, u32[]{:S(2)}) collective-permute-start(bf16[128,1792]{1,0:T(8,128)(2,1)} %get-tuple-element.127.refs_5_.refs_9_), channel_id=1, source_target_pairs={{0,1},{1,0},{2,3},{3,2},{4,5},{5,4},{6,7},{7,6},{8,9},{9,8},{10,11... | collective-permute-start | bytes 1376264 | tf_op jit(solution)/shard_map/ppermute | solution.py:729
  30.3 11.9 %collective-permute-start.9 = (bf16[128,1792]{1,0:T(8,128)(2,1)S(1)}, bf16[128,1792]{1,0:T(8,128)(2,1)S(1)}, u32[]{:S(2)}, u32[]{:S(2)}) collective-permute-start(bf16[128,1792]{1,0:T(8,128)(2,1)S(1)} %collective-permute-done.6.refs_6_.refs_10_), channel_id=1, source_target_pairs={{0,1},{1,0},{2,3},{3,2},{4,5},{5,4},{6,7},{7,6},{8,9},{9,8},{10,11... | collective-permute-start | bytes 1376264 | tf_op jit(solution)/shard_map/ppermute | solution.py:729
  30.5 12.1 %collective-permute-start.7 = (bf16[128,1792]{1,0:T(8,128)(2,1)}, bf16[128,1792]{1,0:T(8,128)(2,1)S(1)}, u32[]{:S(2)}, u32[]{:S(2)}) collective-permute-start(bf16[128,1792]{1,0:T(8,128)(2,1)} %get-tuple-element.127.refs_5_.refs_9_), channel_id=1, source_target_pairs={{0,6},{1,7},{2,0},{3,1},{4,2},{5,3},{6,4},{7,5},{8,14},{9,15},{10,... | collective-permute-start | bytes 1376264 | tf_op jit(solution)/shard_map/ppermute | solution.py:823
  35.5 13.1 %collective-permute-start.2 = (bf16[256,1024]{1,0:T(8,128)(2,1)}, bf16[256,1024]{1,0:T(8,128)(2,1)}, u32[]{:S(2)}, u32[]{:S(2)}) collective-permute-start(bf16[256,1024]{1,0:T(8,128)(2,1)} %get-tuple-element.121.refs_1_.refs_5_), channel_id=1, source_target_pairs={{0,16},{8,24},{16,0},{24,8},{1,17},{9,25},{17,1},{25,9},{2,18},{10... | collective-permute-start | bytes 1572872 | tf_op jit(solution)/shard_map/ppermute | solution.py:710
  42.6 22.8 %collective-permute-start.12 = (bf16[128,1792]{1,0:T(8,128)(2,1)S(1)}, bf16[128,1792]{1,0:T(8,128)(2,1)}, u32[]{:S(2)}, u32[]{:S(2)}) collective-permute-start(bf16[128,1792]{1,0:T(8,128)(2,1)S(1)} %copy-done.40), channel_id=1, source_target_pairs={{0,4},{1,5},{2,6},{3,7},{4,0},{5,1},{6,2},{7,3},{8,12},{9,13},{10,... | collective-permute-start | bytes 1376264 | tf_op jit(solution)/shard_map/ppermute | solution.py:825
  44.2 23.2 %collective-permute-start.10 = (bf16[128,1792]{1,0:T(8,128)(2,1)S(1)}, bf16[128,1792]{1,0:T(8,128)(2,1)S(1)}, u32[]{:S(2)}, u32[]{:S(2)}) collective-permute-start(bf16[128,1792]{1,0:T(8,128)(2,1)S(1)} %collective-permute-done.7.refs_8_.refs_12_), channel_id=1, source_target_pairs={{0,1},{1,0},{2,3},{3,2},{4,5},{5,4},{6,7},{7,6},{8,9},{9,8},{10,11... | collective-permute-start | bytes 1376264 | tf_op jit(solution)/shard_map/ppermute | solution.py:729
  48.6 18.9 %collective-permute-start.14 = (bf16[16,512]{1,0:T(8,128)(2,1)S(1)}, bf16[16,512]{1,0:T(8,128)(2,1)S(1)}, u32[]{:S(2)}, u32[]{:S(2)}) collective-permute-start(bf16[16,512]{1,0:T(8,128)(2,1)S(1)} %copy-done.26), channel_id=1, source_target_pairs={{0,2},{1,3},{2,4},{3,5},{4,6},{5,7},{6,0},{7,1},{8,10},{9,11},{10,... | collective-permute-start | bytes 49160 | tf_op jit(solution)/shard_map/ppermute | solution.py:843
  48.6 19.0 %collective-permute-start.15 = (bf16[16,512]{1,0:T(8,128)(2,1)S(1)}, bf16[16,512]{1,0:T(8,128)(2,1)S(1)}, u32[]{:S(2)}, u32[]{:S(2)}) collective-permute-start(bf16[16,512]{1,0:T(8,128)(2,1)S(1)} %copy-done.26), channel_id=1, source_target_pairs={{0,4},{1,5},{2,6},{3,7},{4,0},{5,1},{6,2},{7,3},{8,12},{9,13},{10,... | collective-permute-start | bytes 49160 | tf_op jit(solution)/shard_map/ppermute | solution.py:843
  50.1 17.6 %collective-permute-start.16 = (bf16[16,512]{1,0:T(8,128)(2,1)S(1)}, bf16[16,512]{1,0:T(8,128)(2,1)S(1)}, u32[]{:S(2)}, u32[]{:S(2)}) collective-permute-start(bf16[16,512]{1,0:T(8,128)(2,1)S(1)} %copy-done.26), channel_id=1, source_target_pairs={{0,6},{1,7},{2,0},{3,1},{4,2},{5,3},{6,4},{7,5},{8,14},{9,15},{10,... | collective-permute-start | bytes 49160 | tf_op jit(solution)/shard_map/ppermute | solution.py:843
  65.5 18.6 %collective-permute-start.1 = (bf16[256,1024]{1,0:T(8,128)(2,1)}, bf16[256,1024]{1,0:T(8,128)(2,1)}, u32[]{:S(2)}, u32[]{:S(2)}) collective-permute-start(bf16[256,1024]{1,0:T(8,128)(2,1)} %get-tuple-element.121.refs_1_.refs_5_), channel_id=1, source_target_pairs={{0,8},{8,0},{16,24},{24,16},{1,9},{9,1},{17,25},{25,17},{2,10},{10... | collective-permute-start | bytes 1572872 | tf_op jit(solution)/shard_map/ppermute | solution.py:711
  67.5 15.7 %collective-permute-start.20 = (bf16[2112,128]{1,0:T(8,128)(2,1)S(1)}, bf16[2112,128]{1,0:T(8,128)(2,1)}, u32[]{:S(2)}, u32[]{:S(2)}) collective-permute-start(bf16[2112,128]{1,0:T(8,128)(2,1)S(1)} %pad_maximum_fusion.refs_9_.refs_2_), channel_id=1, source_target_pairs={{0,2},{1,3},{2,4},{3,5},{4,6},{5,7},{6,0},{7,1},{8,10},{9,11},{10,... | collective-permute-start | bytes 1622024 | tf_op jit(solution)/shard_map/ppermute | solution.py:830
  67.5 18.0 %collective-permute-start.11 = (bf16[256,1024]{1,0:T(8,128)(2,1)}, bf16[256,1024]{1,0:T(8,128)(2,1)}, u32[]{:S(2)}, u32[]{:S(2)}) collective-permute-start(bf16[256,1024]{1,0:T(8,128)(2,1)} %collective-permute-done.2.refs_3_.refs_7_), channel_id=1, source_target_pairs={{0,8},{8,0},{16,24},{24,16},{1,9},{9,1},{17,25},{25,17},{2,10},{10... | collective-permute-start | bytes 1572872 | tf_op jit(solution)/shard_map/ppermute | solution.py:828
  67.6 3.2 %collective-permute-start.18 = (bf16[64,512]{1,0:T(8,128)(2,1)S(1)}, bf16[64,512]{1,0:T(8,128)(2,1)S(1)}, u32[]{:S(2)}, u32[]{:S(2)}) collective-permute-start(bf16[64,512]{1,0:T(8,128)(2,1)S(1)} %pad_maximum_fusion.5.v0), channel_id=1, source_target_pairs={{0,16},{8,24},{16,0},{24,8},{1,17},{9,25},{17,1},{25,9},{2,18},{10... | collective-permute-start | bytes 196616 | tf_op jit(solution)/shard_map/ppermute | solution.py:710
  67.7 12.0 %collective-permute-start.13 = (bf16[128,1792]{1,0:T(8,128)(2,1)}, bf16[128,1792]{1,0:T(8,128)(2,1)}, u32[]{:S(2)}, u32[]{:S(2)}) collective-permute-start(bf16[128,1792]{1,0:T(8,128)(2,1)} %collective-permute-done.12.refs_7_.refs_11_), channel_id=1, source_target_pairs={{0,1},{1,0},{2,3},{3,2},{4,5},{5,4},{6,7},{7,6},{8,9},{9,8},{10,11... | collective-permute-start | bytes 1376264 | tf_op jit(solution)/shard_map/ppermute | solution.py:729
  74.6 22.0 %collective-permute-start.23 = (bf16[256,1024]{1,0:T(8,128)(2,1)}, bf16[256,1024]{1,0:T(8,128)(2,1)}, u32[]{:S(2)}, u32[]{:S(2)}) collective-permute-start(bf16[256,1024]{1,0:T(8,128)(2,1)} %get-tuple-element.169.refs_5_.c0.c_ref), channel_id=1, source_target_pairs={{0,8},{8,0},{16,24},{24,16},{1,9},{9,1},{17,25},{25,17},{2,10},{10... | collective-permute-start | bytes 1572872 | tf_op jit(solution)/shard_map/ppermute | solution.py:711
  79.8 16.8 %collective-permute-start.24 = (bf16[256,1024]{1,0:T(8,128)(2,1)}, bf16[256,1024]{1,0:T(8,128)(2,1)}, u32[]{:S(2)}, u32[]{:S(2)}) collective-permute-start(bf16[256,1024]{1,0:T(8,128)(2,1)} %get-tuple-element.169.refs_5_.c0.c_ref), channel_id=1, source_target_pairs={{0,16},{8,24},{16,0},{24,8},{1,17},{9,25},{17,1},{25,9},{2,18},{10... | collective-permute-start | bytes 1572872 | tf_op jit(solution)/shard_map/ppermute | solution.py:710
  83.2 13.3 %collective-permute-start.22 = (bf16[2112,128]{1,0:T(8,128)(2,1)S(1)}, bf16[2112,128]{1,0:T(8,128)(2,1)}, u32[]{:S(2)}, u32[]{:S(2)}) collective-permute-start(bf16[2112,128]{1,0:T(8,128)(2,1)S(1)} %pad_maximum_fusion.refs_9_.refs_2_), channel_id=1, source_target_pairs={{0,1},{1,0},{2,3},{3,2},{4,5},{5,4},{6,7},{7,6},{8,9},{9,8},{10,11... | collective-permute-start | bytes 1622024 | tf_op jit(solution)/shard_map/ppermute | solution.py:729
  84.1 12.8 %collective-permute-start.21 = (bf16[2112,128]{1,0:T(8,128)(2,1)S(1)}, bf16[2112,128]{1,0:T(8,128)(2,1)}, u32[]{:S(2)}, u32[]{:S(2)}) collective-permute-start(bf16[2112,128]{1,0:T(8,128)(2,1)S(1)} %pad_maximum_fusion.refs_9_.refs_2_), channel_id=1, source_target_pairs={{0,6},{1,7},{2,0},{3,1},{4,2},{5,3},{6,4},{7,5},{8,14},{9,15},{10,... | collective-permute-start | bytes 1622024 | tf_op jit(solution)/shard_map/ppermute | solution.py:831
  96.8 4.7 %collective-permute-start.25 = (bf16[2,256,1152]{2,1,0:T(8,128)(2,1)}, bf16[2,256,1152]{2,1,0:T(8,128)(2,1)S(1)}, u32[]{:S(2)}, u32[]{:S(2)}) collective-permute-start(bf16[2,256,1152]{2,1,0:T(8,128)(2,1)} %get-tuple-element.146), channel_id=1, source_target_pairs={{0,8},{8,0},{16,24},{24,16},{1,9},{9,1},{17,25},{25,17},{2,10},{10... | collective-permute-start | bytes 3538952 | tf_op jit(solution)/shard_map/ppermute | solution.py:935
  102.9 16.5 %collective-permute-start.26 = (bf16[256,1152]{1,0:T(8,128)(2,1)S(1)}, bf16[256,1152]{1,0:T(8,128)(2,1)S(1)}, u32[]{:S(2)}, u32[]{:S(2)}) collective-permute-start(bf16[256,1152]{1,0:T(8,128)(2,1)S(1)} %fusion), channel_id=1, source_target_pairs={{0,16},{8,24},{16,0},{24,8},{1,17},{9,25},{17,1},{25,9},{2,18},{10... | collective-permute-start | bytes 1769480 | tf_op jit(solution)/shard_map/ppermute | solution.py:718
  103.0 13.6 %collective-permute-start.28 = (bf16[2112,128]{1,0:T(8,128)(2,1)}, bf16[2112,128]{1,0:T(8,128)(2,1)S(1)}, u32[]{:S(2)}, u32[]{:S(2)}) collective-permute-start(bf16[2112,128]{1,0:T(8,128)(2,1)} %collective-permute-done.20.refs_10_.refs_3_), channel_id=1, source_target_pairs={{0,1},{1,0},{2,3},{3,2},{4,5},{5,4},{6,7},{7,6},{8,9},{9,8},{10,11... | collective-permute-start | bytes 1622024 | tf_op jit(solution)/shard_map/ppermute | solution.py:729
  103.6 13.5 %collective-permute-start.29 = (bf16[256,1024]{1,0:T(8,128)(2,1)}, bf16[256,1024]{1,0:T(8,128)(2,1)S(1)}, u32[]{:S(2)}, u32[]{:S(2)}) collective-permute-start(bf16[256,1024]{1,0:T(8,128)(2,1)} %collective-permute-done.24.refs_7_.c2), channel_id=1, source_target_pairs={{0,8},{8,0},{16,24},{24,16},{1,9},{9,1},{17,25},{25,17},{2,10},{10... | collective-permute-start | bytes 1572872 | tf_op jit(solution)/shard_map/ppermute | solution.py:712
  104.5 14.9 %collective-permute-start.27 = (bf16[1056,128]{1,0:T(8,128)(2,1)S(1)}, bf16[1056,128]{1,0:T(8,128)(2,1)S(1)}, u32[]{:S(2)}, u32[]{:S(2)}) collective-permute-start(bf16[1056,128]{1,0:T(8,128)(2,1)S(1)} %get-tuple-element.148), channel_id=1, source_target_pairs={{0,4},{1,5},{2,6},{3,7},{4,0},{5,1},{6,2},{7,3},{8,12},{9,13},{10,... | collective-permute-start | bytes 811016 | tf_op jit(solution)/shard_map/ppermute | solution.py:834
  116.5 12.6 %collective-permute-start.32 = (bf16[2112,128]{1,0:T(8,128)(2,1)}, bf16[2112,128]{1,0:T(8,128)(2,1)S(1)}, u32[]{:S(2)}, u32[]{:S(2)}) collective-permute-start(bf16[2112,128]{1,0:T(8,128)(2,1)} %collective-permute-done.21.refs_12_.refs_5_), channel_id=1, source_target_pairs={{0,1},{1,0},{2,3},{3,2},{4,5},{5,4},{6,7},{7,6},{8,9},{9,8},{10,11... | collective-permute-start | bytes 1622024 | tf_op jit(solution)/shard_map/ppermute | solution.py:729
  121.5 16.1 %collective-permute-start.31 = (bf16[256,1024]{1,0:T(8,128)(2,1)S(1)}, bf16[256,1024]{1,0:T(8,128)(2,1)S(1)}, u32[]{:S(2)}, u32[]{:S(2)}) collective-permute-start(bf16[256,1024]{1,0:T(8,128)(2,1)S(1)} %get-tuple-element.153.refs_1_.x0), channel_id=1, source_target_pairs={{0,16},{8,24},{16,0},{24,8},{1,17},{9,25},{17,1},{25,9},{2,18},{10... | collective-permute-start | bytes 1572872 | tf_op jit(solution)/shard_map/ppermute | solution.py:710
  123.0 14.6 %collective-permute-start.34 = (bf16[1056,128]{1,0:T(8,128)(2,1)S(1)}, bf16[1056,128]{1,0:T(8,128)(2,1)S(1)}, u32[]{:S(2)}, u32[]{:S(2)}) collective-permute-start(bf16[1056,128]{1,0:T(8,128)(2,1)S(1)} %get-tuple-element.156), channel_id=1, source_target_pairs={{0,4},{1,5},{2,6},{3,7},{4,0},{5,1},{6,2},{7,3},{8,12},{9,13},{10,... | collective-permute-start | bytes 811016 | tf_op jit(solution)/shard_map/ppermute | solution.py:835
  129.1 8.5 %collective-permute-start.33 = (bf16[1056,128]{1,0:T(8,128)(2,1)S(1)}, bf16[1056,128]{1,0:T(8,128)(2,1)S(1)}, u32[]{:S(2)}, u32[]{:S(2)}) collective-permute-start(bf16[1056,128]{1,0:T(8,128)(2,1)S(1)} %collective-permute-done.27.refs_11_.refs_4_), channel_id=1, source_target_pairs={{0,1},{1,0},{2,3},{3,2},{4,5},{5,4},{6,7},{7,6},{8,9},{9,8},{10,11... | collective-permute-start | bytes 811016 | tf_op jit(solution)/shard_map/ppermute | solution.py:729
  129.7 16.6 %collective-permute-start.30 = (bf16[256,1024]{1,0:T(8,128)(2,1)S(1)}, bf16[256,1024]{1,0:T(8,128)(2,1)S(1)}, u32[]{:S(2)}, u32[]{:S(2)}) collective-permute-start(bf16[256,1024]{1,0:T(8,128)(2,1)S(1)} %get-tuple-element.153.refs_1_.x0), channel_id=1, source_target_pairs={{0,8},{8,0},{16,24},{24,16},{1,9},{9,1},{17,25},{25,17},{2,10},{10... | collective-permute-start | bytes 1572872 | tf_op jit(solution)/shard_map/ppermute | solution.py:711
  137.6 9.5 %collective-permute-start.35 = (bf16[256,1024]{1,0:T(8,128)(2,1)S(1)}, bf16[256,1024]{1,0:T(8,128)(2,1)}, u32[]{:S(2)}, u32[]{:S(2)}) collective-permute-start(bf16[256,1024]{1,0:T(8,128)(2,1)S(1)} %collective-permute-done.31.refs_3_.x2), channel_id=1, source_target_pairs={{0,8},{8,0},{16,24},{24,16},{1,9},{9,1},{17,25},{25,17},{2,10},{10... | collective-permute-start | bytes 1572872 | tf_op jit(solution)/shard_map/ppermute | solution.py:945
  138.2 8.1 %collective-permute-start.36 = (bf16[1056,128]{1,0:T(8,128)(2,1)S(1)}, bf16[1056,128]{1,0:T(8,128)(2,1)S(1)}, u32[]{:S(2)}, u32[]{:S(2)}) collective-permute-start(bf16[1056,128]{1,0:T(8,128)(2,1)S(1)} %collective-permute-done.34.refs_17_.refs_10_), channel_id=1, source_target_pairs={{0,1},{1,0},{2,3},{3,2},{4,5},{5,4},{6,7},{7,6},{8,9},{9,8},{10,11... | collective-permute-start | bytes 811016 | tf_op jit(solution)/shard_map/ppermute | solution.py:729
  162.6 3.4 %collective-permute-start.37 = (bf16[2,256,1024]{2,1,0:T(8,128)(2,1)}, bf16[2,256,1024]{2,1,0:T(8,128)(2,1)S(1)}, u32[]{:S(2)}, u32[]{:S(2)}) collective-permute-start(bf16[2,256,1024]{2,1,0:T(8,128)(2,1)} %get-tuple-element.161), channel_id=1, source_target_pairs={{0,8},{8,0},{16,24},{24,16},{1,9},{9,1},{17,25},{25,17},{2,10},{10... | collective-permute-start | bytes 3145736 | tf_op jit(solution)/shard_map/ppermute | solution.py:962
  163.5 15.4 %collective-permute-start.39 = (bf16[2112,128]{1,0:T(8,128)(2,1)}, bf16[2112,128]{1,0:T(8,128)(2,1)}, u32[]{:S(2)}, u32[]{:S(2)}) collective-permute-start(bf16[2112,128]{1,0:T(8,128)(2,1)} %get-tuple-element.168), channel_id=1, source_target_pairs={{0,1},{1,0},{2,3},{3,2},{4,5},{5,4},{6,7},{7,6},{8,9},{9,8},{10,11... | collective-permute-start | bytes 1622024 | tf_op jit(solution)/shard_map/ppermute | solution.py:729
  168.4 13.8 %collective-permute-start.38 = (bf16[256,1024]{1,0:T(8,128)(2,1)}, bf16[256,1024]{1,0:T(8,128)(2,1)}, u32[]{:S(2)}, u32[]{:S(2)}) collective-permute-start(bf16[256,1024]{1,0:T(8,128)(2,1)} %fusion.3), channel_id=1, source_target_pairs={{0,16},{8,24},{16,0},{24,8},{1,17},{9,25},{17,1},{25,9},{2,18},{10... | collective-permute-start | bytes 1572872 | tf_op jit(solution)/shard_map/ppermute | solution.py:964
  178.9 13.5 %collective-permute-start.42 = (bf16[2112,128]{1,0:T(8,128)(2,1)}, bf16[2112,128]{1,0:T(8,128)(2,1)}, u32[]{:S(2)}, u32[]{:S(2)}) collective-permute-start(bf16[2112,128]{1,0:T(8,128)(2,1)} %get-tuple-element.175), channel_id=1, source_target_pairs={{0,1},{1,0},{2,3},{3,2},{4,5},{5,4},{6,7},{7,6},{8,9},{9,8},{10,11... | collective-permute-start | bytes 1622024 | tf_op jit(solution)/shard_map/ppermute | solution.py:729
  181.6 47.3 %collective-permute-start.46 = (bf16[2112,128]{1,0:T(8,128)(2,1)}, bf16[2112,128]{1,0:T(8,128)(2,1)S(1)}, u32[]{:S(2)}, u32[]{:S(2)}) collective-permute-start(bf16[2112,128]{1,0:T(8,128)(2,1)} %add_convert_fusion.2), channel_id=1, source_target_pairs={{0,4},{1,5},{2,6},{3,7},{4,0},{5,1},{6,2},{7,3},{8,12},{9,13},{10,... | collective-permute-start | bytes 1622024 | tf_op jit(solution)/shard_map/ppermute | solution.py:751
  187.0 18.6 %collective-permute-start.41 = (bf16[256,1152]{1,0:T(8,128)(2,1)}, bf16[256,1152]{1,0:T(8,128)(2,1)S(1)}, u32[]{:S(2)}, u32[]{:S(2)}) collective-permute-start(bf16[256,1152]{1,0:T(8,128)(2,1)} %get-tuple-element.171.refs_1_), channel_id=1, source_target_pairs={{0,16},{8,24},{16,0},{24,8},{1,17},{9,25},{17,1},{25,9},{2,18},{10... | collective-permute-start | bytes 1769480 | tf_op jit(solution)/shard_map/ppermute | solution.py:710
  187.8 21.4 %collective-permute-start.40 = (bf16[256,1152]{1,0:T(8,128)(2,1)}, bf16[256,1152]{1,0:T(8,128)(2,1)S(1)}, u32[]{:S(2)}, u32[]{:S(2)}) collective-permute-start(bf16[256,1152]{1,0:T(8,128)(2,1)} %get-tuple-element.171.refs_1_), channel_id=1, source_target_pairs={{0,8},{8,0},{16,24},{24,16},{1,9},{9,1},{17,25},{25,17},{2,10},{10... | collective-permute-start | bytes 1769480 | tf_op jit(solution)/shard_map/ppermute | solution.py:711
  192.5 12.6 %collective-permute-start.43 = (bf16[2112,128]{1,0:T(8,128)(2,1)}, bf16[2112,128]{1,0:T(8,128)(2,1)S(1)}, u32[]{:S(2)}, u32[]{:S(2)}) collective-permute-start(bf16[2112,128]{1,0:T(8,128)(2,1)} %get-tuple-element.179), channel_id=1, source_target_pairs={{0,1},{1,0},{2,3},{3,2},{4,5},{5,4},{6,7},{7,6},{8,9},{9,8},{10,11... | collective-permute-start | bytes 1622024 | tf_op jit(solution)/shard_map/ppermute | solution.py:729
  195.3 33.6 %collective-permute-start.47 = (bf16[2112,128]{1,0:T(8,128)(2,1)}, bf16[2112,128]{1,0:T(8,128)(2,1)}, u32[]{:S(2)}, u32[]{:S(2)}) collective-permute-start(bf16[2112,128]{1,0:T(8,128)(2,1)} %add_convert_fusion.1), channel_id=1, source_target_pairs={{0,2},{1,3},{2,4},{3,5},{4,6},{5,7},{6,0},{7,1},{8,10},{9,11},{10,... | collective-permute-start | bytes 1622024 | tf_op jit(solution)/shard_map/ppermute | solution.py:751
  205.0 23.9 %collective-permute-start.48 = (bf16[2112,128]{1,0:T(8,128)(2,1)}, bf16[2112,128]{1,0:T(8,128)(2,1)}, u32[]{:S(2)}, u32[]{:S(2)}) collective-permute-start(bf16[2112,128]{1,0:T(8,128)(2,1)} %get-tuple-element.191), channel_id=1, source_target_pairs={{0,1},{1,0},{2,3},{3,2},{4,5},{5,4},{6,7},{7,6},{8,9},{9,8},{10,11... | collective-permute-start | bytes 1622024 | tf_op jit(solution)/shard_map/ppermute | solution.py:729
  205.6 4.3 %collective-permute-start.44 = (bf16[256,1152]{1,0:T(8,128)(2,1)S(1)}, bf16[256,1152]{1,0:T(8,128)(2,1)S(1)}, u32[]{:S(2)}, u32[]{:S(2)}) collective-permute-start(bf16[256,1152]{1,0:T(8,128)(2,1)S(1)} %collective-permute-done.41.refs_3_), channel_id=1, source_target_pairs={{0,8},{8,0},{16,24},{24,16},{1,9},{9,1},{17,25},{25,17},{2,10},{10... | collective-permute-start | bytes 1769480 | tf_op jit(solution)/shard_map/ppermute | solution.py:1004
  228.9 7.1 %collective-permute-start.49 = (bf16[2,256,1024]{2,1,0:T(8,128)(2,1)}, bf16[2,256,1024]{2,1,0:T(8,128)(2,1)S(1)}, u32[]{:S(2)}, u32[]{:S(2)}) collective-permute-start(bf16[2,256,1024]{2,1,0:T(8,128)(2,1)} %get-tuple-element.192), channel_id=1, source_target_pairs={{0,8},{8,0},{16,24},{24,16},{1,9},{9,1},{17,25},{25,17},{2,10},{10... | collective-permute-start | bytes 3145736 | tf_op jit(solution)/shard_map/ppermute | solution.py:1028
  229.4 12.3 %collective-permute-start.45 = (bf16[128,1792]{1,0:T(8,128)(2,1)}, bf16[128,1792]{1,0:T(8,128)(2,1)S(1)}, u32[]{:S(2)}, u32[]{:S(2)}) collective-permute-start(bf16[128,1792]{1,0:T(8,128)(2,1)} %get-tuple-element.187), channel_id=1, source_target_pairs={{0,1},{1,0},{2,3},{3,2},{4,5},{5,4},{6,7},{7,6},{8,9},{9,8},{10,11... | collective-permute-start | bytes 1376264 | tf_op jit(solution)/shard_map/ppermute | solution.py:729
  232.8 22.3 %collective-permute-start.51 = (bf16[2112,128]{1,0:T(8,128)(2,1)}, bf16[2112,128]{1,0:T(8,128)(2,1)}, u32[]{:S(2)}, u32[]{:S(2)}) collective-permute-start(bf16[2112,128]{1,0:T(8,128)(2,1)} %add_convert_fusion), channel_id=1, source_target_pairs={{0,6},{1,7},{2,0},{3,1},{4,2},{5,3},{6,4},{7,5},{8,14},{9,15},{10,... | collective-permute-start | bytes 1622024 | tf_op jit(solution)/shard_map/ppermute | solution.py:751
  237.7 12.9 %collective-permute-start.50 = (bf16[256,1024]{1,0:T(8,128)(2,1)S(1)}, bf16[256,1024]{1,0:T(8,128)(2,1)S(1)}, u32[]{:S(2)}, u32[]{:S(2)}) collective-permute-start(bf16[256,1024]{1,0:T(8,128)(2,1)S(1)} %fusion.2), channel_id=1, source_target_pairs={{0,16},{8,24},{16,0},{24,8},{1,17},{9,25},{17,1},{25,9},{2,18},{10... | collective-permute-start | bytes 1572872 | tf_op jit(solution)/shard_map/ppermute | solution.py:718
  242.6 12.6 %collective-permute-start.58 = (bf16[128,1792]{1,0:T(8,128)(2,1)}, bf16[128,1792]{1,0:T(8,128)(2,1)}, u32[]{:S(2)}, u32[]{:S(2)}) collective-permute-start(bf16[128,1792]{1,0:T(8,128)(2,1)} %get-tuple-element.213), channel_id=1, source_target_pairs={{0,1},{1,0},{2,3},{3,2},{4,5},{5,4},{6,7},{7,6},{8,9},{9,8},{10,11... | collective-permute-start | bytes 1376264 | tf_op jit(solution)/shard_map/ppermute | solution.py:729
  243.4 28.4 %collective-permute-start.57 = (bf16[128,1792]{1,0:T(8,128)(2,1)}, bf16[128,1792]{1,0:T(8,128)(2,1)}, u32[]{:S(2)}, u32[]{:S(2)}) collective-permute-start(bf16[128,1792]{1,0:T(8,128)(2,1)} %add_convert_fusion.5), channel_id=1, source_target_pairs={{0,4},{1,5},{2,6},{3,7},{4,0},{5,1},{6,2},{7,3},{8,12},{9,13},{10,... | collective-permute-start | bytes 1376264 | tf_op jit(solution)/shard_map/ppermute | solution.py:751
  257.2 16.6 %collective-permute-start.59 = (bf16[128,1792]{1,0:T(8,128)(2,1)}, bf16[128,1792]{1,0:T(8,128)(2,1)}, u32[]{:S(2)}, u32[]{:S(2)}) collective-permute-start(bf16[128,1792]{1,0:T(8,128)(2,1)} %get-tuple-element.214), channel_id=1, source_target_pairs={{0,1},{1,0},{2,3},{3,2},{4,5},{5,4},{6,7},{7,6},{8,9},{9,8},{10,11... | collective-permute-start | bytes 1376264 | tf_op jit(solution)/shard_map/ppermute | solution.py:729
  263.4 14.9 %collective-permute-start.52 = (bf16[2,256,1024]{2,1,0:T(8,128)(2,1)}, bf16[2,256,1024]{2,1,0:T(8,128)(2,1)S(1)}, u32[]{:S(2)}, u32[]{:S(2)}) collective-permute-start(bf16[2,256,1024]{2,1,0:T(8,128)(2,1)} %get-tuple-element.200), channel_id=1, source_target_pairs={{0,8},{8,0},{16,24},{24,16},{1,9},{9,1},{17,25},{25,17},{2,10},{10... | collective-permute-start | bytes 3145736 | tf_op jit(solution)/shard_map/ppermute | solution.py:1044
  271.8 20.4 %collective-permute-start.64 = (bf16[128,1792]{1,0:T(8,128)(2,1)}, bf16[128,1792]{1,0:T(8,128)(2,1)S(1)}, u32[]{:S(2)}, u32[]{:S(2)}) collective-permute-start(bf16[128,1792]{1,0:T(8,128)(2,1)} %add_convert_fusion.4), channel_id=1, source_target_pairs={{0,2},{1,3},{2,4},{3,5},{4,6},{5,7},{6,0},{7,1},{8,10},{9,11},{10,... | collective-permute-start | bytes 1376264 | tf_op jit(solution)/shard_map/ppermute | solution.py:751
  275.0 21.5 %collective-permute-start.65 = (bf16[128,1792]{1,0:T(8,128)(2,1)S(1)}, bf16[128,1792]{1,0:T(8,128)(2,1)S(1)}, u32[]{:S(2)}, u32[]{:S(2)}) collective-permute-start(bf16[128,1792]{1,0:T(8,128)(2,1)S(1)} %add_convert_fusion.3), channel_id=1, source_target_pairs={{0,6},{1,7},{2,0},{3,1},{4,2},{5,3},{6,4},{7,5},{8,14},{9,15},{10,... | collective-permute-start | bytes 1376264 | tf_op jit(solution)/shard_map/ppermute | solution.py:751
  277.7 9.3 %collective-permute-start.60 = (bf16[128,1792]{1,0:T(8,128)(2,1)S(1)}, bf16[128,1792]{1,0:T(8,128)(2,1)S(1)}, u32[]{:S(2)}, u32[]{:S(2)}) collective-permute-start(bf16[128,1792]{1,0:T(8,128)(2,1)S(1)} %copy-done.46), channel_id=1, source_target_pairs={{0,1},{1,0},{2,3},{3,2},{4,5},{5,4},{6,7},{7,6},{8,9},{9,8},{10,11... | collective-permute-start | bytes 1376264 | tf_op jit(solution)/shard_map/ppermute | solution.py:729
  278.5 10.5 %collective-permute-start.53 = (bf16[256,1024]{1,0:T(8,128)(2,1)S(1)}, bf16[256,1024]{1,0:T(8,128)(2,1)S(1)}, u32[]{:S(2)}, u32[]{:S(2)}) collective-permute-start(bf16[256,1024]{1,0:T(8,128)(2,1)S(1)} %fusion.1), channel_id=1, source_target_pairs={{0,16},{8,24},{16,0},{24,8},{1,17},{9,25},{17,1},{25,9},{2,18},{10... | collective-permute-start | bytes 1572872 | tf_op jit(solution)/shard_map/ppermute | solution.py:718
  289.0 14.5 %collective-permute-start.61 = (f32[32,160]{1,0:T(8,128)S(1)}, f32[32,160]{1,0:T(8,128)S(1)}, u32[]{:S(2)}, u32[]{:S(2)}) collective-permute-start(f32[32,160]{1,0:T(8,128)S(1)} %add.275), channel_id=1, source_target_pairs={{0,2},{1,3},{2,4},{3,5},{4,6},{5,7},{6,0},{7,1},{8,10},{9,11},{10,... | collective-permute-start | bytes 61448 | tf_op jit(solution)/shard_map/ppermute | solution.py:765
  289.0 17.0 %collective-permute-start.62 = (f32[32,160]{1,0:T(8,128)S(1)}, f32[32,160]{1,0:T(8,128)S(1)}, u32[]{:S(2)}, u32[]{:S(2)}) collective-permute-start(f32[32,160]{1,0:T(8,128)S(1)} %add.275), channel_id=1, source_target_pairs={{0,4},{1,5},{2,6},{3,7},{4,0},{5,1},{6,2},{7,3},{8,12},{9,13},{10,... | collective-permute-start | bytes 61448 | tf_op jit(solution)/shard_map/ppermute | solution.py:765
  289.6 16.4 %collective-permute-start.63 = (f32[32,160]{1,0:T(8,128)S(1)}, f32[32,160]{1,0:T(8,128)S(1)}, u32[]{:S(2)}, u32[]{:S(2)}) collective-permute-start(f32[32,160]{1,0:T(8,128)S(1)} %add.275), channel_id=1, source_target_pairs={{0,6},{1,7},{2,0},{3,1},{4,2},{5,3},{6,4},{7,5},{8,14},{9,15},{10,... | collective-permute-start | bytes 61448 | tf_op jit(solution)/shard_map/ppermute | solution.py:765
  297.9 9.3 %collective-permute-start.66 = (bf16[128,512]{1,0:T(8,128)(2,1)S(1)}, bf16[128,512]{1,0:T(8,128)(2,1)S(1)}, u32[]{:S(2)}, u32[]{:S(2)}) collective-permute-start(bf16[128,512]{1,0:T(8,128)(2,1)S(1)} %pad_maximum_fusion.4), channel_id=1, source_target_pairs={{0,16},{8,24},{16,0},{24,8},{1,17},{9,25},{17,1},{25,9},{2,18},{10... | collective-permute-start | bytes 393224 | tf_op jit(solution)/shard_map/ppermute | solution.py:1084
  298.4 8.9 %collective-permute-start.68 = (bf16[128,256]{1,0:T(8,128)(2,1)S(1)}, bf16[128,256]{1,0:T(8,128)(2,1)S(1)}, u32[]{:S(2)}, u32[]{:S(2)}) collective-permute-start(bf16[128,256]{1,0:T(8,128)(2,1)S(1)} %get-tuple-element.230), channel_id=1, source_target_pairs={{0,0},{8,16},{16,8},{24,24},{1,1},{9,17},{17,9},{25,25},{2,2},{10,... | collective-permute-start | bytes 196616 | tf_op jit(solution)/shard_map/ppermute | solution.py:1088
  303.5 8.1 %collective-permute-start.67 = (bf16[128,512]{1,0:T(8,128)(2,1)S(1)}, bf16[128,512]{1,0:T(8,128)(2,1)S(1)}, u32[]{:S(2)}, u32[]{:S(2)}) collective-permute-start(bf16[128,512]{1,0:T(8,128)(2,1)S(1)} %slice.105), channel_id=1, source_target_pairs={{0,0},{16,1},{8,2},{24,3},{4,4},{20,5},{12,6},{28,7},{2,8},{18,9},... | collective-permute-start | bytes 393224 | tf_op jit(solution)/shard_map/ppermute | solution.py:1059
  (62 other events, 558.0 us)

commit v2 on v1

--- a/solution.py
+++ b/solution.py
@@ -695,6 +695,10 @@
     o_ref[0:rows, :] = o_in[:, 0:ch].astype(F32)
     o_ref[rows:, :] = o_in[:, ch:].astype(F32)
     f_ref[...] = f_in[...].astype(F32)
+
+
+def far_body(k_ref, g_ref, o_ref):
+    o_ref[...] = (k_ref[...].astype(F32) + g_ref[0].astype(F32)).astype(BF)
 
 
 def blockout_body(resid_ref, own_ref, got_ref, ry_ref, out_ref):
@@ -900,7 +904,7 @@
             ],
             axis=1,
         )
-    early = [fz1] if wide else []
+    early = []
     pieces = len(mixes)
     fpieces = len(ffns)
     sign = jnp.where(y == 0, 1.0, -1.0).astype(F32)
@@ -960,7 +964,19 @@
     )
 
     got2 = lax.ppermute(sout2, "seq", CORE)
-    far2 = plus(k12, got2[1])
+    far2 = pl.pallas_call(
+        far_body,
+        grid=(2,),
+        out_shape=sds((blk, width), BF),
+        in_specs=[
+            pl.BlockSpec((blk // 2, width), lambda i: (i, 0)),
+            pl.BlockSpec((1, blk // 2, width), lambda i: (1, i, 0)),
+        ],
+        out_specs=pl.BlockSpec((blk // 2, width), lambda i: (i, 0)),
+        compiler_params=pltpu.CompilerParams(vmem_limit_bytes=63 * MB),
+        cost_estimate=pl.CostEstimate(flops=10**8, bytes_accessed=2 * 10**6, transcendentals=0),
+        name="far",
+    )(k12, got2)
     near2 = lax.ppermute(far2, "seq", YSWAP)
     own_f, kept1, kept3, s1, s3, s0 = call(
         ffn_grad_body,
@@ -1055,7 +1071,7 @@
 
     if wide:
         g_f3 = fsc.total(msc.part[3])
-        g_m = msc.total(near3)
+        g_m = msc.total(block_output)
         o_back = lax.ppermute(g_m[:, 5 * ch :].astype(BF), ("seq", "batch"), OUT_BACK)
     else:
         def whole(parts):

time: 320 us -> 319 us (level)
    convert_element_type x10 -> x9, other arithmetic: 14.8 us -> 12.4 us  [plus(): return (a.astype(F32) + b.astype(F32)).astype(BF)]
    unnamed x114 -> x110, local copies, waits for them, and re-layouts: 7.03 us -> 7.02 us
  transfers between devices with their start and end apart: 69 -> 69, of which waited for: 31 -> 31; matrix products, arithmetic and copies ran while one was open for 8% -> 7% of each run, Pallas kernels for 19% -> 20%
where the time goes in v2:
time: 319 us; the launch traced here: 313 us
  waiting for transfers between devices  129 us (40%)
  Pallas kernels  80.4 us (25%)
  starting transfers between devices  71.5 us (22%)
  other arithmetic  19 us (6%)
  local copies, waits for them, and re-layouts  11.6 us (4%)
    pallas_call x13, Pallas kernels, call(): pl.pallas_call(body, out_shape=outs, in_specs=[pl.BlockSpec(memory_space=...  73.7 us
    ppermute x18, waiting for transfers between devices, xsend(): return lax.ppermute(pack, 'batch', XSWAP)  56.3 us
    ppermute x1, waiting for transfers between devices, per_device(): mz2 = lax.ppermute(after(pack_m, mz3, mx1), 'batch', zshift(2))  13.5 us
    ppermute x18, starting transfers between devices, xsend(): return lax.ppermute(pack, 'batch', XSWAP)  13.2 us
    ppermute x1, waiting for transfers between devices, per_device(): mz1 = lax.ppermute(pack_m, 'batch', zshift(1))  12.6 us
    convert_element_type x9, other arithmetic, plus(): return (a.astype(F32) + b.astype(F32)).astype(BF)  12.4 us
    ppermute x3, waiting for transfers between devices, seq_scatter(): return (got, lax.ppermute(far, 'seq', YSWAP))  8.86 us
    ppermute x5, starting transfers between devices, seq_gather(): cv = lax.ppermute(v, 'seq', CORE)  8.03 us
  transfers between devices with their start and end apart: 69, of which 31 were waited for; matrix products, arithmetic and copies ran while one was open for 7% of the time, Pallas kernels for 20%

profile of v2, /device:TPU:3, one launch (start us, length us, event | category | flops | bytes accessed | tf_op | source)
XLA Modules:
  0.0 312.8 jit_solution(16980078538805152334)
XLA Ops:
  2.9 4.0 %collective-permute-start.4 = (bf16[256,256]{1,0:T(8,128)(2,1)}, bf16[256,256]{1,0:T(8,128)(2,1)}, u32[]{:S(2)}, u32[]{:S(2)}) collective-permute-start(bf16[256,256]{1,0:T(8,128)(2,1)} %param.25), channel_id=1, source_target_pairs={{0,0},{1,16},{2,8},{3,24},{4,4},{5,20},{6,12},{7,28},{8,2},{9,18},... | collective-permute-start | bytes 393224 | tf_op jit(solution)/shard_map/ppermute | solution.py:813
  6.8 1.9 collective-permute-start.3
  8.8 1.4 line.1.l_ref
  10.2 1.7 collective-permute-start.5
  13.9 2.0 pack.1
  16.2 1.5 collective-permute-start.8
  17.7 12.6 %collective-permute-done.6.refs_6_.refs_10_ = bf16[128,1792]{1,0:T(8,128)(2,1)S(1)} collective-permute-done((bf16[128,1792]{1,0:T(8,128)(2,1)}, bf16[128,1792]{1,0:T(8,128)(2,1)S(1)}, u32[]{:S(2)}, u32[]{:S(2)}) %collective-permute-start.6) | collective-permute-done | bytes 458784 | tf_op jit(solution)/shard_map/ppermute | solution.py:825
  30.5 1.7 collective-permute-start.7
  33.3 1.4 norm1.1
  35.5 6.6 %collective-permute-done.9.refs_10_.refs_14_ = bf16[128,1792]{1,0:T(8,128)(2,1)S(1)} collective-permute-done((bf16[128,1792]{1,0:T(8,128)(2,1)S(1)}, bf16[128,1792]{1,0:T(8,128)(2,1)S(1)}, u32[]{:S(2)}, u32[]{:S(2)}) %collective-permute-start.9) | collective-permute-done | bytes 458784 | tf_op jit(solution)/shard_map/ppermute | solution.py:733
  42.6 1.6 collective-permute-start.12
  44.4 4.2 %collective-permute-done.2.refs_3_.refs_7_ = bf16[256,1024]{1,0:T(8,128)(2,1)} collective-permute-done((bf16[256,1024]{1,0:T(8,128)(2,1)}, bf16[256,1024]{1,0:T(8,128)(2,1)}, u32[]{:S(2)}, u32[]{:S(2)}) %collective-permute-start.2) | collective-permute-done | bytes 524320 | tf_op jit(solution)/shard_map/ppermute | solution.py:714
  48.6 1.4 collective-permute-start.15
  50.0 1.8 collective-permute-start.16
  51.9 13.5 %collective-permute-done.12.refs_7_.refs_11_ = bf16[128,1792]{1,0:T(8,128)(2,1)} collective-permute-done((bf16[128,1792]{1,0:T(8,128)(2,1)S(1)}, bf16[128,1792]{1,0:T(8,128)(2,1)}, u32[]{:S(2)}, u32[]{:S(2)}) %collective-permute-start.12) | collective-permute-done | bytes 458784 | tf_op jit(solution)/shard_map/ppermute | solution.py:829
  65.5 2.0 collective-permute-start.1
  68.7 2.2 collective-permute-done.18.v2
  70.8 1.6 collective-permute-start.17
  75.2 2.2 smalls.1
  77.4 2.3 collective-permute-done.13.refs_11_.refs_15_
  80.8 2.4 collective-permute-done.20.refs_10_.refs_3_
  84.1 1.4 collective-permute-start.21
  85.5 11.1 %mixer_fwd.1 = (bf16[4,256,1280]{2,1,0:T(8,128)(2,1)}, f32[4,256,256]{2,1,0:T(8,128)}, f32[4,256,512]{2,1,0:T(8,128)}, f32[4,256,512]{2,1,0:T(8,128)}, bf16[256,...) custom-call(s32[28]{0:T(128)} %stack.115.idx_ref.refs_0_, ...), custom_call_target="tpu_custom_call" | custom-call | flops 40580964352 | bytes 16004208 | tf_op jit(solution)/shard_map/mixer_fwd/pallas_call | solution.py:79
  96.8 2.0 collective-permute-start.25
  98.9 2.7 collective-permute-done.25.got_ref
  105.6 10.9 %collective-permute-done.28.refs_14_.refs_7_ = bf16[2112,128]{1,0:T(8,128)(2,1)S(1)} collective-permute-done((bf16[2112,128]{1,0:T(8,128)(2,1)}, bf16[2112,128]{1,0:T(8,128)(2,1)S(1)}, u32[]{:S(2)}, u32[]{:S(2)}) %collective-permute-start.28) | collective-permute-done | bytes 540704 | tf_op jit(solution)/shard_map/ppermute | solution.py:733
  117.1 2.3 collective-permute-done.27.refs_11_.refs_4_
  121.5 1.5 collective-permute-start.31
  123.0 6.1 %collective-permute-done.32.refs_16_.refs_9_ = bf16[2112,128]{1,0:T(8,128)(2,1)S(1)} collective-permute-done((bf16[2112,128]{1,0:T(8,128)(2,1)}, bf16[2112,128]{1,0:T(8,128)(2,1)S(1)}, u32[]{:S(2)}, u32[]{:S(2)}) %collective-permute-start.32) | collective-permute-done | bytes 540704 | tf_op jit(solution)/shard_map/ppermute | solution.py:733
  129.7 2.6 collective-permute-start.30
  132.3 5.3 %collective-permute-done.34.refs_17_.refs_10_ = bf16[1056,128]{1,0:T(8,128)(2,1)S(1)} collective-permute-done((bf16[1056,128]{1,0:T(8,128)(2,1)S(1)}, bf16[1056,128]{1,0:T(8,128)(2,1)S(1)}, u32[]{:S(2)}, u32[]{:S(2)}) %collective-permute-start.34) | collective-permute-done | bytes 270368 | tf_op jit(solution)/shard_map/ppermute | solution.py:839
  138.7 7.6 %collective-permute-done.36.refs_18_.refs_11_ = bf16[1056,128]{1,0:T(8,128)(2,1)S(1)} collective-permute-done((bf16[1056,128]{1,0:T(8,128)(2,1)S(1)}, bf16[1056,128]{1,0:T(8,128)(2,1)S(1)}, u32[]{:S(2)}, u32[]{:S(2)}) %collective-permute-start.36) | collective-permute-done | bytes 270368 | tf_op jit(solution)/shard_map/ppermute | solution.py:733
  147.1 15.5 %ffn.1 = (bf16[1024,704]{1,0:T(8,128)(2,1)}, bf16[1024,1408]{1,0:T(8,128)(2,1)}, bf16[256,1024]{1,0:T(8,128)(2,1)}, bf16[256,1024]{1,0:T(8,128)(2,1)}, bf16[2,25...) custom-call(s32[28]{0:T(128)} %stack.115.idx_ref.refs_0_, bf16[256,1024]{1,0:T(8,128)(2,1)} %copy-done.3, ...), custom_call_target="tpu_custom_call" | custom-call | flops 76819750912 | bytes 16023664 | tf_op jit(solution)/shard_map/ffn/pallas_call | solution.py:79
  164.0 2.2 collective-permute-done.37.g_ref.got_ref
  166.1 2.0 far.1
  169.1 9.5 %ffn_grad.1 = (f32[2112,128]{1,0:T(8,128)}, bf16[2112,128]{1,0:T(8,128)(2,1)}, bf16[2112,128]{1,0:T(8,128)(2,1)}, bf16[2112,128]{1,0:T(8,128)(2,1)}, bf16[2112,1...) custom-call(s32[28]{0:T(128)} %stack.115.idx_ref.refs_0_, bf16[1024,704]{1,0:T(8,128)(2,1)} %get-tuple-element.196.h_ref.refs_1_, ...), custom_call_target="tpu_custom_call" | custom-call | flops 47291850752 | bytes 12304496 | tf_op jit(solution)/shard_map/ffn_grad/pallas_call | solution.py:79
  179.3 2.0 add_convert_fusion.2
  181.9 4.8 %gresid.1 = (f32[256,1024]{1,0:T(8,128)}, bf16[256,1152]{1,0:T(8,128)(2,1)}, f32[1,1024]{1,0:T(1,128)}) custom-call(bf16[256,1024]{1,0:T(8,128)(2,1)} %get-tuple-element.158.own_ref, bf16[2,256,1024]{2,1,0:T(8,128)(2,1)} %collective-permute-done.37.g_ref.got_ref, bf16[256,1024]{1,0:T(8,128)(2,1)} %collective-permute-done.38.ry_ref, ...), custom_call_target="tpu_custom_call" | custom-call | flops 3000000000 | bytes 6000000 | tf_op jit(solution)/shard_map/gresid/pallas_call | solution.py:1000
  187.5 1.5 collective-permute-start.40
  188.9 3.2 %collective-permute-done.42 = bf16[2112,128]{1,0:T(8,128)(2,1)} collective-permute-done((bf16[2112,128]{1,0:T(8,128)(2,1)}, bf16[2112,128]{1,0:T(8,128)(2,1)}, u32[]{:S(2)}, u32[]{:S(2)}) %collective-permute-start.42) | collective-permute-done | bytes 540704 | tf_op jit(solution)/shard_map/ppermute | solution.py:733
  192.7 2.2 add_convert_fusion.1
  194.9 9.8 %collective-permute-done.43 = bf16[2112,128]{1,0:T(8,128)(2,1)S(1)} collective-permute-done((bf16[2112,128]{1,0:T(8,128)(2,1)}, bf16[2112,128]{1,0:T(8,128)(2,1)S(1)}, u32[]{:S(2)}, u32[]{:S(2)}) %collective-permute-start.43) | collective-permute-done | bytes 540704 | tf_op jit(solution)/shard_map/ppermute | solution.py:733
  205.3 2.6 collective-permute-start.44
  210.4 18.2 %bwd.1 = (f32[1,512]{1,0:T(1,128)}, f32[1,256]{1,0:T(1,128)}, f32[128,1792]{1,0:T(8,128)}, bf16[128,1792]{1,0:T(8,128)(2,1)}, bf16[128,1792]{1,0:T(8,128)(2,1)},...) custom-call(s32[28]{0:T(128)} %stack.115.idx_ref.refs_0_, ...), custom_call_target="tpu_custom_call" | custom-call | flops 83530637312 | bytes 22229104 | tf_op jit(solution)/shard_map/bwd/pallas_call | solution.py:79
  232.5 3.2 %collective-permute-start.51 = (bf16[2112,128]{1,0:T(8,128)(2,1)}, bf16[2112,128]{1,0:T(8,128)(2,1)}, u32[]{:S(2)}, u32[]{:S(2)}) collective-permute-start(bf16[2112,128]{1,0:T(8,128)(2,1)} %add_convert_fusion), channel_id=1, source_target_pairs={{0,6},{1,7},{2,0},{3,1},{4,2},{5,3},{6,4},{7,5},{8,14},{9,15},{10,... | collective-permute-start | bytes 1622024 | tf_op jit(solution)/shard_map/ppermute | solution.py:755
  235.7 1.6 fusion.2
  237.8 3.5 %collective-permute-done.45 = bf16[128,1792]{1,0:T(8,128)(2,1)S(1)} collective-permute-done((bf16[128,1792]{1,0:T(8,128)(2,1)}, bf16[128,1792]{1,0:T(8,128)(2,1)S(1)}, u32[]{:S(2)}, u32[]{:S(2)}) %collective-permute-start.45) | collective-permute-done | bytes 458784 | tf_op jit(solution)/shard_map/ppermute | solution.py:733
  243.3 7.0 %collective-permute-done.50.ry_ref = bf16[256,1024]{1,0:T(8,128)(2,1)S(1)} collective-permute-done((bf16[256,1024]{1,0:T(8,128)(2,1)S(1)}, bf16[256,1024]{1,0:T(8,128)(2,1)S(1)}, u32[]{:S(2)}, u32[]{:S(2)}) %collective-permute-start.50) | collective-permute-done | bytes 524320 | tf_op jit(solution)/shard_map/ppermute | solution.py:722
  251.1 3.7 %gin.1 = (bf16[256,1024]{1,0:T(8,128)(2,1)}, f32[1,1024]{1,0:T(1,128)}) custom-call(bf16[256,1024]{1,0:T(8,128)(2,1)} %get-tuple-element.186.own_ref, bf16[2,256,1024]{2,1,0:T(8,128)(2,1)} %copy-done.23, bf16[256,1024]{1,0:T(8,128)(2,1)} %copy-done.38, bf16[256,1024]{1,0:T(8,128)(2,1)} %copy-done.6, f32[256,1024]{1,0:T(8,128)} %get-tuple-element.192.gres_ref, ...), custom_call_target="tpu_custom_call" | custom-call | flops 3000000000 | bytes 4202496 | tf_op jit(solution)/shard_map/gin/pallas_call | solution.py:79
  254.8 2.0 add_convert_fusion.4
  257.5 5.6 %down.1 = (bf16[256,1024]{1,0:T(8,128)(2,1)}, bf16[256,1024]{1,0:T(8,128)(2,1)}, bf16[2,256,1024]{2,1,0:T(8,128)(2,1)}) custom-call(s32[28]{0:T(128)} %stack.115.idx_ref.refs_0_, bf16[1024,704]{1,0:T(8,128)(2,1)} %get-tuple-element.196.h_ref.refs_1_, bf16[2112,128]{1,0:T(8,128)(2,1)} %copy-done.20, ...), custom_call_target="tpu_custom_call" | custom-call | flops 17763950592 | bytes 7864432 | tf_op jit(solution)/shard_map/down/pallas_call | solution.py:79
  263.2 1.7 collective-permute-start.52
  268.2 2.4 collective-permute-done.55
  271.5 1.9 collective-permute-done.56
  274.7 2.6 collective-permute-start.65
  278.6 1.7 convert_add_fusion.1
  281.3 5.5 %collective-permute-done.60 = bf16[128,1792]{1,0:T(8,128)(2,1)S(1)} collective-permute-done((bf16[128,1792]{1,0:T(8,128)(2,1)}, bf16[128,1792]{1,0:T(8,128)(2,1)S(1)}, u32[]{:S(2)}, u32[]{:S(2)}) %collective-permute-start.60) | collective-permute-done | bytes 458784 | tf_op jit(solution)/shard_map/ppermute | solution.py:733
  286.8 1.9 collective-permute-done.53.ry_ref
  289.4 2.6 collective-permute-start.63
  293.3 2.9 collective-permute-done.65
  298.0 4.7 %collective-permute-start.68 = (bf16[128,256]{1,0:T(8,128)(2,1)S(1)}, bf16[128,256]{1,0:T(8,128)(2,1)S(1)}, u32[]{:S(2)}, u32[]{:S(2)}) collective-permute-start(bf16[128,256]{1,0:T(8,128)(2,1)S(1)} %get-tuple-element.228), channel_id=1, source_target_pairs={{0,0},{8,16},{16,8},{24,24},{1,1},{9,17},{17,9},{25,25},{2,2},{10,... | collective-permute-start | bytes 196616 | tf_op jit(solution)/shard_map/ppermute | solution.py:1104
  302.7 2.4 collective-permute-start.67
  306.4 4.4 %collective-permute-done.67.o_in = bf16[128,512]{1,0:T(8,128)(2,1)S(1)} collective-permute-done((bf16[128,512]{1,0:T(8,128)(2,1)S(1)}, bf16[128,512]{1,0:T(8,128)(2,1)S(1)}, u32[]{:S(2)}, u32[]{:S(2)}) %collective-permute-start.67) | collective-permute-done | bytes 131104 | tf_op jit(solution)/shard_map/ppermute | solution.py:1075
  310.8 1.5 finish.1
  (242 shorter events, 51.3 us)
Async XLA Ops:
  1.6 11.7 %collective-permute-start = (bf16[128,512]{1,0:T(8,128)(2,1)S(1)}, bf16[128,512]{1,0:T(8,128)(2,1)S(1)}, u32[]{:S(2)}, u32[]{:S(2)}) collective-permute-start(bf16[128,512]{1,0:T(8,128)(2,1)S(1)} %pad_maximum_fusion.3), channel_id=1, source_target_pairs={{0,16},{8,24},{16,0},{24,8},{1,17},{9,25},{17,1},{25,9},{2,18},{10... | collective-permute-start | bytes 393224 | tf_op jit(solution)/shard_map/ppermute | solution.py:799
  2.9 10.4 %collective-permute-start.4 = (bf16[256,256]{1,0:T(8,128)(2,1)}, bf16[256,256]{1,0:T(8,128)(2,1)}, u32[]{:S(2)}, u32[]{:S(2)}) collective-permute-start(bf16[256,256]{1,0:T(8,128)(2,1)} %param.25), channel_id=1, source_target_pairs={{0,0},{1,16},{2,8},{3,24},{4,4},{5,20},{6,12},{7,28},{8,2},{9,18},... | collective-permute-start | bytes 393224 | tf_op jit(solution)/shard_map/ppermute | solution.py:813
  6.8 6.4 %collective-permute-start.3 = (bf16[128,256]{1,0:T(8,128)(2,1)}, bf16[128,256]{1,0:T(8,128)(2,1)S(1)}, u32[]{:S(2)}, u32[]{:S(2)}) collective-permute-start(bf16[128,256]{1,0:T(8,128)(2,1)} %param.21), channel_id=1, source_target_pairs={{0,0},{16,8},{8,16},{24,24},{1,1},{17,9},{9,17},{25,25},{2,2},{18,... | collective-permute-start | bytes 196616 | tf_op jit(solution)/shard_map/ppermute | solution.py:800
  10.2 3.0 collective-permute-start.5
  15.9 14.4 %collective-permute-start.6 = (bf16[128,1792]{1,0:T(8,128)(2,1)}, bf16[128,1792]{1,0:T(8,128)(2,1)S(1)}, u32[]{:S(2)}, u32[]{:S(2)}) collective-permute-start(bf16[128,1792]{1,0:T(8,128)(2,1)} %get-tuple-element.126.refs_5_.refs_9_), channel_id=1, source_target_pairs={{0,2},{1,3},{2,4},{3,5},{4,6},{5,7},{6,0},{7,1},{8,10},{9,11},{10,... | collective-permute-start | bytes 1376264 | tf_op jit(solution)/shard_map/ppermute | solution.py:825
  16.2 14.0 %collective-permute-start.8 = (bf16[128,1792]{1,0:T(8,128)(2,1)}, bf16[128,1792]{1,0:T(8,128)(2,1)S(1)}, u32[]{:S(2)}, u32[]{:S(2)}) collective-permute-start(bf16[128,1792]{1,0:T(8,128)(2,1)} %get-tuple-element.126.refs_5_.refs_9_), channel_id=1, source_target_pairs={{0,1},{1,0},{2,3},{3,2},{4,5},{5,4},{6,7},{7,6},{8,9},{9,8},{10,11... | collective-permute-start | bytes 1376264 | tf_op jit(solution)/shard_map/ppermute | solution.py:733
  30.3 11.9 %collective-permute-start.9 = (bf16[128,1792]{1,0:T(8,128)(2,1)S(1)}, bf16[128,1792]{1,0:T(8,128)(2,1)S(1)}, u32[]{:S(2)}, u32[]{:S(2)}) collective-permute-start(bf16[128,1792]{1,0:T(8,128)(2,1)S(1)} %collective-permute-done.6.refs_6_.refs_10_), channel_id=1, source_target_pairs={{0,1},{1,0},{2,3},{3,2},{4,5},{5,4},{6,7},{7,6},{8,9},{9,8},{10,11... | collective-permute-start | bytes 1376264 | tf_op jit(solution)/shard_map/ppermute | solution.py:733
  30.5 12.1 %collective-permute-start.7 = (bf16[128,1792]{1,0:T(8,128)(2,1)}, bf16[128,1792]{1,0:T(8,128)(2,1)S(1)}, u32[]{:S(2)}, u32[]{:S(2)}) collective-permute-start(bf16[128,1792]{1,0:T(8,128)(2,1)} %get-tuple-element.126.refs_5_.refs_9_), channel_id=1, source_target_pairs={{0,6},{1,7},{2,0},{3,1},{4,2},{5,3},{6,4},{7,5},{8,14},{9,15},{10,... | collective-permute-start | bytes 1376264 | tf_op jit(solution)/shard_map/ppermute | solution.py:827
  35.5 13.1 %collective-permute-start.2 = (bf16[256,1024]{1,0:T(8,128)(2,1)}, bf16[256,1024]{1,0:T(8,128)(2,1)}, u32[]{:S(2)}, u32[]{:S(2)}) collective-permute-start(bf16[256,1024]{1,0:T(8,128)(2,1)} %get-tuple-element.120.refs_1_.refs_5_), channel_id=1, source_target_pairs={{0,16},{8,24},{16,0},{24,8},{1,17},{9,25},{17,1},{25,9},{2,18},{10... | collective-permute-start | bytes 1572872 | tf_op jit(solution)/shard_map/ppermute | solution.py:714
  42.6 22.8 %collective-permute-start.12 = (bf16[128,1792]{1,0:T(8,128)(2,1)S(1)}, bf16[128,1792]{1,0:T(8,128)(2,1)}, u32[]{:S(2)}, u32[]{:S(2)}) collective-permute-start(bf16[128,1792]{1,0:T(8,128)(2,1)S(1)} %copy-done.39), channel_id=1, source_target_pairs={{0,4},{1,5},{2,6},{3,7},{4,0},{5,1},{6,2},{7,3},{8,12},{9,13},{10,... | collective-permute-start | bytes 1376264 | tf_op jit(solution)/shard_map/ppermute | solution.py:829
  44.2 23.2 %collective-permute-start.10 = (bf16[128,1792]{1,0:T(8,128)(2,1)S(1)}, bf16[128,1792]{1,0:T(8,128)(2,1)S(1)}, u32[]{:S(2)}, u32[]{:S(2)}) collective-permute-start(bf16[128,1792]{1,0:T(8,128)(2,1)S(1)} %collective-permute-done.7.refs_8_.refs_12_), channel_id=1, source_target_pairs={{0,1},{1,0},{2,3},{3,2},{4,5},{5,4},{6,7},{7,6},{8,9},{9,8},{10,11... | collective-permute-start | bytes 1376264 | tf_op jit(solution)/shard_map/ppermute | solution.py:733
  48.6 18.9 %collective-permute-start.14 = (bf16[16,512]{1,0:T(8,128)(2,1)S(1)}, bf16[16,512]{1,0:T(8,128)(2,1)S(1)}, u32[]{:S(2)}, u32[]{:S(2)}) collective-permute-start(bf16[16,512]{1,0:T(8,128)(2,1)S(1)} %copy-done.25), channel_id=1, source_target_pairs={{0,2},{1,3},{2,4},{3,5},{4,6},{5,7},{6,0},{7,1},{8,10},{9,11},{10,... | collective-permute-start | bytes 49160 | tf_op jit(solution)/shard_map/ppermute | solution.py:847
  48.6 19.0 %collective-permute-start.15 = (bf16[16,512]{1,0:T(8,128)(2,1)S(1)}, bf16[16,512]{1,0:T(8,128)(2,1)S(1)}, u32[]{:S(2)}, u32[]{:S(2)}) collective-permute-start(bf16[16,512]{1,0:T(8,128)(2,1)S(1)} %copy-done.25), channel_id=1, source_target_pairs={{0,4},{1,5},{2,6},{3,7},{4,0},{5,1},{6,2},{7,3},{8,12},{9,13},{10,... | collective-permute-start | bytes 49160 | tf_op jit(solution)/shard_map/ppermute | solution.py:847
  50.0 17.6 %collective-permute-start.16 = (bf16[16,512]{1,0:T(8,128)(2,1)S(1)}, bf16[16,512]{1,0:T(8,128)(2,1)S(1)}, u32[]{:S(2)}, u32[]{:S(2)}) collective-permute-start(bf16[16,512]{1,0:T(8,128)(2,1)S(1)} %copy-done.25), channel_id=1, source_target_pairs={{0,6},{1,7},{2,0},{3,1},{4,2},{5,3},{6,4},{7,5},{8,14},{9,15},{10,... | collective-permute-start | bytes 49160 | tf_op jit(solution)/shard_map/ppermute | solution.py:847
  65.5 18.6 %collective-permute-start.1 = (bf16[256,1024]{1,0:T(8,128)(2,1)}, bf16[256,1024]{1,0:T(8,128)(2,1)}, u32[]{:S(2)}, u32[]{:S(2)}) collective-permute-start(bf16[256,1024]{1,0:T(8,128)(2,1)} %get-tuple-element.120.refs_1_.refs_5_), channel_id=1, source_target_pairs={{0,8},{8,0},{16,24},{24,16},{1,9},{9,1},{17,25},{25,17},{2,10},{10... | collective-permute-start | bytes 1572872 | tf_op jit(solution)/shard_map/ppermute | solution.py:715
  67.4 15.7 %collective-permute-start.20 = (bf16[2112,128]{1,0:T(8,128)(2,1)S(1)}, bf16[2112,128]{1,0:T(8,128)(2,1)}, u32[]{:S(2)}, u32[]{:S(2)}) collective-permute-start(bf16[2112,128]{1,0:T(8,128)(2,1)S(1)} %pad_maximum_fusion.refs_9_.refs_2_), channel_id=1, source_target_pairs={{0,2},{1,3},{2,4},{3,5},{4,6},{5,7},{6,0},{7,1},{8,10},{9,11},{10,... | collective-permute-start | bytes 1622024 | tf_op jit(solution)/shard_map/ppermute | solution.py:834
  67.5 18.0 %collective-permute-start.11 = (bf16[256,1024]{1,0:T(8,128)(2,1)}, bf16[256,1024]{1,0:T(8,128)(2,1)}, u32[]{:S(2)}, u32[]{:S(2)}) collective-permute-start(bf16[256,1024]{1,0:T(8,128)(2,1)} %collective-permute-done.2.refs_3_.refs_7_), channel_id=1, source_target_pairs={{0,8},{8,0},{16,24},{24,16},{1,9},{9,1},{17,25},{25,17},{2,10},{10... | collective-permute-start | bytes 1572872 | tf_op jit(solution)/shard_map/ppermute | solution.py:832
  67.6 3.2 %collective-permute-start.18 = (bf16[64,512]{1,0:T(8,128)(2,1)S(1)}, bf16[64,512]{1,0:T(8,128)(2,1)S(1)}, u32[]{:S(2)}, u32[]{:S(2)}) collective-permute-start(bf16[64,512]{1,0:T(8,128)(2,1)S(1)} %pad_maximum_fusion.5.v0), channel_id=1, source_target_pairs={{0,16},{8,24},{16,0},{24,8},{1,17},{9,25},{17,1},{25,9},{2,18},{10... | collective-permute-start | bytes 196616 | tf_op jit(solution)/shard_map/ppermute | solution.py:714
  67.7 12.0 %collective-permute-start.13 = (bf16[128,1792]{1,0:T(8,128)(2,1)}, bf16[128,1792]{1,0:T(8,128)(2,1)}, u32[]{:S(2)}, u32[]{:S(2)}) collective-permute-start(bf16[128,1792]{1,0:T(8,128)(2,1)} %collective-permute-done.12.refs_7_.refs_11_), channel_id=1, source_target_pairs={{0,1},{1,0},{2,3},{3,2},{4,5},{5,4},{6,7},{7,6},{8,9},{9,8},{10,11... | collective-permute-start | bytes 1376264 | tf_op jit(solution)/shard_map/ppermute | solution.py:733
  74.6 22.0 %collective-permute-start.23 = (bf16[256,1024]{1,0:T(8,128)(2,1)}, bf16[256,1024]{1,0:T(8,128)(2,1)}, u32[]{:S(2)}, u32[]{:S(2)}) collective-permute-start(bf16[256,1024]{1,0:T(8,128)(2,1)} %get-tuple-element.167.refs_5_.c0.c_ref), channel_id=1, source_target_pairs={{0,8},{8,0},{16,24},{24,16},{1,9},{9,1},{17,25},{25,17},{2,10},{10... | collective-permute-start | bytes 1572872 | tf_op jit(solution)/shard_map/ppermute | solution.py:715
  79.7 16.8 %collective-permute-start.24 = (bf16[256,1024]{1,0:T(8,128)(2,1)}, bf16[256,1024]{1,0:T(8,128)(2,1)}, u32[]{:S(2)}, u32[]{:S(2)}) collective-permute-start(bf16[256,1024]{1,0:T(8,128)(2,1)} %get-tuple-element.167.refs_5_.c0.c_ref), channel_id=1, source_target_pairs={{0,16},{8,24},{16,0},{24,8},{1,17},{9,25},{17,1},{25,9},{2,18},{10... | collective-permute-start | bytes 1572872 | tf_op jit(solution)/shard_map/ppermute | solution.py:714
  83.2 13.4 %collective-permute-start.22 = (bf16[2112,128]{1,0:T(8,128)(2,1)S(1)}, bf16[2112,128]{1,0:T(8,128)(2,1)}, u32[]{:S(2)}, u32[]{:S(2)}) collective-permute-start(bf16[2112,128]{1,0:T(8,128)(2,1)S(1)} %pad_maximum_fusion.refs_9_.refs_2_), channel_id=1, source_target_pairs={{0,1},{1,0},{2,3},{3,2},{4,5},{5,4},{6,7},{7,6},{8,9},{9,8},{10,11... | collective-permute-start | bytes 1622024 | tf_op jit(solution)/shard_map/ppermute | solution.py:733
  84.1 12.8 %collective-permute-start.21 = (bf16[2112,128]{1,0:T(8,128)(2,1)S(1)}, bf16[2112,128]{1,0:T(8,128)(2,1)}, u32[]{:S(2)}, u32[]{:S(2)}) collective-permute-start(bf16[2112,128]{1,0:T(8,128)(2,1)S(1)} %pad_maximum_fusion.refs_9_.refs_2_), channel_id=1, source_target_pairs={{0,6},{1,7},{2,0},{3,1},{4,2},{5,3},{6,4},{7,5},{8,14},{9,15},{10,... | collective-permute-start | bytes 1622024 | tf_op jit(solution)/shard_map/ppermute | solution.py:835
  96.8 4.7 %collective-permute-start.25 = (bf16[2,256,1152]{2,1,0:T(8,128)(2,1)}, bf16[2,256,1152]{2,1,0:T(8,128)(2,1)S(1)}, u32[]{:S(2)}, u32[]{:S(2)}) collective-permute-start(bf16[2,256,1152]{2,1,0:T(8,128)(2,1)} %get-tuple-element.144), channel_id=1, source_target_pairs={{0,8},{8,0},{16,24},{24,16},{1,9},{9,1},{17,25},{25,17},{2,10},{10... | collective-permute-start | bytes 3538952 | tf_op jit(solution)/shard_map/ppermute | solution.py:939
  102.9 16.5 %collective-permute-start.26 = (bf16[256,1152]{1,0:T(8,128)(2,1)S(1)}, bf16[256,1152]{1,0:T(8,128)(2,1)S(1)}, u32[]{:S(2)}, u32[]{:S(2)}) collective-permute-start(bf16[256,1152]{1,0:T(8,128)(2,1)S(1)} %fusion), channel_id=1, source_target_pairs={{0,16},{8,24},{16,0},{24,8},{1,17},{9,25},{17,1},{25,9},{2,18},{10... | collective-permute-start | bytes 1769480 | tf_op jit(solution)/shard_map/ppermute | solution.py:722
  103.0 13.6 %collective-permute-start.28 = (bf16[2112,128]{1,0:T(8,128)(2,1)}, bf16[2112,128]{1,0:T(8,128)(2,1)S(1)}, u32[]{:S(2)}, u32[]{:S(2)}) collective-permute-start(bf16[2112,128]{1,0:T(8,128)(2,1)} %collective-permute-done.20.refs_10_.refs_3_), channel_id=1, source_target_pairs={{0,1},{1,0},{2,3},{3,2},{4,5},{5,4},{6,7},{7,6},{8,9},{9,8},{10,11... | collective-permute-start | bytes 1622024 | tf_op jit(solution)/shard_map/ppermute | solution.py:733
  103.6 13.5 %collective-permute-start.29 = (bf16[256,1024]{1,0:T(8,128)(2,1)}, bf16[256,1024]{1,0:T(8,128)(2,1)S(1)}, u32[]{:S(2)}, u32[]{:S(2)}) collective-permute-start(bf16[256,1024]{1,0:T(8,128)(2,1)} %collective-permute-done.24.refs_7_.c2), channel_id=1, source_target_pairs={{0,8},{8,0},{16,24},{24,16},{1,9},{9,1},{17,25},{25,17},{2,10},{10... | collective-permute-start | bytes 1572872 | tf_op jit(solution)/shard_map/ppermute | solution.py:716
  104.5 14.9 %collective-permute-start.27 = (bf16[1056,128]{1,0:T(8,128)(2,1)S(1)}, bf16[1056,128]{1,0:T(8,128)(2,1)S(1)}, u32[]{:S(2)}, u32[]{:S(2)}) collective-permute-start(bf16[1056,128]{1,0:T(8,128)(2,1)S(1)} %get-tuple-element.146), channel_id=1, source_target_pairs={{0,4},{1,5},{2,6},{3,7},{4,0},{5,1},{6,2},{7,3},{8,12},{9,13},{10,... | collective-permute-start | bytes 811016 | tf_op jit(solution)/shard_map/ppermute | solution.py:838
  116.5 12.6 %collective-permute-start.32 = (bf16[2112,128]{1,0:T(8,128)(2,1)}, bf16[2112,128]{1,0:T(8,128)(2,1)S(1)}, u32[]{:S(2)}, u32[]{:S(2)}) collective-permute-start(bf16[2112,128]{1,0:T(8,128)(2,1)} %collective-permute-done.21.refs_12_.refs_5_), channel_id=1, source_target_pairs={{0,1},{1,0},{2,3},{3,2},{4,5},{5,4},{6,7},{7,6},{8,9},{9,8},{10,11... | collective-permute-start | bytes 1622024 | tf_op jit(solution)/shard_map/ppermute | solution.py:733
  121.5 16.1 %collective-permute-start.31 = (bf16[256,1024]{1,0:T(8,128)(2,1)S(1)}, bf16[256,1024]{1,0:T(8,128)(2,1)S(1)}, u32[]{:S(2)}, u32[]{:S(2)}) collective-permute-start(bf16[256,1024]{1,0:T(8,128)(2,1)S(1)} %get-tuple-element.151.refs_1_.x0), channel_id=1, source_target_pairs={{0,16},{8,24},{16,0},{24,8},{1,17},{9,25},{17,1},{25,9},{2,18},{10... | collective-permute-start | bytes 1572872 | tf_op jit(solution)/shard_map/ppermute | solution.py:714
  123.0 14.6 %collective-permute-start.34 = (bf16[1056,128]{1,0:T(8,128)(2,1)S(1)}, bf16[1056,128]{1,0:T(8,128)(2,1)S(1)}, u32[]{:S(2)}, u32[]{:S(2)}) collective-permute-start(bf16[1056,128]{1,0:T(8,128)(2,1)S(1)} %get-tuple-element.154), channel_id=1, source_target_pairs={{0,4},{1,5},{2,6},{3,7},{4,0},{5,1},{6,2},{7,3},{8,12},{9,13},{10,... | collective-permute-start | bytes 811016 | tf_op jit(solution)/shard_map/ppermute | solution.py:839
  129.1 8.5 %collective-permute-start.33 = (bf16[1056,128]{1,0:T(8,128)(2,1)S(1)}, bf16[1056,128]{1,0:T(8,128)(2,1)S(1)}, u32[]{:S(2)}, u32[]{:S(2)}) collective-permute-start(bf16[1056,128]{1,0:T(8,128)(2,1)S(1)} %collective-permute-done.27.refs_11_.refs_4_), channel_id=1, source_target_pairs={{0,1},{1,0},{2,3},{3,2},{4,5},{5,4},{6,7},{7,6},{8,9},{9,8},{10,11... | collective-permute-start | bytes 811016 | tf_op jit(solution)/shard_map/ppermute | solution.py:733
  129.7 16.6 %collective-permute-start.30 = (bf16[256,1024]{1,0:T(8,128)(2,1)S(1)}, bf16[256,1024]{1,0:T(8,128)(2,1)S(1)}, u32[]{:S(2)}, u32[]{:S(2)}) collective-permute-start(bf16[256,1024]{1,0:T(8,128)(2,1)S(1)} %get-tuple-element.151.refs_1_.x0), channel_id=1, source_target_pairs={{0,8},{8,0},{16,24},{24,16},{1,9},{9,1},{17,25},{25,17},{2,10},{10... | collective-permute-start | bytes 1572872 | tf_op jit(solution)/shard_map/ppermute | solution.py:715
  137.6 9.5 %collective-permute-start.35 = (bf16[256,1024]{1,0:T(8,128)(2,1)S(1)}, bf16[256,1024]{1,0:T(8,128)(2,1)}, u32[]{:S(2)}, u32[]{:S(2)}) collective-permute-start(bf16[256,1024]{1,0:T(8,128)(2,1)S(1)} %collective-permute-done.31.refs_3_.x2), channel_id=1, source_target_pairs={{0,8},{8,0},{16,24},{24,16},{1,9},{9,1},{17,25},{25,17},{2,10},{10... | collective-permute-start | bytes 1572872 | tf_op jit(solution)/shard_map/ppermute | solution.py:949
  138.2 8.1 %collective-permute-start.36 = (bf16[1056,128]{1,0:T(8,128)(2,1)S(1)}, bf16[1056,128]{1,0:T(8,128)(2,1)S(1)}, u32[]{:S(2)}, u32[]{:S(2)}) collective-permute-start(bf16[1056,128]{1,0:T(8,128)(2,1)S(1)} %collective-permute-done.34.refs_17_.refs_10_), channel_id=1, source_target_pairs={{0,1},{1,0},{2,3},{3,2},{4,5},{5,4},{6,7},{7,6},{8,9},{9,8},{10,11... | collective-permute-start | bytes 811016 | tf_op jit(solution)/shard_map/ppermute | solution.py:733
  162.6 3.5 %collective-permute-start.37 = (bf16[2,256,1024]{2,1,0:T(8,128)(2,1)}, bf16[2,256,1024]{2,1,0:T(8,128)(2,1)}, u32[]{:S(2)}, u32[]{:S(2)}) collective-permute-start(bf16[2,256,1024]{2,1,0:T(8,128)(2,1)} %get-tuple-element.159), channel_id=1, source_target_pairs={{0,8},{8,0},{16,24},{24,16},{1,9},{9,1},{17,25},{25,17},{2,10},{10... | collective-permute-start | bytes 3145736 | tf_op jit(solution)/shard_map/ppermute | solution.py:966
  163.5 15.1 %collective-permute-start.39 = (bf16[2112,128]{1,0:T(8,128)(2,1)}, bf16[2112,128]{1,0:T(8,128)(2,1)}, u32[]{:S(2)}, u32[]{:S(2)}) collective-permute-start(bf16[2112,128]{1,0:T(8,128)(2,1)} %get-tuple-element.166), channel_id=1, source_target_pairs={{0,1},{1,0},{2,3},{3,2},{4,5},{5,4},{6,7},{7,6},{8,9},{9,8},{10,11... | collective-permute-start | bytes 1622024 | tf_op jit(solution)/shard_map/ppermute | solution.py:733
  168.1 13.8 %collective-permute-start.38 = (bf16[256,1024]{1,0:T(8,128)(2,1)}, bf16[256,1024]{1,0:T(8,128)(2,1)}, u32[]{:S(2)}, u32[]{:S(2)}) collective-permute-start(bf16[256,1024]{1,0:T(8,128)(2,1)} %far.1), channel_id=1, source_target_pairs={{0,16},{8,24},{16,0},{24,8},{1,17},{9,25},{17,1},{25,9},{2,18},{10... | collective-permute-start | bytes 1572872 | tf_op jit(solution)/shard_map/ppermute | solution.py:980
  178.6 13.5 %collective-permute-start.42 = (bf16[2112,128]{1,0:T(8,128)(2,1)}, bf16[2112,128]{1,0:T(8,128)(2,1)}, u32[]{:S(2)}, u32[]{:S(2)}) collective-permute-start(bf16[2112,128]{1,0:T(8,128)(2,1)} %get-tuple-element.173), channel_id=1, source_target_pairs={{0,1},{1,0},{2,3},{3,2},{4,5},{5,4},{6,7},{7,6},{8,9},{9,8},{10,11... | collective-permute-start | bytes 1622024 | tf_op jit(solution)/shard_map/ppermute | solution.py:733
  181.3 47.3 %collective-permute-start.46 = (bf16[2112,128]{1,0:T(8,128)(2,1)}, bf16[2112,128]{1,0:T(8,128)(2,1)S(1)}, u32[]{:S(2)}, u32[]{:S(2)}) collective-permute-start(bf16[2112,128]{1,0:T(8,128)(2,1)} %add_convert_fusion.2), channel_id=1, source_target_pairs={{0,4},{1,5},{2,6},{3,7},{4,0},{5,1},{6,2},{7,3},{8,12},{9,13},{10,... | collective-permute-start | bytes 1622024 | tf_op jit(solution)/shard_map/ppermute | solution.py:755
  186.7 18.6 %collective-permute-start.41 = (bf16[256,1152]{1,0:T(8,128)(2,1)}, bf16[256,1152]{1,0:T(8,128)(2,1)S(1)}, u32[]{:S(2)}, u32[]{:S(2)}) collective-permute-start(bf16[256,1152]{1,0:T(8,128)(2,1)} %get-tuple-element.169.refs_1_), channel_id=1, source_target_pairs={{0,16},{8,24},{16,0},{24,8},{1,17},{9,25},{17,1},{25,9},{2,18},{10... | collective-permute-start | bytes 1769480 | tf_op jit(solution)/shard_map/ppermute | solution.py:714
  187.5 21.4 %collective-permute-start.40 = (bf16[256,1152]{1,0:T(8,128)(2,1)}, bf16[256,1152]{1,0:T(8,128)(2,1)S(1)}, u32[]{:S(2)}, u32[]{:S(2)}) collective-permute-start(bf16[256,1152]{1,0:T(8,128)(2,1)} %get-tuple-element.169.refs_1_), channel_id=1, source_target_pairs={{0,8},{8,0},{16,24},{24,16},{1,9},{9,1},{17,25},{25,17},{2,10},{10... | collective-permute-start | bytes 1769480 | tf_op jit(solution)/shard_map/ppermute | solution.py:715
  192.2 12.6 %collective-permute-start.43 = (bf16[2112,128]{1,0:T(8,128)(2,1)}, bf16[2112,128]{1,0:T(8,128)(2,1)S(1)}, u32[]{:S(2)}, u32[]{:S(2)}) collective-permute-start(bf16[2112,128]{1,0:T(8,128)(2,1)} %get-tuple-element.177), channel_id=1, source_target_pairs={{0,1},{1,0},{2,3},{3,2},{4,5},{5,4},{6,7},{7,6},{8,9},{9,8},{10,11... | collective-permute-start | bytes 1622024 | tf_op jit(solution)/shard_map/ppermute | solution.py:733
  194.9 33.6 %collective-permute-start.47 = (bf16[2112,128]{1,0:T(8,128)(2,1)}, bf16[2112,128]{1,0:T(8,128)(2,1)}, u32[]{:S(2)}, u32[]{:S(2)}) collective-permute-start(bf16[2112,128]{1,0:T(8,128)(2,1)} %add_convert_fusion.1), channel_id=1, source_target_pairs={{0,2},{1,3},{2,4},{3,5},{4,6},{5,7},{6,0},{7,1},{8,10},{9,11},{10,... | collective-permute-start | bytes 1622024 | tf_op jit(solution)/shard_map/ppermute | solution.py:755
  204.7 23.8 %collective-permute-start.48 = (bf16[2112,128]{1,0:T(8,128)(2,1)}, bf16[2112,128]{1,0:T(8,128)(2,1)}, u32[]{:S(2)}, u32[]{:S(2)}) collective-permute-start(bf16[2112,128]{1,0:T(8,128)(2,1)} %get-tuple-element.189), channel_id=1, source_target_pairs={{0,1},{1,0},{2,3},{3,2},{4,5},{5,4},{6,7},{7,6},{8,9},{9,8},{10,11... | collective-permute-start | bytes 1622024 | tf_op jit(solution)/shard_map/ppermute | solution.py:733
  205.3 4.3 %collective-permute-start.44 = (bf16[256,1152]{1,0:T(8,128)(2,1)S(1)}, bf16[256,1152]{1,0:T(8,128)(2,1)S(1)}, u32[]{:S(2)}, u32[]{:S(2)}) collective-permute-start(bf16[256,1152]{1,0:T(8,128)(2,1)S(1)} %collective-permute-done.41.refs_3_), channel_id=1, source_target_pairs={{0,8},{8,0},{16,24},{24,16},{1,9},{9,1},{17,25},{25,17},{2,10},{10... | collective-permute-start | bytes 1769480 | tf_op jit(solution)/shard_map/ppermute | solution.py:1020
  228.6 7.2 %collective-permute-start.49 = (bf16[2,256,1024]{2,1,0:T(8,128)(2,1)}, bf16[2,256,1024]{2,1,0:T(8,128)(2,1)S(1)}, u32[]{:S(2)}, u32[]{:S(2)}) collective-permute-start(bf16[2,256,1024]{2,1,0:T(8,128)(2,1)} %get-tuple-element.190), channel_id=1, source_target_pairs={{0,8},{8,0},{16,24},{24,16},{1,9},{9,1},{17,25},{25,17},{2,10},{10... | collective-permute-start | bytes 3145736 | tf_op jit(solution)/shard_map/ppermute | solution.py:1044
  229.0 12.3 %collective-permute-start.45 = (bf16[128,1792]{1,0:T(8,128)(2,1)}, bf16[128,1792]{1,0:T(8,128)(2,1)S(1)}, u32[]{:S(2)}, u32[]{:S(2)}) collective-permute-start(bf16[128,1792]{1,0:T(8,128)(2,1)} %get-tuple-element.185), channel_id=1, source_target_pairs={{0,1},{1,0},{2,3},{3,2},{4,5},{5,4},{6,7},{7,6},{8,9},{9,8},{10,11... | collective-permute-start | bytes 1376264 | tf_op jit(solution)/shard_map/ppermute | solution.py:733
  232.5 22.3 %collective-permute-start.51 = (bf16[2112,128]{1,0:T(8,128)(2,1)}, bf16[2112,128]{1,0:T(8,128)(2,1)}, u32[]{:S(2)}, u32[]{:S(2)}) collective-permute-start(bf16[2112,128]{1,0:T(8,128)(2,1)} %add_convert_fusion), channel_id=1, source_target_pairs={{0,6},{1,7},{2,0},{3,1},{4,2},{5,3},{6,4},{7,5},{8,14},{9,15},{10,... | collective-permute-start | bytes 1622024 | tf_op jit(solution)/shard_map/ppermute | solution.py:755
  237.3 12.9 %collective-permute-start.50 = (bf16[256,1024]{1,0:T(8,128)(2,1)S(1)}, bf16[256,1024]{1,0:T(8,128)(2,1)S(1)}, u32[]{:S(2)}, u32[]{:S(2)}) collective-permute-start(bf16[256,1024]{1,0:T(8,128)(2,1)S(1)} %fusion.2), channel_id=1, source_target_pairs={{0,16},{8,24},{16,0},{24,8},{1,17},{9,25},{17,1},{25,9},{2,18},{10... | collective-permute-start | bytes 1572872 | tf_op jit(solution)/shard_map/ppermute | solution.py:722
  242.2 12.6 %collective-permute-start.58 = (bf16[128,1792]{1,0:T(8,128)(2,1)}, bf16[128,1792]{1,0:T(8,128)(2,1)}, u32[]{:S(2)}, u32[]{:S(2)}) collective-permute-start(bf16[128,1792]{1,0:T(8,128)(2,1)} %get-tuple-element.211), channel_id=1, source_target_pairs={{0,1},{1,0},{2,3},{3,2},{4,5},{5,4},{6,7},{7,6},{8,9},{9,8},{10,11... | collective-permute-start | bytes 1376264 | tf_op jit(solution)/shard_map/ppermute | solution.py:733
  243.1 28.4 %collective-permute-start.57 = (bf16[128,1792]{1,0:T(8,128)(2,1)}, bf16[128,1792]{1,0:T(8,128)(2,1)}, u32[]{:S(2)}, u32[]{:S(2)}) collective-permute-start(bf16[128,1792]{1,0:T(8,128)(2,1)} %add_convert_fusion.5), channel_id=1, source_target_pairs={{0,4},{1,5},{2,6},{3,7},{4,0},{5,1},{6,2},{7,3},{8,12},{9,13},{10,... | collective-permute-start | bytes 1376264 | tf_op jit(solution)/shard_map/ppermute | solution.py:755
  256.8 16.6 %collective-permute-start.59 = (bf16[128,1792]{1,0:T(8,128)(2,1)}, bf16[128,1792]{1,0:T(8,128)(2,1)}, u32[]{:S(2)}, u32[]{:S(2)}) collective-permute-start(bf16[128,1792]{1,0:T(8,128)(2,1)} %get-tuple-element.212), channel_id=1, source_target_pairs={{0,1},{1,0},{2,3},{3,2},{4,5},{5,4},{6,7},{7,6},{8,9},{9,8},{10,11... | collective-permute-start | bytes 1376264 | tf_op jit(solution)/shard_map/ppermute | solution.py:733
  263.2 14.9 %collective-permute-start.52 = (bf16[2,256,1024]{2,1,0:T(8,128)(2,1)}, bf16[2,256,1024]{2,1,0:T(8,128)(2,1)S(1)}, u32[]{:S(2)}, u32[]{:S(2)}) collective-permute-start(bf16[2,256,1024]{2,1,0:T(8,128)(2,1)} %get-tuple-element.198), channel_id=1, source_target_pairs={{0,8},{8,0},{16,24},{24,16},{1,9},{9,1},{17,25},{25,17},{2,10},{10... | collective-permute-start | bytes 3145736 | tf_op jit(solution)/shard_map/ppermute | solution.py:1060
  271.5 21.8 %collective-permute-start.64 = (bf16[128,1792]{1,0:T(8,128)(2,1)}, bf16[128,1792]{1,0:T(8,128)(2,1)S(1)}, u32[]{:S(2)}, u32[]{:S(2)}) collective-permute-start(bf16[128,1792]{1,0:T(8,128)(2,1)} %add_convert_fusion.4), channel_id=1, source_target_pairs={{0,2},{1,3},{2,4},{3,5},{4,6},{5,7},{6,0},{7,1},{8,10},{9,11},{10,... | collective-permute-start | bytes 1376264 | tf_op jit(solution)/shard_map/ppermute | solution.py:755
  274.7 21.5 %collective-permute-start.65 = (bf16[128,1792]{1,0:T(8,128)(2,1)S(1)}, bf16[128,1792]{1,0:T(8,128)(2,1)S(1)}, u32[]{:S(2)}, u32[]{:S(2)}) collective-permute-start(bf16[128,1792]{1,0:T(8,128)(2,1)S(1)} %add_convert_fusion.3), channel_id=1, source_target_pairs={{0,6},{1,7},{2,0},{3,1},{4,2},{5,3},{6,4},{7,5},{8,14},{9,15},{10,... | collective-permute-start | bytes 1376264 | tf_op jit(solution)/shard_map/ppermute | solution.py:755
  277.4 9.5 %collective-permute-start.60 = (bf16[128,1792]{1,0:T(8,128)(2,1)}, bf16[128,1792]{1,0:T(8,128)(2,1)S(1)}, u32[]{:S(2)}, u32[]{:S(2)}) collective-permute-start(bf16[128,1792]{1,0:T(8,128)(2,1)} %get-tuple-element.213), channel_id=1, source_target_pairs={{0,1},{1,0},{2,3},{3,2},{4,5},{5,4},{6,7},{7,6},{8,9},{9,8},{10,11... | collective-permute-start | bytes 1376264 | tf_op jit(solution)/shard_map/ppermute | solution.py:733
  278.3 10.5 %collective-permute-start.53 = (bf16[256,1024]{1,0:T(8,128)(2,1)S(1)}, bf16[256,1024]{1,0:T(8,128)(2,1)S(1)}, u32[]{:S(2)}, u32[]{:S(2)}) collective-permute-start(bf16[256,1024]{1,0:T(8,128)(2,1)S(1)} %fusion.1), channel_id=1, source_target_pairs={{0,16},{8,24},{16,0},{24,8},{1,17},{9,25},{17,1},{25,9},{2,18},{10... | collective-permute-start | bytes 1572872 | tf_op jit(solution)/shard_map/ppermute | solution.py:722
  288.7 14.0 %collective-permute-start.61 = (f32[32,160]{1,0:T(8,128)S(1)}, f32[32,160]{1,0:T(8,128)S(1)}, u32[]{:S(2)}, u32[]{:S(2)}) collective-permute-start(f32[32,160]{1,0:T(8,128)S(1)} %add.271), channel_id=1, source_target_pairs={{0,2},{1,3},{2,4},{3,5},{4,6},{5,7},{6,0},{7,1},{8,10},{9,11},{10,... | collective-permute-start | bytes 61448 | tf_op jit(solution)/shard_map/ppermute | solution.py:769
  288.7 16.4 %collective-permute-start.62 = (f32[32,160]{1,0:T(8,128)S(1)}, f32[32,160]{1,0:T(8,128)S(1)}, u32[]{:S(2)}, u32[]{:S(2)}) collective-permute-start(f32[32,160]{1,0:T(8,128)S(1)} %add.271), channel_id=1, source_target_pairs={{0,4},{1,5},{2,6},{3,7},{4,0},{5,1},{6,2},{7,3},{8,12},{9,13},{10,... | collective-permute-start | bytes 61448 | tf_op jit(solution)/shard_map/ppermute | solution.py:769
  289.4 15.8 %collective-permute-start.63 = (f32[32,160]{1,0:T(8,128)S(1)}, f32[32,160]{1,0:T(8,128)S(1)}, u32[]{:S(2)}, u32[]{:S(2)}) collective-permute-start(f32[32,160]{1,0:T(8,128)S(1)} %add.271), channel_id=1, source_target_pairs={{0,6},{1,7},{2,0},{3,1},{4,2},{5,3},{6,4},{7,5},{8,14},{9,15},{10,... | collective-permute-start | bytes 61448 | tf_op jit(solution)/shard_map/ppermute | solution.py:769
  297.5 8.8 %collective-permute-start.66 = (bf16[128,512]{1,0:T(8,128)(2,1)S(1)}, bf16[128,512]{1,0:T(8,128)(2,1)S(1)}, u32[]{:S(2)}, u32[]{:S(2)}) collective-permute-start(bf16[128,512]{1,0:T(8,128)(2,1)S(1)} %pad_maximum_fusion.4), channel_id=1, source_target_pairs={{0,16},{8,24},{16,0},{24,8},{1,17},{9,25},{17,1},{25,9},{2,18},{10... | collective-permute-start | bytes 393224 | tf_op jit(solution)/shard_map/ppermute | solution.py:1100
  298.0 8.4 %collective-permute-start.68 = (bf16[128,256]{1,0:T(8,128)(2,1)S(1)}, bf16[128,256]{1,0:T(8,128)(2,1)S(1)}, u32[]{:S(2)}, u32[]{:S(2)}) collective-permute-start(bf16[128,256]{1,0:T(8,128)(2,1)S(1)} %get-tuple-element.228), channel_id=1, source_target_pairs={{0,0},{8,16},{16,8},{24,24},{1,1},{9,17},{17,9},{25,25},{2,2},{10,... | collective-permute-start | bytes 196616 | tf_op jit(solution)/shard_map/ppermute | solution.py:1104
  302.7 8.1 %collective-permute-start.67 = (bf16[128,512]{1,0:T(8,128)(2,1)S(1)}, bf16[128,512]{1,0:T(8,128)(2,1)S(1)}, u32[]{:S(2)}, u32[]{:S(2)}) collective-permute-start(bf16[128,512]{1,0:T(8,128)(2,1)S(1)} %slice.100), channel_id=1, source_target_pairs={{0,0},{16,1},{8,2},{24,3},{4,4},{20,5},{12,6},{28,7},{2,8},{18,9},... | collective-permute-start | bytes 393224 | tf_op jit(solution)/shard_map/ppermute | solution.py:1075
  (60 other events, 548.7 us)
